TPU v7x, 256 devices: a whole 4x4x8 slice. The times are simulated.
256 devices in a mesh: vel: 32 (over z, x), space: 8 (over y, core).
Axes of the slice: x: 4, y: 4, z: 8, core: 2. Of those that a mesh axis runs over, the one named last changes fastest.
Arguments:
- distribution: float32 [3, 32768, 16, 256], P(None, 'vel', 'space'), may hold values from 0.005 to 2.5, as said below
- wall_temp: float32 [1024], P('space'), may hold values from 0.6 to 1.6
- coverage: float32 [12, 1024], P(None, 'space'), may hold values from 0 to 0.15
- face_cell: int32 [8, 128], P('space'), may hold values from 0 to 127, each once within a row
- face_owner: int32 [1024], P('space'), may hold values from 0 to 3
- stoichiometry: int32 [12, 3], replicated, may hold values from 0 to 2
- sticking: float32 [4, 3], replicated, may hold values from 0.1 to 0.9
- surface_rates: float32 [4, 2, 12], replicated, may hold values from 0.02 to 2
Outputs:
- advanced: float32 [3, 32768, 16, 256], P(None, 'vel', 'space')
- new_coverage: float32 [12, 1024], P(None, 'space')
Inputs may be any that keep to these rules, and one draw needn't show every extreme that they name: `distribution`: positive everywhere. `face_cell`: row p lists each wall column x * 64 + z of space block p once, x counted within the block.
All inputs are finite; a program needn't handle non-finite values.
Results may differ from a plain program's by a relative error of at most 0.0001.
Values sent between devices are 32-bit elements; how exact they have to be, the bound alone decides.
No kernel may reach another device: no remote copies, remote signals or barrier semaphores. Data moves between devices by JAX's collectives and lax.ppermute only.
A program may use at most 192 MiB of HBM per device.

v0:
```python
import jax
import jax.numpy as jnp
from jax import lax
from jax.sharding import PartitionSpec as P

S = 3
VG = 32
NZ = 64
CX = 2
NEWTON = 8


SPEED_LIMIT = 4.0
SPECIES_MASS = (1.0, 2.0, 4.0)
COLLISION_RATE = (0.3, 0.2, 0.15)
TIME_STEP = 0.08
SURFACE_STEP = 2.0
DAMPING = 0.25
ACTIVATION = 2.0


def shifted(value, axis, by):
    peers = lax.axis_size(axis)
    return lax.ppermute(value, axis, [(i, (i + by) % peers) for i in range(peers)])


def component(position):
    spacing = 2.0 * SPEED_LIMIT / VG
    return (position.astype(jnp.float32) + 0.5) * spacing - SPEED_LIMIT


def velocity_grid(vel_index):
    return (
        component(vel_index % VG),
        component(vel_index // VG % VG),
        component(vel_index // (VG * VG)),
    )


def surface_solve(incident, wall_temps, start_cov, owners, stoichiometry, sticking, surface_rates):
    precise = lax.Precision.HIGHEST
    patch_ids = jnp.arange(sticking.shape[0], dtype=jnp.int32)
    onehot = (owners[None, :] == patch_ids[:, None]).astype(jnp.float32)
    stick_face = jnp.dot(sticking.T, onehot, precision=precise)
    arrhenius = jnp.exp(ACTIVATION * (1.0 - 1.0 / wall_temps))
    desorb = jnp.dot(surface_rates[:, 0, :].T, onehot, precision=precise) * arrhenius[None, :]
    lateral = jnp.dot(surface_rates[:, 1, :].T, onehot, precision=precise)
    counts = stoichiometry.astype(jnp.float32)
    share_in = counts / (1.0 + jnp.sum(counts, axis=0, keepdims=True))
    share_out = counts / (1.0 + jnp.sum(counts, axis=1, keepdims=True))
    feed_rate = jnp.dot(share_in, stick_face * incident, precision=precise)
    covers = start_cov
    for newton_turn in range(NEWTON):
        vacant = 1.0 - jnp.sum(covers, axis=0, keepdims=True)
        cubed_cov = covers * covers * covers
        net_rate = feed_rate * vacant - desorb * covers - lateral * cubed_cov
        residual = covers - start_cov - SURFACE_STEP * net_rate
        diagonal = 1.0 + SURFACE_STEP * (desorb + 3.0 * lateral * covers * covers)
        scaled = residual / diagonal
        coupling = SURFACE_STEP * feed_rate / diagonal
        update = scaled - coupling * (
            jnp.sum(scaled, axis=0, keepdims=True)
            / (1.0 + jnp.sum(coupling, axis=0, keepdims=True))
        )
        covers = covers - DAMPING * update
    released = desorb * covers + lateral * covers * covers * covers
    vacant = 1.0 - jnp.sum(covers, axis=0, keepdims=True)
    emitted = incident * (1.0 - stick_face * vacant) + jnp.dot(
        share_out.T, released, precision=precise
    )
    return (covers, emitted)


def upwind(velocity, field, lower_cell, upper_cell):
    return jnp.maximum(velocity, 0.0) * (field - lower_cell) + jnp.minimum(velocity, 0.0) * (
        upper_cell - field
    )


def per_device(
    distribution, wall_temp, coverage, face_cell, face_owner, stoichiometry, sticking, surface_rates
):
    precise = lax.Precision.HIGHEST
    vel_rows = distribution.shape[1]
    cells_yz = distribution.shape[3]
    spacing = 2.0 * SPEED_LIMIT / VG
    weight = spacing * spacing * spacing
    vel_index = lax.axis_index("vel") * vel_rows + jnp.arange(vel_rows, dtype=jnp.int32)
    speed_x, speed_y, speed_z = velocity_grid(vel_index)
    speed_sq = speed_x * speed_x + speed_y * speed_y + speed_z * speed_z
    molecule_weights = jnp.array(SPECIES_MASS, jnp.float32)
    columns = CX * NZ
    wall_layer = distribution[:, :, :, :NZ].reshape(S, vel_rows, columns)
    toward = jnp.maximum(-speed_y, 0.0)
    column_part = weight * jnp.einsum("v,svc->sc", toward, wall_layer, precision=precise)
    face_col = face_cell[0]
    selector = (jnp.arange(columns, dtype=jnp.int32)[:, None] == face_col[None, :]).astype(
        jnp.float32
    )
    incident_part = jnp.dot(column_part, selector, precision=precise)
    outward = jnp.maximum(speed_y, 0.0)
    emission_shape = jnp.exp(
        -molecule_weights[:, None, None]
        * speed_sq[None, :, None]
        / (2.0 * wall_temp[None, None, :])
    )
    norm_part = weight * jnp.einsum("v,svf->sf", outward, emission_shape, precision=precise)
    incident, normalizer = lax.psum((incident_part, norm_part), "vel")
    covers, emitted = surface_solve(
        incident, wall_temp, coverage, face_owner, stoichiometry, sticking, surface_rates
    )
    wall_density = emitted / normalizer
    col_density = jnp.dot(wall_density, selector.T, precision=precise)
    col_temp = jnp.dot(wall_temp[None, :], selector.T, precision=precise)
    wall_ghost = col_density[:, None, :] * jnp.exp(
        -molecule_weights[:, None, None] * speed_sq[None, :, None] / (2.0 * col_temp[:, None, :])
    )
    wall_ghost = wall_ghost.reshape(S, vel_rows, CX, NZ)
    cross_y = speed_y[None, :, None, None]
    cross_z = speed_z[None, :, None, None]
    half_grid = VG // 2
    grouped = distribution.reshape(S, vel_rows // VG, VG, CX, cells_yz)
    falling = grouped[:, :, :half_grid]
    rising = grouped[:, :, half_grid:]
    from_left = shifted(rising[:, :, :, CX - 1 :], "space", 1)
    from_right = shifted(falling[:, :, :, :1], "space", -1)
    lower_rim = jnp.concatenate([from_left, rising[:, :, :, :-1]], axis=3)
    upper_rim = jnp.concatenate([falling[:, :, :, 1:], from_right], axis=3)
    x_speeds = speed_x.reshape(vel_rows // VG, VG)
    negative_part = x_speeds[None, :, :half_grid, None, None] * (upper_rim - falling)
    positive_part = x_speeds[None, :, half_grid:, None, None] * (rising - lower_rim)
    along_x = jnp.concatenate([negative_part, positive_part], axis=2).reshape(distribution.shape)
    lower_cell = jnp.concatenate([wall_ghost, distribution[:, :, :, :-NZ]], axis=3)
    upper_cell = jnp.concatenate([distribution[:, :, :, NZ:], distribution[:, :, :, -NZ:]], axis=3)
    position = jnp.arange(cells_yz, dtype=jnp.int32) % NZ
    back_cell = jnp.where(
        position == 0, jnp.roll(distribution, -(NZ - 1), axis=3), jnp.roll(distribution, 1, axis=3)
    )
    front_cell = jnp.where(
        position == NZ - 1,
        jnp.roll(distribution, NZ - 1, axis=3),
        jnp.roll(distribution, -1, axis=3),
    )
    transported = distribution - TIME_STEP * (
        along_x
        + upwind(cross_y, distribution, lower_cell, upper_cell)
        + upwind(cross_z, distribution, back_cell, front_cell)
    )
    cells = CX * cells_yz
    flattened = transported.reshape(S, vel_rows, cells)
    moment_basis = weight * jnp.stack([jnp.ones_like(speed_x), speed_x, speed_y, speed_z, speed_sq])
    partial_sums = jnp.einsum("kv,svc->skc", moment_basis, flattened, precision=precise)
    moment_totals = lax.psum(partial_sums, "vel")
    density = moment_totals[:, 0]
    combined_gas_weight = jnp.sum(density, axis=0)
    constituent_weight_per_volume = jnp.sum(molecule_weights[:, None] * density, axis=0)
    bulk_x = (
        jnp.sum(molecule_weights[:, None] * moment_totals[:, 1], axis=0)
        / constituent_weight_per_volume
    )
    bulk_y = (
        jnp.sum(molecule_weights[:, None] * moment_totals[:, 2], axis=0)
        / constituent_weight_per_volume
    )
    bulk_z = (
        jnp.sum(molecule_weights[:, None] * moment_totals[:, 3], axis=0)
        / constituent_weight_per_volume
    )
    mean_flow_norm_sq = bulk_x * bulk_x + bulk_y * bulk_y + bulk_z * bulk_z
    gas_heat_level = (
        jnp.sum(molecule_weights[:, None] * moment_totals[:, 4], axis=0)
        - constituent_weight_per_volume * mean_flow_norm_sq
    ) / (3.0 * combined_gas_weight)
    offset_x = speed_x[:, None] - bulk_x[None, :]
    offset_y = speed_y[:, None] - bulk_y[None, :]
    offset_z = speed_z[:, None] - bulk_z[None, :]
    relative_velocity_norm_sq = offset_x * offset_x + offset_y * offset_y + offset_z * offset_z
    maxwellian_argument = jnp.exp(
        -molecule_weights[:, None, None]
        * relative_velocity_norm_sq[None, :, :]
        / (2.0 * gas_heat_level[None, None, :])
    )
    maxwell_norm = lax.psum(weight * jnp.sum(maxwellian_argument, axis=1), "vel")
    maxwell = density[:, None, :] * maxwellian_argument / maxwell_norm[:, None, :]
    collision = jnp.array(COLLISION_RATE, jnp.float32)
    relaxation = 1.0 - jnp.exp(-TIME_STEP * collision[:, None] * combined_gas_weight[None, :])
    advanced = flattened + relaxation[:, None, :] * (maxwell - flattened)
    return (advanced.reshape(distribution.shape), covers)


def solution(mesh):
    return jax.shard_map(
        per_device,
        mesh=mesh,
        in_specs=(
            P(None, "vel", "space", None),
            P("space"),
            P(None, "space"),
            P("space", None),
            P("space"),
            P(),
            P(),
            P(),
        ),
        out_specs=(P(None, "vel", "space", None), P(None, "space")),
        check_vma=False,
    )
```

profile of v0, /device:TPU:2, one launch (start us, length us, event | category | flops | bytes accessed | tf_op | source)
XLA Modules:
  0.0 474.9 jit_solution(1739571930275569758)
XLA Ops:
  0.6 0.0 copy-start
  0.6 11.0 %fusion.182 = (f32[3,32,16,1,256]{4,3,2,1,0:T(1,128)}, f32[3,32,16,1,256]{4,3,2,1,0:T(1,128)}, f32[3,32,16,1,256]{4,3,2,1,0:T(1,128)}, f32[3,32,16,1,256]{4,3,2,1,0:T(1,128)}) fusion(f32[3,32,32,2,256]{4,3,2,1,0:T(2,128)} %bitcast.71), kind=kLoop, calls=%fused_computation.305 | loop fusion | bytes 12582912 | tf_op jit(solution)/shard_map/slice | solution.py:128
  11.6 2.5 collective-permute-start
  14.1 0.0 collective-permute-start.1
  14.1 0.0 slice-start.1
  14.2 8.0 %fusion.180 = (f32[3,1024,2,64]{3,2,1,0:T(2,128)S(1)}, f32[3,1024,2,64]{3,2,1,0:T(2,128)}) fusion(f32[3,1024,2,256]{3,2,1,0:T(2,128)} %param.10), kind=kLoop, calls=%fused_computation.303 | loop fusion | bytes 6291456 | tf_op jit(solution)/shard_map/slice | solution.py:93
  22.2 0.0 slice-done
  22.2 0.0 slice-done.1
  22.2 9.9 %fusion.181 = (f32[3,1024,2,192]{3,2,1,0:T(2,128)}, f32[3,1024,2,192]{3,2,1,0:T(2,128)}) fusion(f32[3,1024,2,256]{3,2,1,0:T(2,128)S(1)} %bitcast.74), kind=kLoop, calls=%fused_computation.304 | loop fusion | bytes 18874368 | tf_op jit(solution)/shard_map/slice | solution.py:133
  32.1 9.9 %fusion.183 = (f32[3,1024,2,193]{3,2,1,0:T(2,128)}, f32[3,1024,2,193]{3,2,1,0:T(2,128)}) fusion(f32[3,1024,2,256]{3,2,1,0:T(2,128)S(1)} %bitcast.74), kind=kLoop, calls=%fused_computation.306 | loop fusion | bytes 18972672 | tf_op jit(solution)/shard_map/jit(_roll_static)/slice | solution.py:137
  42.1 10.1 %fusion.186 = (f32[3,1024,2,255]{3,2,1,0:T(2,128)}, f32[3,1024,2,255]{3,2,1,0:T(2,128)}) fusion(f32[3,1024,2,256]{3,2,1,0:T(2,128)S(1)} %bitcast.74), kind=kLoop, calls=%fused_computation.309 | loop fusion | bytes 25067520 | tf_op jit(solution)/shard_map/jit(_roll_static)/slice | solution.py:137
  52.2 6.9 %fusion.184 = (f32[3,1024,2,63]{3,2,1,0:T(2,128)}, f32[3,1024,2,63]{3,2,1,0:T(2,128)}) fusion(f32[3,1024,2,256]{3,2,1,0:T(2,128)S(1)} %bitcast.74), kind=kLoop, calls=%fused_computation.307 | loop fusion | bytes 6193152 | tf_op jit(solution)/shard_map/jit(_roll_static)/slice | solution.py:137
  59.1 6.9 %fusion.185 = (f32[3,1024,2,1]{3,2,1,0:T(2,128)}, f32[3,1024,2,1]{3,2,1,0:T(2,128)}) fusion(f32[3,1024,2,256]{3,2,1,0:T(2,128)S(1)} %bitcast.74), kind=kLoop, calls=%fused_computation.308 | loop fusion | bytes 98304 | tf_op jit(solution)/shard_map/jit(_roll_static)/slice | solution.py:137
  65.9 0.1 multiply_add_fusion.3
  66.0 0.1 fusion.124
  66.1 0.0 copy-done.9
  66.1 0.0 copy-done.5
  66.2 0.1 broadcast_multiply_fusion
  66.2 1.1 fusion.13
  67.3 0.0 copy-start.4
  67.3 0.0 copy-start.10
  67.3 0.0 copy-start.2
  67.3 3.1 copy.28
  70.5 0.0 copy-done.11
  70.5 0.1 fusion.16
  70.6 2.9 convolution_reduce_fusion
  73.4 0.1 fusion.20
  73.6 0.0 copy-done.6
  73.6 0.1 convert_reduce_fusion
  73.7 0.0 copy-done.4
  73.7 0.0 copy-done
  73.8 0.2 convolution_bitcast_fusion.2
  73.9 0.2 convolution_bitcast_fusion.1
  74.2 73.9 %all-reduce = (f32[3,128]{1,0:T(4,128)S(1)}, f32[3,128]{1,0:T(4,128)S(1)}) all-reduce(f32[3,128]{1,0:T(4,128)S(1)} %bitcast_multiply_fusion.4, f32[3,128]{1,0:T(4,128)S(1)} %fusion.20), channel_id=1, replica_groups=mesh['vel'=32,'space'=8] {'vel'}, use_global_device_ids=true, to_apply=%region_28.29 | all-reduce | flops 768 | bytes 6144 | tf_op jit(solution)/shard_map/psum | solution.py:108
  148.1 0.3 fusion.138
  148.3 0.2 fusion.177
  149.4 0.0 copy-start.3
  149.4 0.1 fusion.15
  149.6 0.1 fusion.19
  149.7 0.1 mul.997
  149.9 0.1 div.322
  149.9 0.1 stack.2
  150.0 0.1 fusion.188
  150.1 8.1 %fusion.10 = f32[3,1024,2,64]{3,2,1,0:T(2,128)S(1)} fusion(f32[2,64]{1,0:T(2,128)S(1)} %div.322, f32[3,1024]{1,0:T(4,128)S(1)} %broadcast_multiply_fusion, f32[3,2,64]{2,1,0:T(2,128)S(1)} %mul.997), kind=kLoop, calls=%fused_computation.20 | loop fusion | flops 786432 | bytes 1587200 | tf_op jit(solution)/shard_map/mul | solution.py:115
  158.2 0.0 collective-permute-done
  158.2 0.0 collective-permute-done.1
  158.2 10.9 %fusion.12 = (f32[3,32,16,2,256]{4,3,2,1,0:T(2,128)}, f32[3,32,16,2,256]{4,3,2,1,0:T(2,128)}) fusion(f32[3,32,32,2,256]{4,3,2,1,0:T(2,128)} %bitcast.72, f32[3,32,16,1,256]{4,3,2,1,0:T(1,128)} %collective-permute-done, f32[3,32,16,1,256]{4,3,2,1,0:T(1,128)} %get-tuple-element.68, f32[32,16]{1,0:T(8,128)S(1)} %get-tuple-element.89, ...), kind=kLoop, calls=%fused_computation.24 | loop fusion | flops 4718592 | bytes 18878464 | tf_op jit(solution)/shard_map/mul | solution.py:130
  169.1 0.0 copy-done.3
  169.1 11.6 %pad_maximum_fusion = f32[3,32,32,2,256]{4,3,2,1,0:T(2,128)} fusion(f32[3,32,16,2,256]{4,3,2,1,0:T(2,128)} %get-tuple-element.67, f32[3,32,16,2,256]{4,3,2,1,0:T(2,128)} %get-tuple-element.66), kind=kLoop, calls=%fused_computation.1 | loop fusion | flops 1572864 | bytes 12582912 | tf_op jit(solution)/shard_map/concatenate | solution.py:132
  180.7 47.5 %multiply_subtract_fusion = f32[3,1024,2,256]{3,2,1,0:T(2,128)} fusion(f32[3,1024,2,256]{3,2,1,0:T(2,128)} %param.10, f32[3,1024,2,1]{3,2,1,0:T(2,128)} %get-tuple-element.77, f32[3,1024,2,255]{3,2,1,0:T(2,128)} %get-tuple-element.79, f32[3,1024,2,193]{3,2,1,0:T(2,128)} %get-tuple-element.73, f32[3,1024,2,63]{3,2,1,0:T(2,128)} %get-tuple-element.75, ...), kind=kLoop, calls=%fused_computation.18 | loop fusion | flops 34603008 | bytes 56640000 | tf_op jit(solution)/shard_map/sub | solution.py:144
  228.2 9.0 %reshape.769 = f32[3,1024,512]{2,1,0:T(8,128)} reshape(f32[3,1024,2,256]{3,2,1,0:T(2,128)} %multiply_subtract_fusion) | data formatting | bytes 12582912 | tf_op jit(solution)/shard_map/reshape | solution.py:150
  237.2 5.3 %convolution_bitcast_fusion = f32[3,5,512]{2,1,0:T(8,128)S(1)} fusion(f32[3,1024,512]{2,1,0:T(8,128)} %reshape.769, f32[5,1024]{1,0:T(8,128)S(1)} %stack.2), kind=kOutput, calls=%fused_computation.29 | convolution fusion | flops 94376960 | bytes 6342656 | tf_op jit(solution)/shard_map/kv,svc->skc/dot_general | solution.py:152
  242.6 0.0 copy-start.7
  242.6 139.1 %psum.30 = f32[3,5,512]{2,1,0:T(8,128)S(1)} all-reduce(f32[3,5,512]{2,1,0:T(8,128)S(1)} %convolution_bitcast_fusion), channel_id=1, replica_groups=mesh['vel'=32,'space'=8] {'vel'}, use_global_device_ids=true, to_apply=%region_29.30 | all-reduce | flops 7680 | bytes 61440 | tf_op jit(solution)/shard_map/psum | solution.py:153
  381.7 0.5 broadcast.1377
  382.2 0.7 fusion.187
  382.9 0.1 fusion.104
  383.1 0.6 multiply_add_fusion.1
  383.8 1.1 exponential_reduce_fusion
  384.9 74.0 %psum.31 = f32[3,2,256]{2,1,0:T(2,128)S(1)} all-reduce(f32[3,2,256]{2,1,0:T(2,128)S(1)} %div.345), channel_id=1, replica_groups=mesh['vel'=32,'space'=8] {'vel'}, use_global_device_ids=true, to_apply=%region_37.38 | all-reduce | flops 1536 | bytes 12288 | tf_op jit(solution)/shard_map/psum | solution.py:183
  458.9 0.1 exponential_subtract_fusion
  459.0 4.6 multiply_add_fusion.2
  463.6 0.0 copy-start.1
  463.6 10.8 %multiply_add_fusion = f32[3,1024,2,256]{3,2,1,0:T(2,128)} fusion(f32[3,1024,2,256]{3,2,1,0:T(2,128)} %multiply_subtract_fusion, f32[3,2,256]{2,1,0:T(2,128)S(1)} %psum.31, f32[2,256]{1,0:T(2,128)S(1)} %get-tuple-element.13, f32[1024,2,256]{2,1,0:T(2,128)S(1)} %multiply_add_fusion.2, f32[3]{0:T(128)S(1)} %copy-done.5, f32[3,2,256]{2,1,0:T(2,128)S(1)} %mul.1024, ...), kind=kLoop, calls=%fused_computation.16 | loop fusion | flops 11010048 | bytes 14700556 | tf_op jit(solution)/shard_map/add | solution.py:187
  (76 shorter events, 1.1 us)
Async XLA Ops:
  0.6 73.1 %copy-start = (f32[4,3]{1,0:T(4,128)S(1)}, f32[4,3]{1,0:T(4,128)}, u32[]{:S(2)}) copy-start(f32[4,3]{1,0:T(4,128)} %param.16) | copy-start | bytes 148
  11.6 146.6 %collective-permute-start = (f32[3,32,16,1,256]{4,3,2,1,0:T(1,128)}, f32[3,32,16,1,256]{4,3,2,1,0:T(1,128)}, u32[]{:S(2)}, u32[]{:S(2)}) collective-permute-start(f32[3,32,16,1,256]{4,3,2,1,0:T(1,128)} %get-tuple-element.71), channel_id=1, source_target_pairs={{0,7},{1,0},{2,1},{3,2},{4,3},{5,4},{6,5},{7,6},{8,15},{9,8},{10,9... | collective-permute-start | bytes 4718600 | tf_op jit(solution)/shard_map/ppermute | solution.py:24
  14.1 144.1 %collective-permute-start.1 = (f32[3,32,16,1,256]{4,3,2,1,0:T(1,128)}, f32[3,32,16,1,256]{4,3,2,1,0:T(1,128)}, u32[]{:S(2)}, u32[]{:S(2)}) collective-permute-start(f32[3,32,16,1,256]{4,3,2,1,0:T(1,128)} %get-tuple-element.70), channel_id=1, source_target_pairs={{0,1},{1,2},{2,3},{3,4},{4,5},{5,6},{6,7},{7,0},{8,9},{9,10},{10,1... | collective-permute-start | bytes 4718600 | tf_op jit(solution)/shard_map/ppermute | solution.py:24
  14.1 8.1 %slice-start = ((s8[6291456]{0:T(1024)(128)(4,1)}), s8[4194304]{0:T(1024)(128)(4,1)S(1)}, s32[]{:S(2)}) async-start(s8[6291456]{0:T(1024)(128)(4,1)} %bitcast.73), calls=%async_computation | async-start | bytes 8388608
  14.1 8.1 %slice-start.1 = ((s8[6291456]{0:T(1024)(128)(4,1)}), s8[2097152]{0:T(1024)(128)(4,1)S(1)}, s32[]{:S(2)}) async-start(s8[6291456]{0:T(1024)(128)(4,1)} %bitcast.73), calls=%async_computation.1 | async-start | bytes 4194304
  59.1 7.1 %copy-start.9 = (f32[128]{0:T(128)S(1)}, f32[128]{0:T(128)}, u32[]{:S(2)}) copy-start(f32[128]{0:T(128)} %param.11) | copy-start | bytes 1540
  59.1 7.1 %copy-start.5 = (f32[3]{0:T(128)S(1)}, f32[3]{0:T(128)}, u32[]{:S(2)}) copy-start(f32[3]{0:T(128)} %constant.130) | copy-start | bytes 40
  67.3 3.2 copy-start.11
  67.3 6.3 %copy-start.6 = (s32[12,3]{0,1:T(4,128)S(1)}, s32[12,3]{0,1:T(4,128)}, u32[]{:S(2)}) copy-start(s32[12,3]{0,1:T(4,128)} %param.15) | copy-start | bytes 436
  67.3 6.4 %copy-start.4 = (f32[4,2,12]{2,1,0:T(2,128)S(1)}, f32[4,2,12]{2,1,0:T(2,128)}, u32[]{:S(2)}) copy-start(f32[4,2,12]{2,1,0:T(2,128)} %param.17) | copy-start | bytes 1156
  67.3 6.4 %copy-start.10 = (s32[128]{0:T(128)S(1)}, s32[128]{0:T(128)}, u32[]{:S(2)}) copy-start(s32[128]{0:T(128)} %param.14) | copy-start | bytes 1540
  67.3 6.8 %copy-start.2 = (f32[12,128]{1,0:T(8,128)S(1)}, f32[12,128]{1,0:T(8,128)}, u32[]{:S(2)}) copy-start(f32[12,128]{1,0:T(8,128)} %param.12) | copy-start | bytes 18436
  149.4 19.7 %copy-start.3 = (f32[12,128]{1,0:T(8,128)}, f32[12,128]{1,0:T(8,128)S(1)}, u32[]{:S(2)}) copy-start(f32[12,128]{1,0:T(8,128)S(1)} %get-tuple-element.22) | copy-start | bytes 18436
  237.2 145.7 %copy-start.8 = (f32[3]{0:T(128)S(1)}, f32[3]{0:T(128)}, u32[]{:S(2)}) copy-start(f32[3]{0:T(128)} %constant.126.clone) | copy-start | bytes 40
  242.6 216.4 %copy-start.7 = (f32[3]{0:T(128)S(1)}, f32[3]{0:T(128)}, u32[]{:S(2)}) copy-start(f32[3]{0:T(128)} %constant.131) | copy-start | bytes 40
  463.6 10.8 %copy-start.1 = (f32[4,3]{1,0:T(4,128)S(1)}, f32[4,3]{1,0:T(4,128)}, u32[]{:S(2)}) copy-start(f32[4,3]{1,0:T(4,128)} %param.16) | copy-start | bytes 148
where the time goes:
time: 483 us; the launch traced here: 475 us
  blocking collectives  287 us (59%)
  other arithmetic  97.5 us (20%)
  local copies, waits for them, and re-layouts  75.8 us (16%)
  matrix products  10.7 us (2%)
    psum x1, blocking collectives, per_device(): moment_totals = lax.psum(partial_sums, 'vel')  139 us
    psum x1, blocking collectives, per_device(): lax.psum(weight * jnp.sum(maxwellian_argument, axis=1), 'vel')  74 us
    psum x1, blocking collectives, per_device(): incident, normalizer = lax.psum((incident_part, norm_part), 'vel')  73.9 us
    sub x1, other arithmetic, per_device(): distribution - TIME_STEP * (along_x + upwind(cross_y, distribution, lower...  47.5 us
    slice x2, local copies, waits for them, and re-layouts, per_device(): jnp.roll(distribution, 1, axis=3)  17 us
    slice x2, local copies, waits for them, and re-layouts, per_device(): jnp.roll(distribution, -(NZ - 1), axis=3)  16.8 us
    concatenate x1, other arithmetic, per_device(): jnp.concatenate([negative_part, positive_part], axis=2)  11.6 us
    slice x1, local copies, waits for them, and re-layouts, per_device(): upper_rim = jnp.concatenate([falling[:, :, :, 1:], from_right], axis=3)  11 us
  transfers between devices with their start and end apart: 2, of which 0 were waited for; matrix products, arithmetic and copies ran while one was open for 15% of the time, Pallas kernels for 0%

commit v1 on v0

v1 whole, which is shorter than its diff:
```python
import jax
import jax.numpy as jnp
from jax import lax
from jax.experimental import pallas as pl
from jax.experimental.pallas import tpu as pltpu
from jax.sharding import PartitionSpec as P

S = 3
VG = 32
NZ = 64
CX = 2
NEWTON = 8
NSURF = 12
PATCHES = 4
N_VEL = 32
N_SPACE = 8

SPEED_LIMIT = 4.0
SPACING = 2.0 * SPEED_LIMIT / VG
WEIGHT = SPACING * SPACING * SPACING
SPECIES_MASS = (1.0, 2.0, 4.0)
COLLISION_RATE = (0.3, 0.2, 0.15)
TIME_STEP = 0.08
SURFACE_STEP = 2.0
DAMPING = 0.25
ACTIVATION = 2.0

PAIRS = VG // 2
HALF = PAIRS // 2
BLOCKS = 12
KYS = S * VG // BLOCKS
TILE = (8, 128)
PRECISE = lax.Precision.HIGHEST


def rows():
    return lax.broadcasted_iota(jnp.int32, TILE, 0)


def lanes():
    return lax.broadcasted_iota(jnp.int32, TILE, 1)


def down(value, by):
    return pltpu.roll(value, by % 8, 0)


def along(value, by):
    return pltpu.roll(value, by % 128, 1)


def pair_speed():
    parity = (rows() >= 4).astype(jnp.float32)
    return (parity + 0.5) * SPACING - SPEED_LIMIT


def speed_of(position):
    return (position.astype(jnp.float32) + 0.5) * SPACING - SPEED_LIMIT


def moments_kernel(kz_ref, f_ref, own_ref, rim_ref, acc_ref):
    step = pl.program_id(0)
    species = step // 4
    quarter = step % 4
    half = quarter // 2
    base = pair_speed()
    speeds = [jnp.abs(base + 2.0 * SPACING * j) for j in range(PAIRS)]

    @pl.when(quarter == 0)
    def _():
        acc_ref[species] = jnp.zeros((20,) + TILE, jnp.float32)

    def one(k, carry):
        zero = jnp.zeros(TILE, jnp.float32)
        sums = []
        for side in range(2):
            n0, n1, n2, n3 = zero, zero, zero, zero
            for j in range(side * HALF, (side + 1) * HALF):
                f = f_ref[k, 8 * j : 8 * j + 8, :]
                g = f * speeds[j]
                n0 = n0 + f
                n1 = n1 + g
                g = g * speeds[j]
                n2 = n2 + g
                n3 = n3 + g * speeds[j]
            sums.append((n0, n1, n2, n3))
        (a0, a1, a2, a3), (b0, b1, b2, b3) = sums
        cy = speed_of(quarter * KYS + k)
        cy2 = cy * cy
        acy = jnp.abs(cy)
        d = a0 + b0
        x1 = b1 - a1
        e = a2 + b2 + cy2 * d
        yd = cy * d
        new = (
            d, x1, yd, e,
            b1, b2, cy * b1, b3 + cy2 * b1,
            a1, -a2, cy * a1, a3 + cy2 * a1,
            acy * d, acy * x1, acy * yd, acy * e,
        )
        return tuple(c + n for c, n in zip(carry, new))

    start = tuple(jnp.zeros(TILE, jnp.float32) for _ in range(16))
    total = lax.fori_loop(0, KYS, one, start)
    for q in range(12):
        acc_ref[species, q] += total[q]
    for q in range(4):
        acc_ref[species, 12 + 4 * half + q] += total[12 + q]

    @pl.when(step == BLOCKS - 1)
    def _():
        row = rows()
        lane = lanes()
        cz = speed_of(kz_ref[0])
        acz = jnp.abs(cz)
        rise = cz > 0.0
        odd = row % 2 == 1
        upper_h = (row // 2) % 2 == 1
        low = lane < 64
        own = []
        rim = []
        incident = []
        for s in range(S):
            full = []
            for q in range(20):
                v = acc_ref[s, q]
                full.append(v + down(v, 4))
            for q in range(4):
                b, xp, xm = full[q], full[4 + q], full[8 + q]
                ym, yp = full[12 + q], full[16 + q]
                zp = jnp.where(lane % 64 == 0, along(b, 65), along(b, 1))
                zm = jnp.where(lane % 64 == 63, along(b, 63), along(b, 127))
                shifted_z = jnp.where(rise, zp, zm)
                rp = along(yp, 64)
                rm = along(ym, 64)
                from_low = jnp.where(low, jnp.where(upper_h, down(rp, 2), 0.0), rp)
                from_high = jnp.where(low, rm, jnp.where(upper_h, ym, down(rm, -2)))
                inner = jnp.where(odd, down(xp, 1), down(xm, -1))
                stay = (1.0 - TIME_STEP * acz) * b - TIME_STEP * (xp + xm + yp + ym)
                own.append(
                    stay
                    + TIME_STEP * (acz * shifted_z + from_low + from_high + inner)
                )
                rim.append(TIME_STEP * jnp.where(odd, xp, xm))
            ym = full[12]
            incident.append(jnp.where(low, ym, along(down(ym, -1), 64)))
        for values, out in ((own, own_ref), (rim, rim_ref)):
            packed = [values[0], values[4], values[8]]
            momenta = [0.0, 0.0, 0.0, 0.0]
            for s in range(S):
                m = SPECIES_MASS[s]
                d, px, py, e = values[4 * s : 4 * s + 4]
                momenta[0] = momenta[0] + m * px
                momenta[1] = momenta[1] + m * py
                momenta[2] = momenta[2] + (m * cz) * d
                momenta[3] = momenta[3] + m * (e + cz * cz * d)
            packed = packed + momenta
            if out is own_ref:
                last = jnp.where(
                    row == 4,
                    down(incident[0], 4),
                    jnp.where(
                        row == 5,
                        down(incident[1], 5),
                        jnp.where(row == 6, down(incident[2], 6), 0.0),
                    ),
                )
            else:
                last = jnp.zeros(TILE, jnp.float32)
            packed.append(last)
            for t in range(4):
                out[t] = WEIGHT * jnp.where(row < 4, packed[2 * t], packed[2 * t + 1])


def pack_kernel(f_ref, rise_ref, fall_ref):
    odd = rows() % 2 == 1

    def one(k, carry):
        for t in range(4):
            a = f_ref[k, 16 * t : 16 * t + 8, :]
            b = f_ref[k, 16 * t + 8 : 16 * t + 16, :]
            fall_ref[k, 8 * t : 8 * t + 8, :] = jnp.where(odd, down(b, 1), a)
            a = f_ref[k, 64 + 16 * t : 64 + 16 * t + 8, :]
            b = f_ref[k, 64 + 16 * t + 8 : 64 + 16 * t + 16, :]
            rise_ref[k, 8 * t : 8 * t + 8, :] = jnp.where(odd, a, down(b, -1))
        return carry

    lax.fori_loop(0, KYS, one, 0)


def spread_kernel(own_ref, left_ref, right_ref, out_ref):
    odd = rows() % 2 == 1
    for t in range(4):
        moved = jnp.where(odd, down(right_ref[t], 1), down(left_ref[t], -1))
        value = own_ref[t] + moved
        for peer in range(N_VEL):
            out_ref[peer, t] = value


def selector(face_cell):
    column = lax.broadcasted_iota(jnp.int32, (128, 128), 0)
    return (column == face_cell).astype(jnp.float32)


def to_tile(value):
    row = rows() % 4
    low = lanes() < 64
    wide = jnp.broadcast_to(value, TILE)
    return jnp.where(
        jnp.logical_and(row == 0, low),
        wide,
        jnp.where(jnp.logical_and(row == 1, low), along(wide, 64), 0.0),
    )


def wall_kernel(
    kz_ref, stoich_ref, stick_ref, rates_ref, temp_ref, cover_ref, cell_ref, owner_ref,
    surface_ref, sums_ref, wall_x_ref, wall_y_ref,
):
    select = selector(cell_ref[...])
    pieces = jnp.concatenate(
        [cover_ref[...], temp_ref[...], owner_ref[...].astype(jnp.float32),
         jnp.zeros((2, 128), jnp.float32)], axis=0,
    )
    placed = lax.dot_general(
        pieces, select, (((1,), (1,)), ((), ())), precision=PRECISE,
        preferred_element_type=jnp.float32,
    )
    temp = placed[12:13]
    owner = placed[13:14]
    arrhenius = jnp.exp(ACTIVATION * (1.0 - 1.0 / temp))
    zero = jnp.zeros((1, 128), jnp.float32)
    masks = [jnp.abs(owner - float(p)) < 0.5 for p in range(PATCHES)]

    def by_owner(read):
        value = zero
        for p in range(PATCHES):
            value = jnp.where(masks[p], read(p), value)
        return value

    surface_ref[0] = jnp.concatenate([placed[0:12], jnp.zeros((4, 128), jnp.float32)], axis=0)
    desorb = [by_owner(lambda p: rates_ref[p, 0, j]) * arrhenius for j in range(NSURF)]
    lateral = [by_owner(lambda p: rates_ref[p, 1, j]) for j in range(NSURF)]
    stick = [by_owner(lambda p: stick_ref[p, s]) for s in range(S)]
    surface_ref[1] = jnp.concatenate(desorb + [zero] * 4, axis=0)
    surface_ref[2] = jnp.concatenate(lateral + [zero] * 4, axis=0)
    counts = [[stoich_ref[j, s].astype(jnp.float32) for s in range(S)] for j in range(NSURF)]
    for s in range(S):
        column_sum = counts[0][s]
        for j in range(1, NSURF):
            column_sum = column_sum + counts[j][s]
        into = jnp.concatenate(
            [(zero + counts[j][s]) / (zero + (1.0 + column_sum)) * stick[s] for j in range(NSURF)]
            + [zero] * 4, axis=0,
        )
        out = jnp.concatenate(
            [(zero + counts[j][s]) / (zero + (1.0 + counts[j][0] + counts[j][1] + counts[j][2]))
             for j in range(NSURF)]
            + [zero] * 4, axis=0,
        )
        surface_ref[3 + s] = into
        surface_ref[6 + s] = out

    k_rows = lax.broadcasted_iota(jnp.int32, (VG, 128), 0)
    c = speed_of(k_rows)
    up = jnp.maximum(c, 0.0)
    cz = speed_of(kz_ref[0])
    temp_tile = to_tile(temp)
    inside = temp_tile > 0.0
    safe = jnp.where(inside, temp_tile, 1.0)
    base = pair_speed()
    for s in range(S):
        m = SPECIES_MASS[s]
        e = jnp.exp(-m * (c * c) / (2.0 * temp))

        def total(v):
            return jnp.sum(v, axis=0, keepdims=True)

        s0 = total(e)
        s1 = total(c * e)
        s2 = total(c * c * e)
        u1 = total(up * e)
        u2 = total(up * c * e)
        u3 = total(up * c * c * e)
        norm = WEIGHT * u1 * s0 * s0
        scale = WEIGHT * TIME_STEP
        sums_ref[s] = jnp.concatenate(
            [
                1.0 / norm,
                scale * u1 * s0 * s0,
                scale * u1 * s1 * s0,
                scale * u2 * s0 * s0,
                scale * u1 * s0 * s1,
                scale * (u3 * s0 * s0 + u1 * s2 * s0 + u1 * s0 * s2),
                stick[s],
                zero,
            ],
            axis=0,
        )
        rate = -m / (2.0 * safe)
        ez = jnp.where(inside, jnp.exp(rate * (cz * cz)), 0.0)
        for j in range(PAIRS):
            cx = base + 2.0 * SPACING * j
            wall_x_ref[s, j] = jnp.exp(rate * (cx * cx))
            cy = (PAIRS + j + 0.5) * SPACING - SPEED_LIMIT
            wall_y_ref[s, j] = (TIME_STEP * cy) * ez * jnp.exp(rate * (cy * cy))


def solve_kernel(
    kz_ref, parts_ref, surface_ref, sums_ref, cell_ref,
    cover_ref, ex_ref, ey_ref, coef_ref,
):
    row = rows()
    totals = []
    for t in range(4):
        v = parts_ref[0, t]
        for peer in range(1, N_VEL):
            v = v + parts_ref[peer, t]
        totals.append(v)
    incident = [totals[3][4 + s : 5 + s] for s in range(S)]
    start = surface_ref[0]
    desorb = surface_ref[1]
    lateral = surface_ref[2]
    feed = (
        surface_ref[3] * incident[0]
        + surface_ref[4] * incident[1]
        + surface_ref[5] * incident[2]
    )
    covers = start

    def total(v):
        return jnp.sum(v, axis=0, keepdims=True)

    for _ in range(NEWTON):
        vacant = 1.0 - total(covers)
        squared = covers * covers
        net = feed * vacant - desorb * covers - lateral * (squared * covers)
        residual = covers - start - SURFACE_STEP * net
        inverse = 1.0 / (1.0 + SURFACE_STEP * (desorb + 3.0 * lateral * squared))
        scaled = residual * inverse
        coupling = SURFACE_STEP * feed * inverse
        update = scaled - coupling * (total(scaled) / (1.0 + total(coupling)))
        covers = covers - DAMPING * update
    released = desorb * covers + lateral * (covers * covers * covers)
    vacant = 1.0 - total(covers)
    cover_face = jnp.dot(
        covers, selector(cell_ref[...]), precision=PRECISE, preferred_element_type=jnp.float32
    )
    cover_ref[...] = cover_face[0:NSURF]

    def quantity(q):
        v = totals[q // 2]
        other = down(v, 4)
        return jnp.where(row < 4, v, other) if q % 2 == 0 else jnp.where(row < 4, other, v)

    dens = [quantity(s) for s in range(S)]
    mom = [quantity(3 + a) for a in range(3)]
    energy = quantity(6)
    wall_dens = []
    for s in range(S):
        m = SPECIES_MASS[s]
        emitted = incident[s] * (1.0 - sums_ref[s, 6:7] * vacant) + total(
            surface_ref[6 + s] * released
        )
        wd = emitted * sums_ref[s, 0:1]
        wall_dens.append(to_tile(wd))
        dens[s] = dens[s] + to_tile(wd * sums_ref[s, 1:2])
        for a in range(3):
            mom[a] = mom[a] + to_tile((m * wd) * sums_ref[s, 2 + a : 3 + a])
        energy = energy + to_tile((m * wd) * sums_ref[s, 5:6])
    gas = dens[0] + dens[1] + dens[2]
    mass = SPECIES_MASS[0] * dens[0] + SPECIES_MASS[1] * dens[1] + SPECIES_MASS[2] * dens[2]
    bulk = [v / mass for v in mom]
    flow = bulk[0] * bulk[0] + bulk[1] * bulk[1] + bulk[2] * bulk[2]
    temperature = (energy - mass * flow) / (3.0 * gas)
    base = pair_speed()
    cz = speed_of(kz_ref[0])
    for s in range(S):
        rate = -SPECIES_MASS[s] / (2.0 * temperature)

        def pair_table(drift, store):
            sum_pairs = jnp.zeros(TILE, jnp.float32)
            for j in range(PAIRS):
                off = (base + 2.0 * SPACING * j) - drift
                e = jnp.exp(rate * (off * off))
                if store:
                    ex_ref[s, j] = e
                sum_pairs = sum_pairs + e
            return sum_pairs + down(sum_pairs, 4)

        sum_x = pair_table(bulk[0], True)
        sum_z = pair_table(bulk[2], False)
        sum_y = jnp.zeros(TILE, jnp.float32)
        tables = []
        for k in range(VG):
            off = ((k + 0.5) * SPACING - SPEED_LIMIT) - bulk[1]
            e = jnp.exp(rate * (off * off))
            tables.append(e)
            sum_y = sum_y + e
        keep = jnp.exp((-TIME_STEP * COLLISION_RATE[s]) * gas)
        off = cz - bulk[2]
        own_z = jnp.exp(rate * (off * off))
        factor = (1.0 - keep) * dens[s] * own_z / (WEIGHT * sum_x * sum_y * sum_z)
        for k in range(VG):
            ey_ref[s, k] = tables[k] * factor
        coef_ref[s, 0] = keep
        coef_ref[s, 1] = keep * wall_dens[s]


def step_kernel(
    kz_ref, f_ref, left_ref, right_ref, wall_x_ref, wall_y_ref, ex_ref, ey_ref, coef_ref, out_ref,
):
    step = pl.program_id(0)
    species = step // 4
    quarter = step % 4
    row = rows()
    lane = lanes()
    odd = row % 2 == 1
    upper_h = (row // 2) % 2 == 1
    low = lane < 64
    cz = speed_of(kz_ref[0])
    acz = jnp.abs(cz)
    rise_z = cz > 0.0
    shift_z = jnp.where(rise_z, 1, 127)
    edge = (lane % 64) == jnp.where(rise_z, 63, 0)
    base = pair_speed()
    keep = coef_ref[species, 0]
    wall_scale = coef_ref[species, 1]
    coef_z = (TIME_STEP * acz) * keep
    drift = TIME_STEP * keep

    def body(lower):
        def one(k, carry):
            ky = quarter * KYS + k
            cy = speed_of(ky)
            acy = jnp.abs(cy)
            coef_y = acy * drift
            coef_own = keep - coef_z - coef_y
            if lower:
                at_wall = jnp.logical_and(low, jnp.logical_not(upper_h))
                coef_y = jnp.where(at_wall, 0.0, coef_y)
                wall = wall_y_ref[species, ky - PAIRS] * wall_scale
            else:
                at_top = jnp.logical_and(jnp.logical_not(low), upper_h)
                coef_own = jnp.where(at_top, coef_own + coef_y, coef_own)
                coef_y = jnp.where(at_top, 0.0, coef_y)
            ey = ey_ref[species, ky]
            for j in range(PAIRS):
                f = f_ref[k, 8 * j : 8 * j + 8, :]
                coef_x = jnp.abs(base + 2.0 * SPACING * j) * drift
                t = (j % HALF) // 2
                if j < HALF:
                    halo = right_ref[k, 8 * t : 8 * t + 8, :]
                    if j % 2 == 0:
                        halo = down(halo, 1)
                    fnx = jnp.where(odd, halo, down(f, -1))
                else:
                    halo = left_ref[k, 8 * t : 8 * t + 8, :]
                    if j % 2 == 0:
                        halo = down(halo, -1)
                    fnx = jnp.where(odd, down(f, 1), halo)
                swapped = along(f, 64)
                if lower:
                    fny = jnp.where(low, down(swapped, 2), swapped)
                else:
                    fny = jnp.where(low, swapped, down(swapped, -2))
                fnz = pltpu.roll(jnp.where(edge, swapped, f), shift_z, 1)
                value = (
                    coef_own * f
                    + coef_x * (fnx - f)
                    + coef_y * fny
                    + coef_z * fnz
                    + ex_ref[species, j] * ey
                )
                if lower:
                    value = value + wall_x_ref[species, j] * wall
                out_ref[k, 8 * j : 8 * j + 8, :] = value
            return carry

        lax.fori_loop(0, KYS, one, 0)

    @pl.when(quarter < 2)
    def _():
        body(False)

    @pl.when(quarter >= 2)
    def _():
        body(True)


def whole(*shape):
    return pl.BlockSpec(shape, lambda i: (0,) * len(shape))


def block(size):
    return pl.BlockSpec((KYS, size, 128), lambda i: (i, 0, 0))


SMEM = pl.BlockSpec(memory_space=pltpu.SMEM)
VMEM = pl.BlockSpec(memory_space=pltpu.VMEM)
F32 = jnp.float32


def shape(*dims):
    return jax.ShapeDtypeStruct(dims, F32)


def shifted(value, axis, by):
    peers = lax.axis_size(axis)
    return lax.ppermute(value, axis, [(i, (i + by) % peers) for i in range(peers)])


def per_device(
    distribution, wall_temp, coverage, face_cell, face_owner, stoichiometry, sticking, surface_rates
):
    kz = lax.axis_index("vel").astype(jnp.int32).reshape(1)
    field = (
        distribution.reshape(S, VG * VG, CX, 2, 128)
        .transpose(0, 1, 3, 2, 4)
        .reshape(S * VG, 128, 128)
    )
    own, rim = pl.pallas_call(
        moments_kernel,
        grid=(BLOCKS,),
        in_specs=[SMEM, block(128)],
        out_specs=[whole(4, 8, 128)] * 2,
        out_shape=[shape(4, 8, 128)] * 2,
        scratch_shapes=[pltpu.VMEM((S, 20, 8, 128), F32)],
    )(kz, field)
    rim_left = shifted(rim, "space", 1)
    rim_right = shifted(rim, "space", -1)
    rise, fall = pl.pallas_call(
        pack_kernel,
        grid=(BLOCKS,),
        in_specs=[block(128)],
        out_specs=[block(32)] * 2,
        out_shape=[shape(S * VG, 32, 128)] * 2,
    )(field)
    from_left = shifted(rise, "space", 1)
    from_right = shifted(fall, "space", -1)
    copies = pl.pallas_call(
        spread_kernel,
        in_specs=[VMEM] * 3,
        out_specs=VMEM,
        out_shape=shape(N_VEL, 4, 8, 128),
    )(own, rim_left, rim_right)
    parts = lax.all_to_all(copies, "vel", 0, 0)
    face_row = face_cell.reshape(1, 128)
    surface, sums, wall_x, wall_y = pl.pallas_call(
        wall_kernel,
        in_specs=[SMEM] * 4 + [VMEM] * 4,
        out_specs=[VMEM] * 4,
        out_shape=[shape(9, 16, 128), shape(S, 8, 128), shape(S, 16, 8, 128), shape(S, 16, 8, 128)],
    )(
        kz, stoichiometry, sticking, surface_rates,
        wall_temp.reshape(1, 128), coverage, face_row, face_owner.reshape(1, 128),
    )
    covers, ex, ey, coef = pl.pallas_call(
        solve_kernel,
        in_specs=[SMEM] + [VMEM] * 4,
        out_specs=[VMEM] * 4,
        out_shape=[
            shape(NSURF, 128), shape(S, 16, 8, 128), shape(S, 32, 8, 128), shape(S, 2, 8, 128)
        ],
    )(kz, parts, surface, sums, face_row)
    advanced = pl.pallas_call(
        step_kernel,
        grid=(BLOCKS,),
        in_specs=[
            SMEM, block(128), block(32), block(32),
            whole(S, 16, 8, 128), whole(S, 16, 8, 128), whole(S, 16, 8, 128),
            whole(S, 32, 8, 128), whole(S, 2, 8, 128),
        ],
        out_specs=block(128),
        out_shape=shape(S * VG, 128, 128),
    )(kz, field, from_left, from_right, wall_x, wall_y, ex, ey, coef)
    advanced = (
        advanced.reshape(S, VG * VG, 2, CX, 128)
        .transpose(0, 1, 3, 2, 4)
        .reshape(distribution.shape)
    )
    return advanced, covers


def solution(mesh):
    return jax.shard_map(
        per_device,
        mesh=mesh,
        in_specs=(
            P(None, "vel", "space", None),
            P("space"),
            P(None, "space"),
            P("space", None),
            P("space"),
            P(),
            P(),
            P(),
        ),
        out_specs=(P(None, "vel", "space", None), P(None, "space")),
        check_vma=False,
    )
```

time: 483 us -> 85.8 us (0.18)
  the two profiles are of different devices: /device:TPU:2 before, /device:TPU:32 now
where the time goes in v1:
time: 85.8 us; the launch traced here: 84.3 us
  Pallas kernels  41.9 us (49%)
  waiting for transfers between devices  23.9 us (28%)
  starting transfers between devices  14.7 us (17%)
  local copies, waits for them, and re-layouts  3.23 us (4%)
    pallas_call x1, Pallas kernels, per_device(): pl.pallas_call(step_kernel, grid=(BLOCKS,), in_specs=[SMEM, block(128), b...  18.1 us
    all_to_all x1, waiting for transfers between devices, per_device(): parts = lax.all_to_all(copies, 'vel', 0, 0)  14.7 us
    all_to_all x1, starting transfers between devices, per_device(): parts = lax.all_to_all(copies, 'vel', 0, 0)  11.2 us
    ppermute x4, waiting for transfers between devices, shifted(): lax.ppermute(value, axis, [(i, (i + by) % peers) for i in range(peers)])  9.2 us
    pallas_call x1, Pallas kernels, per_device(): pl.pallas_call(moments_kernel, grid=(BLOCKS,), in_specs=[SMEM, block(128)...  8.77 us
    pallas_call x1, Pallas kernels, per_device(): pl.pallas_call(pack_kernel, grid=(BLOCKS,), in_specs=[block(128)], out_sp...  8.67 us
    ppermute x4, starting transfers between devices, shifted(): lax.ppermute(value, axis, [(i, (i + by) % peers) for i in range(peers)])  3.47 us
    unnamed x11, local copies, waits for them, and re-layouts  3.23 us
  transfers between devices with their start and end apart: 5, of which 3 were waited for; matrix products, arithmetic and copies ran while one was open for 1% of the time, Pallas kernels for 18%

profile of v1, /device:TPU:32, one launch (start us, length us, event | category | flops | bytes accessed | tf_op | source)
XLA Modules:
  0.0 84.3 jit_solution(7479542674062173698)
XLA Ops:
  0.6 8.7 %shard_map.95 = (f32[96,32,128]{2,1,0:T(8,128)}, f32[96,32,128]{2,1,0:T(8,128)}) custom-call(f32[96,128,128]{2,1,0:T(8,128)} %bitcast.13), custom_call_target="tpu_custom_call" | custom-call | tf_op jit(solution)/shard_map/pallas_call | solution.py:532
  9.3 0.0 collective-permute-start
  9.3 3.0 %collective-permute-start.1 = (f32[96,32,128]{2,1,0:T(8,128)}, f32[96,32,128]{2,1,0:T(8,128)}, u32[]{:S(2)}, u32[]{:S(2)}) collective-permute-start(f32[96,32,128]{2,1,0:T(8,128)} %get-tuple-element.15), channel_id=1, source_target_pairs={{0,7},{1,0},{2,1},{3,2},{4,3},{5,4},{6,5},{7,6},{8,15},{9,8},{10,9... | collective-permute-start | bytes 4718600 | tf_op jit(solution)/shard_map/ppermute | solution.py:510
  12.3 8.8 %shard_map.97 = (f32[4,8,128]{2,1,0:T(8,128)}, f32[4,8,128]{2,1,0:T(8,128)}) custom-call(s32[1]{0:T(128)} %bitcast.kz_ref, f32[96,128,128]{2,1,0:T(8,128)} %bitcast.14), custom_call_target="tpu_custom_call" | custom-call | tf_op jit(solution)/shard_map/pallas_call | solution.py:522
  21.0 0.0 copy-start.4
  21.0 0.2 collective-permute-start.3
  21.2 0.3 collective-permute-start.2
  21.5 9.0 %collective-permute-done.3.right_ref = f32[4,8,128]{2,1,0:T(8,128)S(1)} collective-permute-done((f32[4,8,128]{2,1,0:T(8,128)}, f32[4,8,128]{2,1,0:T(8,128)S(1)}, u32[]{:S(2)}, u32[]{:S(2)}) %collective-permute-start.3) | collective-permute-done | bytes 16416 | tf_op jit(solution)/shard_map/ppermute | solution.py:510
  30.6 0.0 copy-start.2
  30.6 0.2 collective-permute-done.2.left_ref
  30.7 0.0 copy-start.3
  30.7 0.4 copy-done.2
  31.2 0.2 copy-done.3
  31.3 1.6 %shard_map.98 = f32[32,4,8,128]{3,2,1,0:T(8,128)} custom-call(f32[4,8,128]{2,1,0:T(8,128)} %get-tuple-element.18.own_ref, f32[4,8,128]{2,1,0:T(8,128)} %copy-done.3, f32[4,8,128]{2,1,0:T(8,128)} %copy-done.2), custom_call_target="tpu_custom_call" | custom-call | tf_op jit(solution)/shard_map/pallas_call | solution.py:541
  33.0 11.2 %all-to-all-start = ((f32[32,4,8,128]{3,2,1,0:T(8,128)}), f32[32,4,8,128]{3,2,1,0:T(8,128)S(1)}, u32[]{:S(2)}, u32[]{:S(2)}) async-start(f32[32,4,8,128]{3,2,1,0:T(8,128)} %shard_map.98), calls=%async_computation | async-start | bytes 1048576 | tf_op jit(solution)/shard_map/all_to_all | solution.py:547
  44.2 0.0 copy-done.4
  44.2 0.7 copy.11.stoich_ref
  44.8 2.2 %shard_map.96 = (f32[9,16,128]{2,1,0:T(8,128)}, f32[3,8,128]{2,1,0:T(8,128)}, f32[3,16,8,128]{3,2,1,0:T(8,128)}, f32[3,16,8,128]{3,2,1,0:T(8,128)}) custom-call(s32[1]{0:T(128)} %bitcast.kz_ref, s32[12,3]{1,0:T(8,128)} %copy.11.stoich_ref, f32[4,3]{1,0:T(4,128)} %stick_ref.1, f32[4,2,12]{2,1,0:T(2,128)} %rates_ref.1, f32[1,128]{1,0:T(1,128)} %bitcast.17, ...), custom_call_target="tpu_custom_call" | custom-call | tf_op jit(solution)/shard_map/pallas_call | solution.py:549
  47.1 14.7 %all-to-all-done.parts_ref = f32[32,4,8,128]{3,2,1,0:T(8,128)S(1)} async-done(((f32[32,4,8,128]{3,2,1,0:T(8,128)}), f32[32,4,8,128]{3,2,1,0:T(8,128)S(1)}, u32[]{:S(2)}, u32[]{:S(2)}) %all-to-all-start) | async-done | bytes 524320 | tf_op jit(solution)/shard_map/all_to_all | solution.py:547
  61.7 0.0 copy-start
  61.7 0.8 copy-done
  62.6 2.5 %shard_map.99 = (f32[12,128]{1,0:T(8,128)}, f32[3,16,8,128]{3,2,1,0:T(8,128)}, f32[3,32,8,128]{3,2,1,0:T(8,128)}, f32[3,2,8,128]{3,2,1,0:T(8,128)}) custom-call(s32[1]{0:T(128)} %bitcast.kz_ref, f32[32,4,8,128]{3,2,1,0:T(8,128)} %copy-done, f32[9,16,128]{2,1,0:T(8,128)} %get-tuple-element.20.surface_ref, f32[3,8,128]{2,1,0:T(8,128)} %get-tuple-element.21.sums_ref, ...), custom_call_target="tpu_custom_call" | custom-call | tf_op jit(solution)/shard_map/pallas_call | solution.py:558
  65.0 0.0 collective-permute-done.left_ref
  65.0 0.0 copy-start.1
  65.0 0.0 collective-permute-done.1.right_ref
  65.0 1.1 %copy-done.1 = f32[96,32,128]{2,1,0:T(8,128)} copy-done((f32[96,32,128]{2,1,0:T(8,128)}, f32[96,32,128]{2,1,0:T(8,128)S(1)}, u32[]{:S(2)}) %copy-start.1) | copy-done | bytes 1572888
  66.2 18.1 %shard_map.100 = f32[96,128,128]{2,1,0:T(8,128)} custom-call(s32[1]{0:T(128)} %bitcast.kz_ref, f32[96,128,128]{2,1,0:T(8,128)} %bitcast.15, f32[96,32,128]{2,1,0:T(8,128)} %copy-done.1, f32[96,32,128]{2,1,0:T(8,128)} %collective-permute-done.1.right_ref, f32[3,16,8,128]{3,2,1,0:T(8,128)} %get-tuple-element.16.wall_x_ref, ...), custom_call_target="tpu_custom_call" | custom-call | tf_op jit(solution)/shard_map/pallas_call | solution.py:566
Async XLA Ops:
  9.3 55.7 %collective-permute-start = (f32[96,32,128]{2,1,0:T(8,128)}, f32[96,32,128]{2,1,0:T(8,128)S(1)}, u32[]{:S(2)}, u32[]{:S(2)}) collective-permute-start(f32[96,32,128]{2,1,0:T(8,128)} %get-tuple-element.14), channel_id=1, source_target_pairs={{0,1},{1,2},{2,3},{3,4},{4,5},{5,6},{6,7},{7,0},{8,9},{9,10},{10,1... | collective-permute-start | bytes 4718600 | tf_op jit(solution)/shard_map/ppermute | solution.py:510
  9.3 55.7 %collective-permute-start.1 = (f32[96,32,128]{2,1,0:T(8,128)}, f32[96,32,128]{2,1,0:T(8,128)}, u32[]{:S(2)}, u32[]{:S(2)}) collective-permute-start(f32[96,32,128]{2,1,0:T(8,128)} %get-tuple-element.15), channel_id=1, source_target_pairs={{0,7},{1,0},{2,1},{3,2},{4,3},{5,4},{6,5},{7,6},{8,15},{9,8},{10,9... | collective-permute-start | bytes 4718600 | tf_op jit(solution)/shard_map/ppermute | solution.py:510
  21.0 23.1 %copy-start.4 = (s32[12,3]{0,1:T(4,128)S(1)}, s32[12,3]{0,1:T(4,128)}, u32[]{:S(2)}) copy-start(s32[12,3]{0,1:T(4,128)} %param.13) | copy-start | bytes 436
  21.0 9.5 %collective-permute-start.3 = (f32[4,8,128]{2,1,0:T(8,128)}, f32[4,8,128]{2,1,0:T(8,128)S(1)}, u32[]{:S(2)}, u32[]{:S(2)}) collective-permute-start(f32[4,8,128]{2,1,0:T(8,128)} %get-tuple-element.19), channel_id=1, source_target_pairs={{0,7},{1,0},{2,1},{3,2},{4,3},{5,4},{6,5},{7,6},{8,15},{9,8},{10,9... | collective-permute-start | bytes 49160 | tf_op jit(solution)/shard_map/ppermute | solution.py:510
  21.2 9.5 %collective-permute-start.2 = (f32[4,8,128]{2,1,0:T(8,128)}, f32[4,8,128]{2,1,0:T(8,128)S(1)}, u32[]{:S(2)}, u32[]{:S(2)}) collective-permute-start(f32[4,8,128]{2,1,0:T(8,128)} %get-tuple-element.19), channel_id=1, source_target_pairs={{0,1},{1,2},{2,3},{3,4},{4,5},{5,6},{6,7},{7,0},{8,9},{9,10},{10,1... | collective-permute-start | bytes 49160 | tf_op jit(solution)/shard_map/ppermute | solution.py:510
  30.6 0.6 copy-start.2
  30.7 0.6 copy-start.3
  33.0 28.8 %all-to-all-start = ((f32[32,4,8,128]{3,2,1,0:T(8,128)}), f32[32,4,8,128]{3,2,1,0:T(8,128)S(1)}, u32[]{:S(2)}, u32[]{:S(2)}) async-start(f32[32,4,8,128]{3,2,1,0:T(8,128)} %shard_map.98), calls=%async_computation | async-start | bytes 1048576 | tf_op jit(solution)/shard_map/all_to_all | solution.py:547
  61.7 0.8 copy-start
  65.0 1.2 %copy-start.1 = (f32[96,32,128]{2,1,0:T(8,128)}, f32[96,32,128]{2,1,0:T(8,128)S(1)}, u32[]{:S(2)}) copy-start(f32[96,32,128]{2,1,0:T(8,128)S(1)} %collective-permute-done.left_ref) | copy-start | bytes 4718596

commit v2 on v1

v2 whole, which is shorter than its diff:
```python
import jax
import jax.numpy as jnp
from jax import lax
from jax.experimental import pallas as pl
from jax.experimental.pallas import tpu as pltpu
from jax.sharding import Mesh
from jax.sharding import PartitionSpec as P

S = 3
VG = 32
NZ = 64
CX = 2
NEWTON = 8
NSURF = 12
PATCHES = 4
N_Z = 8
N_X = 4

SPEED_LIMIT = 4.0
SPACING = 2.0 * SPEED_LIMIT / VG
WEIGHT = SPACING * SPACING * SPACING
SPECIES_MASS = (1.0, 2.0, 4.0)
COLLISION_RATE = (0.3, 0.2, 0.15)
TIME_STEP = 0.08
SURFACE_STEP = 2.0
DAMPING = 0.25
ACTIVATION = 2.0

PAIRS = VG // 2
HALF = PAIRS // 2
BLOCKS = 12
KYS = S * VG // BLOCKS
TILE = (8, 128)
PRECISE = lax.Precision.HIGHEST


def rows():
    return lax.broadcasted_iota(jnp.int32, TILE, 0)


def lanes():
    return lax.broadcasted_iota(jnp.int32, TILE, 1)


def down(value, by):
    return pltpu.roll(value, by % 8, 0)


def along(value, by):
    return pltpu.roll(value, by % 128, 1)


def pair_speed():
    parity = (rows() >= 4).astype(jnp.float32)
    return (parity + 0.5) * SPACING - SPEED_LIMIT


def speed_of(position):
    return (position.astype(jnp.float32) + 0.5) * SPACING - SPEED_LIMIT


def chunk(src, dst, sems, c):
    part = pl.ds(c * KYS, KYS)
    return pltpu.make_async_copy(src.at[part], dst.at[part], sems.at[c])


def moments_kernel(
    kz_ref, f_hbm, own_ref, to_right_ref, to_left_ref, rise_ref, fall_ref, f_ref, acc_ref, f_sem,
):
    for c in range(BLOCKS):
        chunk(f_hbm, f_ref, f_sem, c).start()
    base = pair_speed()
    speeds = [jnp.abs(base + 2.0 * SPACING * j) for j in range(PAIRS)]
    acc_ref[...] = jnp.zeros_like(acc_ref)

    def one(k, carry):
        zero = jnp.zeros(TILE, jnp.float32)
        sums = []
        for side in range(2):
            n0, n1, n2, n3 = zero, zero, zero, zero
            for j in range(side * HALF, (side + 1) * HALF):
                f = f_ref[k, 8 * j : 8 * j + 8, :]
                g = f * speeds[j]
                n0 = n0 + f
                n1 = n1 + g
                g = g * speeds[j]
                n2 = n2 + g
                n3 = n3 + g * speeds[j]
            sums.append((n0, n1, n2, n3))
        (a0, a1, a2, a3), (b0, b1, b2, b3) = sums
        for h in range(2):
            for q in range(2):
                to = pl.ds(16 * h + 8 * q, 8)
                fall_ref[k, to, :] = f_ref[k, pl.ds(32 * q + 2 * h, 8, 4), :]
                rise_ref[k, to, :] = f_ref[k, pl.ds(64 + 32 * q + 2 * h + 1, 8, 4), :]
        cy = speed_of(k % VG)
        cy2 = cy * cy
        acy = jnp.abs(cy)
        d = a0 + b0
        x1 = b1 - a1
        e = a2 + b2 + cy2 * d
        yd = cy * d
        new = (
            d, x1, yd, e,
            b1, b2, cy * b1, b3 + cy2 * b1,
            a1, -a2, cy * a1, a3 + cy2 * a1,
            acy * d, acy * x1, acy * yd, acy * e,
        )
        return tuple(c + n for c, n in zip(carry, new))

    start = tuple(jnp.zeros(TILE, jnp.float32) for _ in range(16))
    def turn(c, carry):
        species, half = c // 4, c % 4 // 2
        chunk(f_hbm, f_ref, f_sem, c).wait()
        total = lax.fori_loop(0, KYS, lambda i, v: one(c * KYS + i, v), start, unroll=4)
        for q in range(12):
            acc_ref[species, q] += total[q]
        for q in range(4):
            acc_ref[species, 12 + 4 * half + q] += total[12 + q]
        return carry

    lax.fori_loop(0, BLOCKS, turn, 0)
    row = rows()
    lane = lanes()
    cz = speed_of(kz_ref[0])
    acz = jnp.abs(cz)
    rise = cz > 0.0
    odd = row % 2 == 1
    upper_h = (row // 2) % 2 == 1
    low = lane < 64
    own = []
    rim = []
    incident = []
    for s in range(S):
        full = []
        for q in range(20):
            v = acc_ref[s, q]
            full.append(v + down(v, 4))
        for q in range(4):
            b, xp, xm = full[q], full[4 + q], full[8 + q]
            ym, yp = full[12 + q], full[16 + q]
            zp = jnp.where(lane % 64 == 0, along(b, 65), along(b, 1))
            zm = jnp.where(lane % 64 == 63, along(b, 63), along(b, 127))
            shifted_z = jnp.where(rise, zp, zm)
            rp = along(yp, 64)
            rm = along(ym, 64)
            from_low = jnp.where(low, jnp.where(upper_h, down(rp, 2), 0.0), rp)
            from_high = jnp.where(low, rm, jnp.where(upper_h, ym, down(rm, -2)))
            inner = jnp.where(odd, down(xp, 1), down(xm, -1))
            stay = (1.0 - TIME_STEP * acz) * b - TIME_STEP * (xp + xm + yp + ym)
            own.append(
                stay
                + TIME_STEP * (acz * shifted_z + from_low + from_high + inner)
            )
            rim.append(TIME_STEP * jnp.where(odd, xp, xm))
        ym = full[12]
        incident.append(jnp.where(low, ym, along(down(ym, -1), 64)))
    for values, out in ((own, own_ref), (rim, None)):
        packed = [values[0], values[4], values[8]]
        momenta = [0.0, 0.0, 0.0, 0.0]
        for s in range(S):
            m = SPECIES_MASS[s]
            d, px, py, e = values[4 * s : 4 * s + 4]
            momenta[0] = momenta[0] + m * px
            momenta[1] = momenta[1] + m * py
            momenta[2] = momenta[2] + (m * cz) * d
            momenta[3] = momenta[3] + m * (e + cz * cz * d)
        packed = packed + momenta
        if out is own_ref:
            last = jnp.where(
                row == 4,
                down(incident[0], 4),
                jnp.where(
                    row == 5,
                    down(incident[1], 5),
                    jnp.where(row == 6, down(incident[2], 6), 0.0),
                ),
            )
        else:
            last = jnp.zeros(TILE, jnp.float32)
        packed.append(last)
        for t in range(4):
            value = WEIGHT * jnp.where(row < 4, packed[2 * t], packed[2 * t + 1])
            if out is own_ref:
                out[t] = value
            else:
                to_right_ref[t] = jnp.where(odd, 0.0, down(value, -1))
                to_left_ref[t] = jnp.where(odd, down(value, 1), 0.0)


def selector(face_cell):
    column = lax.broadcasted_iota(jnp.int32, (128, 128), 0)
    return (column == face_cell).astype(jnp.float32)


def to_tile(value):
    row = rows() % 4
    low = lanes() < 64
    wide = jnp.broadcast_to(value, TILE)
    return jnp.where(
        jnp.logical_and(row == 0, low),
        wide,
        jnp.where(jnp.logical_and(row == 1, low), along(wide, 64), 0.0),
    )


def wall_kernel(
    kz_ref, stoich_ref, stick_ref, rates_ref, temp_ref, cover_ref, cell_ref, owner_ref,
    surface_ref, sums_ref, wall_x_ref, wall_y_ref,
):
    select = selector(cell_ref[...])
    pieces = jnp.concatenate(
        [cover_ref[...], temp_ref[...], owner_ref[...].astype(jnp.float32),
         jnp.zeros((2, 128), jnp.float32)], axis=0,
    )
    placed = lax.dot_general(
        pieces, select, (((1,), (1,)), ((), ())), precision=PRECISE,
        preferred_element_type=jnp.float32,
    )
    temp = placed[12:13]
    owner = placed[13:14]
    arrhenius = jnp.exp(ACTIVATION * (1.0 - 1.0 / temp))
    zero = jnp.zeros((1, 128), jnp.float32)
    masks = [jnp.abs(owner - float(p)) < 0.5 for p in range(PATCHES)]

    def by_owner(read):
        value = zero
        for p in range(PATCHES):
            value = jnp.where(masks[p], read(p), value)
        return value

    surface_ref[0] = jnp.concatenate([placed[0:12], jnp.zeros((4, 128), jnp.float32)], axis=0)
    desorb = [by_owner(lambda p: rates_ref[p, 0, j]) * arrhenius for j in range(NSURF)]
    lateral = [by_owner(lambda p: rates_ref[p, 1, j]) for j in range(NSURF)]
    stick = [by_owner(lambda p: stick_ref[p, s]) for s in range(S)]
    surface_ref[1] = jnp.concatenate(desorb + [zero] * 4, axis=0)
    surface_ref[2] = jnp.concatenate(lateral + [zero] * 4, axis=0)
    counts = [[stoich_ref[j, s].astype(jnp.float32) for s in range(S)] for j in range(NSURF)]
    for s in range(S):
        column_sum = counts[0][s]
        for j in range(1, NSURF):
            column_sum = column_sum + counts[j][s]
        into = jnp.concatenate(
            [(zero + counts[j][s]) / (zero + (1.0 + column_sum)) * stick[s] for j in range(NSURF)]
            + [zero] * 4, axis=0,
        )
        out = jnp.concatenate(
            [(zero + counts[j][s]) / (zero + (1.0 + counts[j][0] + counts[j][1] + counts[j][2]))
             for j in range(NSURF)]
            + [zero] * 4, axis=0,
        )
        surface_ref[3 + s] = into
        surface_ref[6 + s] = out

    k_rows = lax.broadcasted_iota(jnp.int32, (VG, 128), 0)
    c = speed_of(k_rows)
    up = jnp.maximum(c, 0.0)
    cz = speed_of(kz_ref[0])
    cy = c[VG // 2 :]
    temps = [temp, pltpu.roll(temp, 64, 1)]
    for s in range(S):
        m = SPECIES_MASS[s]
        e = jnp.exp(-m * (c * c) / (2.0 * temp))

        def total(v):
            return jnp.sum(v, axis=0, keepdims=True)

        s0 = total(e)
        s1 = total(c * e)
        s2 = total(c * c * e)
        u1 = total(up * e)
        u2 = total(up * c * e)
        u3 = total(up * c * c * e)
        norm = WEIGHT * u1 * s0 * s0
        scale = WEIGHT * TIME_STEP
        sums_ref[s] = jnp.concatenate(
            [
                1.0 / norm,
                scale * u1 * s0 * s0,
                scale * u1 * s1 * s0,
                scale * u2 * s0 * s0,
                scale * u1 * s0 * s1,
                scale * (u3 * s0 * s0 + u1 * s2 * s0 + u1 * s0 * s2),
                stick[s],
                zero,
            ],
            axis=0,
        )
        for x in range(CX):
            rate = -m / (2.0 * temps[x])
            wall_x_ref[s, x] = jnp.exp(rate * (c * c))
            wall_y_ref[s, x] = (TIME_STEP * cy) * jnp.exp(rate * (cy * cy)) * jnp.exp(rate * (cz * cz))


def step_kernel(
    kz_ref, parts_ref, surface_ref, sums_ref, cell_ref, wall_x_ref, wall_y_ref,
    left_ref, right_ref, f_hbm,
    cover_ref, out_hbm,
    f_ref, out_ref, ex_ref, ey_ref, wy_ref, f_sem, out_sem,
):
    for c in range(BLOCKS):
        chunk(f_hbm, f_ref, f_sem, c).start()
    row = rows()
    totals = []
    for t in range(4):
        v = parts_ref[0, t]
        for peer in range(1, N_Z):
            v = v + parts_ref[peer, t]
        totals.append(v)
    incident = [totals[3][4 + s : 5 + s] for s in range(S)]
    start = surface_ref[0]
    desorb = surface_ref[1]
    lateral = surface_ref[2]
    feed = (
        surface_ref[3] * incident[0]
        + surface_ref[4] * incident[1]
        + surface_ref[5] * incident[2]
    )
    covers = start

    def total(v):
        return jnp.sum(v, axis=0, keepdims=True)

    for _ in range(NEWTON):
        vacant = 1.0 - total(covers)
        squared = covers * covers
        net = feed * vacant - desorb * covers - lateral * (squared * covers)
        residual = covers - start - SURFACE_STEP * net
        inverse = 1.0 / (1.0 + SURFACE_STEP * (desorb + 3.0 * lateral * squared))
        scaled = residual * inverse
        coupling = SURFACE_STEP * feed * inverse
        update = scaled - coupling * (total(scaled) / (1.0 + total(coupling)))
        covers = covers - DAMPING * update
    released = desorb * covers + lateral * (covers * covers * covers)
    vacant = 1.0 - total(covers)
    cover_face = jnp.dot(
        covers, selector(cell_ref[...]), precision=PRECISE, preferred_element_type=jnp.float32
    )
    cover_ref[...] = cover_face[0:NSURF]

    def quantity(q):
        v = totals[q // 2]
        other = down(v, 4)
        return jnp.where(row < 4, v, other) if q % 2 == 0 else jnp.where(row < 4, other, v)

    dens = [quantity(s) for s in range(S)]
    mom = [quantity(3 + a) for a in range(3)]
    energy = quantity(6)
    wall_dens = []
    for s in range(S):
        m = SPECIES_MASS[s]
        emitted = incident[s] * (1.0 - sums_ref[s, 6:7] * vacant) + total(
            surface_ref[6 + s] * released
        )
        wd = emitted * sums_ref[s, 0:1]
        wall_dens.append(wd)
        dens[s] = dens[s] + to_tile(wd * sums_ref[s, 1:2])
        for a in range(3):
            mom[a] = mom[a] + to_tile((m * wd) * sums_ref[s, 2 + a : 3 + a])
        energy = energy + to_tile((m * wd) * sums_ref[s, 5:6])
    gas = dens[0] + dens[1] + dens[2]
    mass = SPECIES_MASS[0] * dens[0] + SPECIES_MASS[1] * dens[1] + SPECIES_MASS[2] * dens[2]
    bulk = [v / mass for v in mom]
    flow = bulk[0] * bulk[0] + bulk[1] * bulk[1] + bulk[2] * bulk[2]
    temperature = (energy - mass * flow) / (3.0 * gas)
    cz = speed_of(kz_ref[0])
    grid = speed_of(lax.broadcasted_iota(jnp.int32, (VG, 128), 0))
    keeps = []
    for s in range(S):
        rate = -SPECIES_MASS[s] / (2.0 * temperature)
        keep = jnp.exp((-TIME_STEP * COLLISION_RATE[s]) * gas)
        off = cz - bulk[2]
        scale = (1.0 - keep) * dens[s] * jnp.exp(rate * (off * off))
        keeps.append(keep)
        for r in range(4):
            at = slice(r, r + 1)

            def table(drift):
                gap = grid - drift[at]
                return jnp.exp(rate[at] * (gap * gap))

            ex = table(bulk[0])
            ey = table(bulk[1])
            factor = scale[at] / (WEIGHT * total(ex) * total(ey) * total(table(bulk[2])))
            ex_ref[s, r] = ex
            ey_ref[s, r] = ey * factor
        other = pltpu.roll(wall_dens[s], 64, 1)
        wy_ref[s, 0] = wall_y_ref[s, 0] * wall_dens[s]
        wy_ref[s, 1] = wall_y_ref[s, 1] * other

    lane = lanes()
    low = lane < 64
    acz = jnp.abs(cz)
    rise_z = cz > 0.0
    shift_z = jnp.where(rise_z, 1, 127)
    edge = (lane % 64) == jnp.where(rise_z, 63, 0)
    coef_z = TIME_STEP * acz
    octet = speed_of(lax.broadcasted_iota(jnp.int32, TILE, 0))
    coef_x = [TIME_STEP * jnp.abs(octet + 8.0 * SPACING * q) for q in range(4)]

    for s in range(S):
        keep = [jnp.broadcast_to(keeps[s][r : r + 1], TILE) for r in range(4)]
        for lower in (False, True):

            def one(k, carry, s=s, lower=lower, keep=keep):
                ky = k - s * VG
                acy = jnp.abs(speed_of(ky))
                coef_y = TIME_STEP * acy
                coef_own = 1.0 - coef_z - coef_y
                ey = [
                    jnp.broadcast_to(ey_ref[s, r, pl.ds(ky, 1), :], TILE) for r in range(4)
                ]
                if lower:
                    wy = [
                        jnp.broadcast_to(wy_ref[s, x, pl.ds(ky - PAIRS, 1), :], TILE)
                        for x in range(CX)
                    ]
                for q in range(4):
                    f = [f_ref[k, pl.ds(32 * q + r, 8, 4), :] for r in range(4)]
                    far = [along(v, 64) for v in f]
                    for r in range(4):
                        h, x = r // 2, r % 2
                        if q < 2:
                            near = f[r + 1] if x == 0 else right_ref[k, pl.ds(16 * h + 8 * q, 8), :]
                        else:
                            near = (
                                f[r - 1] if x == 1
                                else left_ref[k, pl.ds(16 * h + 8 * (q - 2), 8), :]
                            )
                        value = (
                            coef_own * f[r]
                            + coef_x[q] * (near - f[r])
                            + coef_z * pltpu.roll(jnp.where(edge, far[r], f[r]), shift_z, 1)
                        )
                        if lower and h == 0:
                            wall = wall_x_ref[s, x, 8 * q : 8 * q + 8, :] * wy[x]
                            value = value + jnp.where(low, wall, coef_y * far[r])
                        elif lower or h == 0:
                            value = value + coef_y * jnp.where(low, far[x], far[x + 2])
                        else:
                            value = value + coef_y * jnp.where(low, far[r], f[r])
                        value = keep[r] * value + ex_ref[s, r, 8 * q : 8 * q + 8, :] * ey[r]
                        out_ref[k, pl.ds(32 * q + r, 8, 4), :] = value
                return carry

            for part in range(2):
                c = 4 * s + 2 * int(lower) + part
                chunk(f_hbm, f_ref, f_sem, c).wait()
                lax.fori_loop(0, KYS, lambda i, v: one(c * KYS + i, v), 0, unroll=4)
                chunk(out_ref, out_hbm, out_sem, c).start()
    for c in range(BLOCKS):
        chunk(out_ref, out_hbm, out_sem, c).wait()


SMEM = pl.BlockSpec(memory_space=pltpu.SMEM)
VMEM = pl.BlockSpec(memory_space=pltpu.VMEM)
HBM = pl.BlockSpec(memory_space=pl.ANY)
F32 = jnp.float32
BIG = pltpu.CompilerParams(vmem_limit_bytes=16 * 1024 * 1024)
DMA = pltpu.SemaphoreType.DMA


def shape(*dims):
    return jax.ShapeDtypeStruct(dims, F32)


def shifted(value, axis, by):
    peers = lax.axis_size(axis)
    return lax.ppermute(value, axis, [(i, (i + by) % peers) for i in range(peers)])


def near(value):
    return pltpu.with_memory_space_constraint(value, pltpu.VMEM)


def moments_call(kz, field):
    return pl.pallas_call(
        moments_kernel,
        in_specs=[SMEM, HBM],
        out_specs=[VMEM] * 5,
        out_shape=[pltpu.VMEM((4, 8, 128), F32)] * 3
        + [pltpu.VMEM((S * VG, 32, 128), F32)] * 2,
        scratch_shapes=[
            pltpu.VMEM((S * VG, 128, 128), F32),
            pltpu.VMEM((S, 20, 8, 128), F32),
            DMA((BLOCKS,)),
        ],
        compiler_params=BIG,
    )(kz, field)


def wall_call(*args):
    return pl.pallas_call(
        wall_kernel,
        in_specs=[SMEM] * 4 + [VMEM] * 4,
        out_specs=[VMEM] * 4,
        out_shape=[
            pltpu.VMEM((9, 16, 128), F32),
            pltpu.VMEM((S, 8, 128), F32),
            pltpu.VMEM((S, CX, VG, 128), F32),
            pltpu.VMEM((S, CX, VG // 2, 128), F32),
        ],
    )(*args)


def step_call(*args):
    return pl.pallas_call(
        step_kernel,
        in_specs=[SMEM] + [VMEM] * 8 + [HBM],
        out_specs=[VMEM, HBM],
        out_shape=[shape(NSURF, 128), shape(S * VG, 128, 128)],
        scratch_shapes=[
            pltpu.VMEM((S * VG, 128, 128), F32),
            pltpu.VMEM((S * VG, 128, 128), F32),
            pltpu.VMEM((S, 4, VG, 128), F32),
            pltpu.VMEM((S, 4, VG, 128), F32),
            pltpu.VMEM((S, CX, VG // 2, 128), F32),
            DMA((BLOCKS,)),
            DMA((BLOCKS,)),
        ],
        compiler_params=BIG,
    )(*args)


def per_device(
    distribution, wall_temp, coverage, face_cell, face_owner, stoichiometry, sticking, surface_rates
):
    kz = lax.axis_index(("z", "x")).astype(jnp.int32).reshape(1)
    field = (
        distribution.reshape(S, VG * VG, CX, 2, 128)
        .transpose(0, 1, 3, 2, 4)
        .reshape(S * VG, 128, 128)
    )
    field = pltpu.with_memory_space_constraint(field, pltpu.HBM)
    own, to_right, to_left, rise, fall = moments_call(kz, field)
    own = own + shifted(to_right, "space", 1) + shifted(to_left, "space", -1)
    own, rise, fall = lax.optimization_barrier((own, rise, fall))
    from_left = shifted(rise, "space", 1)
    from_right = shifted(fall, "space", -1)
    own = own + shifted(own, "x", 1) + shifted(own, "x", 3) + shifted(own, "x", 2)
    copies = jnp.broadcast_to(own[None], (N_Z,) + own.shape)
    parts = lax.all_to_all(copies, "z", 0, 0)
    face_row = face_cell.reshape(1, 128)
    surface, sums, wall_x, wall_y = wall_call(
        kz, stoichiometry, sticking, surface_rates,
        wall_temp.reshape(1, 128), coverage, face_row, face_owner.reshape(1, 128),
    )
    covers, advanced = step_call(
        kz, near(parts), near(surface), near(sums), face_row, near(wall_x), near(wall_y),
        near(from_left), near(from_right), field,
    )
    advanced = (
        advanced.reshape(S, VG * VG, 2, CX, 128)
        .transpose(0, 1, 3, 2, 4)
        .reshape(distribution.shape)
    )
    return advanced, covers


def solution(mesh):
    fine = Mesh(mesh.devices.reshape(N_Z, N_X, mesh.shape["space"]), ("z", "x", "space"))
    return jax.shard_map(
        per_device,
        mesh=fine,
        in_specs=(
            P(None, ("z", "x"), "space", None),
            P("space"),
            P(None, "space"),
            P("space", None),
            P("space"),
            P(),
            P(),
            P(),
        ),
        out_specs=(P(None, ("z", "x"), "space", None), P(None, "space")),
        check_vma=False,
    )
```

time: 85.8 us -> 48.6 us (0.57); the launches traced: 84.3 us -> 48.3 us
  Pallas kernels: 41.9 us -> 15.7 us
  waiting for transfers between devices: 23.9 us -> 11 us
  starting transfers between devices: 14.7 us -> 19.5 us
  local copies, waits for them, and re-layouts: 3.23 us -> 1.35 us
    pallas_call x6 -> x3, Pallas kernels: 41.9 us -> 15.7 us  [the longest x1 9.19 us: step_call(): pl.pallas_call(step_kernel, in_specs=[SMEM] + [VMEM] * 8 + [HBM], out_spe...]
    all_to_all x1, waiting for transfers between devices: 14.7 us -> 5.53 us  [per_device(): parts = lax.all_to_all(copies, 'z', 0, 0)]
    ppermute x4 -> x7, starting transfers between devices: 3.47 us -> 11 us  [shifted(): lax.ppermute(value, axis, [(i, (i + by) % peers) for i in range(peers)])]
    ppermute x4 -> x7, waiting for transfers between devices: 9.2 us -> 5.51 us  [shifted(): lax.ppermute(value, axis, [(i, (i + by) % peers) for i in range(peers)])]
    all_to_all x1, starting transfers between devices: 11.2 us -> 8.57 us  [per_device(): parts = lax.all_to_all(copies, 'z', 0, 0)]
    unnamed x11 -> x5, local copies, waits for them, and re-layouts: 3.23 us -> 0.7 us
  transfers between devices with their start and end apart: 5 -> 8, of which waited for: 3 -> 5; matrix products, arithmetic and copies ran while one was open for 1% -> 3% of each run, Pallas kernels for 18% -> 3%
where the time goes in v2:
time: 48.6 us; the launch traced here: 48.3 us
  starting transfers between devices  19.5 us (40%)
  Pallas kernels  15.7 us (32%)
  waiting for transfers between devices  11 us (23%)
  local copies, waits for them, and re-layouts  1.35 us (3%)
  between operations  0.68 us (1%)
    ppermute x7, starting transfers between devices, shifted(): lax.ppermute(value, axis, [(i, (i + by) % peers) for i in range(peers)])  11 us
    pallas_call x1, Pallas kernels, step_call(): pl.pallas_call(step_kernel, in_specs=[SMEM] + [VMEM] * 8 + [HBM], out_spe...  9.19 us
    all_to_all x1, starting transfers between devices, per_device(): parts = lax.all_to_all(copies, 'z', 0, 0)  8.57 us
    all_to_all x1, waiting for transfers between devices, per_device(): parts = lax.all_to_all(copies, 'z', 0, 0)  5.53 us
    ppermute x7, waiting for transfers between devices, shifted(): lax.ppermute(value, axis, [(i, (i + by) % peers) for i in range(peers)])  5.51 us
    pallas_call x1, Pallas kernels, moments_call(): pl.pallas_call(moments_kernel, in_specs=[SMEM, HBM], out_specs=[VMEM] * 5...  5.1 us
    pallas_call x1, Pallas kernels, wall_call(): pl.pallas_call(wall_kernel, in_specs=[SMEM] * 4 + [VMEM] * 4, out_specs=[...  1.4 us
  transfers between devices with their start and end apart: 8, of which 5 were waited for; matrix products, arithmetic and copies ran while one was open for 3% of the time, Pallas kernels for 3%

profile of v2, /device:TPU:32, one launch (start us, length us, event | category | flops | bytes accessed | tf_op | source)
XLA Modules:
  0.0 48.3 jit_solution(2144589353549167202)
XLA Ops:
  0.6 0.0 copy-start.1
  0.6 0.0 copy-start
  0.7 5.1 %shard_map.95 = (f32[4,8,128]{2,1,0:T(8,128)S(1)}, f32[4,8,128]{2,1,0:T(8,128)S(1)}, f32[4,8,128]{2,1,0:T(8,128)S(1)}, f32[96,32,128]{2,1,0:T(8,128)}, f32[96,32,128]{2,1,0:T(8,128)}) custom-call(s32[1]{0:T(128)} %bitcast.kz_ref, f32[96,128,128]{2,1,0:T(8,128)} %bitcast.13), custom_call_target="tpu_custom_call" | custom-call | tf_op jit(solution)/shard_map/pallas_call | solution.py:477
  5.8 0.0 collective-permute-start
  5.8 2.9 %collective-permute-start.1 = (f32[4,8,128]{2,1,0:T(8,128)S(1)}, f32[4,8,128]{2,1,0:T(8,128)S(1)}, u32[]{:S(2)}, u32[]{:S(2)}) collective-permute-start(f32[4,8,128]{2,1,0:T(8,128)S(1)} %get-tuple-element.18), channel_id=1, source_target_pairs={{0,7},{1,0},{2,1},{3,2},{4,3},{5,4},{6,5},{7,6},{8,15},{9,8},{10,9... | collective-permute-start | bytes 49160 | tf_op jit(solution)/shard_map/ppermute | solution.py:469
  8.7 1.4 %collective-permute-done = f32[4,8,128]{2,1,0:T(8,128)S(1)} collective-permute-done((f32[4,8,128]{2,1,0:T(8,128)S(1)}, f32[4,8,128]{2,1,0:T(8,128)S(1)}, u32[]{:S(2)}, u32[]{:S(2)}) %collective-permute-start) | collective-permute-done | bytes 16416 | tf_op jit(solution)/shard_map/ppermute | solution.py:469
  10.2 0.0 collective-permute-done.1
  10.2 0.5 collective-permute-start.5
  10.6 2.5 %collective-permute-start.6 = (f32[96,32,128]{2,1,0:T(8,128)}, f32[96,32,128]{2,1,0:T(8,128)S(1)}, u32[]{:S(2)}, u32[]{:S(2)}) collective-permute-start(f32[96,32,128]{2,1,0:T(8,128)} %get-tuple-element.27), channel_id=1, source_target_pairs={{0,7},{1,0},{2,1},{3,2},{4,3},{5,4},{6,5},{7,6},{8,15},{9,8},{10,9... | collective-permute-start | bytes 4718600 | tf_op jit(solution)/shard_map/ppermute | solution.py:469
  13.1 3.0 %collective-permute-start.4 = (f32[4,8,128]{2,1,0:T(8,128)S(1)}, f32[4,8,128]{2,1,0:T(8,128)S(1)}, u32[]{:S(2)}, u32[]{:S(2)}) collective-permute-start(f32[4,8,128]{2,1,0:T(8,128)S(1)} %add_add_fusion.1), channel_id=1, source_target_pairs={{0,16},{8,24},{16,0},{24,8},{1,17},{9,25},{17,1},{25,9},{2,18},{10... | collective-permute-start | bytes 49160 | tf_op jit(solution)/shard_map/ppermute | solution.py:469
  16.2 1.1 %collective-permute-start.3 = (f32[4,8,128]{2,1,0:T(8,128)S(1)}, f32[4,8,128]{2,1,0:T(8,128)S(1)}, u32[]{:S(2)}, u32[]{:S(2)}) collective-permute-start(f32[4,8,128]{2,1,0:T(8,128)S(1)} %add_add_fusion.1), channel_id=1, source_target_pairs={{0,24},{8,0},{16,8},{24,16},{1,25},{9,1},{17,9},{25,17},{2,26},{10... | collective-permute-start | bytes 49160 | tf_op jit(solution)/shard_map/ppermute | solution.py:469
  17.3 0.9 %collective-permute-start.2 = (f32[4,8,128]{2,1,0:T(8,128)S(1)}, f32[4,8,128]{2,1,0:T(8,128)S(1)}, u32[]{:S(2)}, u32[]{:S(2)}) collective-permute-start(f32[4,8,128]{2,1,0:T(8,128)S(1)} %add_add_fusion.1), channel_id=1, source_target_pairs={{0,8},{8,16},{16,24},{24,0},{1,9},{9,17},{17,25},{25,1},{2,10},{10... | collective-permute-start | bytes 49160 | tf_op jit(solution)/shard_map/ppermute | solution.py:469
  18.2 0.2 collective-permute-done.4
  18.4 1.5 %collective-permute-done.3 = f32[4,8,128]{2,1,0:T(8,128)S(1)} collective-permute-done((f32[4,8,128]{2,1,0:T(8,128)S(1)}, f32[4,8,128]{2,1,0:T(8,128)S(1)}, u32[]{:S(2)}, u32[]{:S(2)}) %collective-permute-start.3) | collective-permute-done | bytes 16416 | tf_op jit(solution)/shard_map/ppermute | solution.py:469
  19.9 2.4 %collective-permute-done.2 = f32[4,8,128]{2,1,0:T(8,128)S(1)} collective-permute-done((f32[4,8,128]{2,1,0:T(8,128)S(1)}, f32[4,8,128]{2,1,0:T(8,128)S(1)}, u32[]{:S(2)}, u32[]{:S(2)}) %collective-permute-start.2) | collective-permute-done | bytes 16416 | tf_op jit(solution)/shard_map/ppermute | solution.py:469
  22.3 0.7 %broadcast_in_dim.2 = f32[8,4,8,128]{3,2,1,0:T(8,128)} broadcast(f32[4,8,128]{2,1,0:T(8,128)S(1)} %add_add_fusion), dimensions={1,2,3} | broadcast | bytes 147456 | tf_op jit(solution)/shard_map/broadcast_in_dim | solution.py:541
  22.9 8.6 %all-to-all-start = ((f32[8,4,8,128]{3,2,1,0:T(8,128)}), f32[8,4,8,128]{3,2,1,0:T(8,128)S(1)}, u32[]{:S(2)}, u32[]{:S(2)}) async-start(f32[8,4,8,128]{3,2,1,0:T(8,128)} %broadcast_in_dim.2), calls=%async_computation | async-start | bytes 262144 | tf_op jit(solution)/shard_map/all_to_all | solution.py:542
  31.5 0.0 copy-done.1
  31.5 0.7 %copy.11.stoich_ref = s32[12,3]{1,0:T(8,128)} copy(s32[12,3]{0,1:T(4,128)S(1)} %copy-done.1) | data formatting | bytes 288 | tf_op args[5]
  32.2 1.4 %shard_map.96 = (f32[9,16,128]{2,1,0:T(8,128)S(1)}, f32[3,8,128]{2,1,0:T(8,128)S(1)}, f32[3,2,32,128]{3,2,1,0:T(8,128)S(1)}, f32[3,2,16,128]{3,2,1,0:T(8,128)S(1)}) custom-call(s32[1]{0:T(128)} %bitcast.kz_ref, s32[12,3]{1,0:T(8,128)} %copy.11.stoich_ref, f32[4,3]{1,0:T(4,128)} %stick_ref.1, f32[4,2,12]{2,1,0:T(2,128)} %rates_ref.1, f32[1,128]{1,0:T(1,128)} %bitcast.15, ...), custom_call_target="tpu_custom_call" | custom-call | tf_op jit(solution)/shard_map/pallas_call | solution.py:493
  33.6 5.5 %all-to-all-done.parts_ref = f32[8,4,8,128]{3,2,1,0:T(8,128)S(1)} async-done(((f32[8,4,8,128]{3,2,1,0:T(8,128)}), f32[8,4,8,128]{3,2,1,0:T(8,128)S(1)}, u32[]{:S(2)}, u32[]{:S(2)}) %all-to-all-start) | async-done | bytes 131104 | tf_op jit(solution)/shard_map/all_to_all | solution.py:542
  39.1 0.0 collective-permute-done.5.left_ref
  39.1 0.0 collective-permute-done.6.right_ref
  39.1 0.0 copy-done
  39.1 9.2 %shard_map.97 = (f32[12,128]{1,0:T(8,128)}, f32[96,128,128]{2,1,0:T(8,128)}) custom-call(s32[1]{0:T(128)} %bitcast.kz_ref, f32[8,4,8,128]{3,2,1,0:T(8,128)S(1)} %all-to-all-done.parts_ref, f32[9,16,128]{2,1,0:T(8,128)S(1)} %get-tuple-element.22.surface_ref, f32[3,8,128]{2,1,0:T(8,128)S(1)} %get-tuple-element.23.sums_ref, s32[1,128]{1,0:T(1,128)S(1)} %copy-done, ...), custom_call_target="tpu_custom_call" | custom-call | tf_op jit(solution)/shard_map/pallas_call | solution.py:507
  (2 shorter events, 0.0 us)
Async XLA Ops:
  0.6 30.9 %copy-start.1 = (s32[12,3]{0,1:T(4,128)S(1)}, s32[12,3]{0,1:T(4,128)}, u32[]{:S(2)}) copy-start(s32[12,3]{0,1:T(4,128)} %param.13) | copy-start | bytes 436
  0.6 38.5 %copy-start = (s32[1,128]{1,0:T(1,128)S(1)}, s32[1,128]{1,0:T(1,128)}, u32[]{:S(2)}) copy-start(s32[1,128]{1,0:T(1,128)} %cell_ref.3) | copy-start | bytes 1540
  5.8 4.4 %collective-permute-start = (f32[4,8,128]{2,1,0:T(8,128)S(1)}, f32[4,8,128]{2,1,0:T(8,128)S(1)}, u32[]{:S(2)}, u32[]{:S(2)}) collective-permute-start(f32[4,8,128]{2,1,0:T(8,128)S(1)} %get-tuple-element.17), channel_id=1, source_target_pairs={{0,1},{1,2},{2,3},{3,4},{4,5},{5,6},{6,7},{7,0},{8,9},{9,10},{10,1... | collective-permute-start | bytes 49160 | tf_op jit(solution)/shard_map/ppermute | solution.py:469
  5.8 4.4 %collective-permute-start.1 = (f32[4,8,128]{2,1,0:T(8,128)S(1)}, f32[4,8,128]{2,1,0:T(8,128)S(1)}, u32[]{:S(2)}, u32[]{:S(2)}) collective-permute-start(f32[4,8,128]{2,1,0:T(8,128)S(1)} %get-tuple-element.18), channel_id=1, source_target_pairs={{0,7},{1,0},{2,1},{3,2},{4,3},{5,4},{6,5},{7,6},{8,15},{9,8},{10,9... | collective-permute-start | bytes 49160 | tf_op jit(solution)/shard_map/ppermute | solution.py:469
  10.2 28.9 %collective-permute-start.5 = (f32[96,32,128]{2,1,0:T(8,128)}, f32[96,32,128]{2,1,0:T(8,128)S(1)}, u32[]{:S(2)}, u32[]{:S(2)}) collective-permute-start(f32[96,32,128]{2,1,0:T(8,128)} %get-tuple-element.26), channel_id=1, source_target_pairs={{0,1},{1,2},{2,3},{3,4},{4,5},{5,6},{6,7},{7,0},{8,9},{9,10},{10,1... | collective-permute-start | bytes 4718600 | tf_op jit(solution)/shard_map/ppermute | solution.py:469
  10.6 28.5 %collective-permute-start.6 = (f32[96,32,128]{2,1,0:T(8,128)}, f32[96,32,128]{2,1,0:T(8,128)S(1)}, u32[]{:S(2)}, u32[]{:S(2)}) collective-permute-start(f32[96,32,128]{2,1,0:T(8,128)} %get-tuple-element.27), channel_id=1, source_target_pairs={{0,7},{1,0},{2,1},{3,2},{4,3},{5,4},{6,5},{7,6},{8,15},{9,8},{10,9... | collective-permute-start | bytes 4718600 | tf_op jit(solution)/shard_map/ppermute | solution.py:469
  13.1 5.2 %collective-permute-start.4 = (f32[4,8,128]{2,1,0:T(8,128)S(1)}, f32[4,8,128]{2,1,0:T(8,128)S(1)}, u32[]{:S(2)}, u32[]{:S(2)}) collective-permute-start(f32[4,8,128]{2,1,0:T(8,128)S(1)} %add_add_fusion.1), channel_id=1, source_target_pairs={{0,16},{8,24},{16,0},{24,8},{1,17},{9,25},{17,1},{25,9},{2,18},{10... | collective-permute-start | bytes 49160 | tf_op jit(solution)/shard_map/ppermute | solution.py:469
  16.2 3.7 %collective-permute-start.3 = (f32[4,8,128]{2,1,0:T(8,128)S(1)}, f32[4,8,128]{2,1,0:T(8,128)S(1)}, u32[]{:S(2)}, u32[]{:S(2)}) collective-permute-start(f32[4,8,128]{2,1,0:T(8,128)S(1)} %add_add_fusion.1), channel_id=1, source_target_pairs={{0,24},{8,0},{16,8},{24,16},{1,25},{9,1},{17,9},{25,17},{2,26},{10... | collective-permute-start | bytes 49160 | tf_op jit(solution)/shard_map/ppermute | solution.py:469
  17.3 4.9 %collective-permute-start.2 = (f32[4,8,128]{2,1,0:T(8,128)S(1)}, f32[4,8,128]{2,1,0:T(8,128)S(1)}, u32[]{:S(2)}, u32[]{:S(2)}) collective-permute-start(f32[4,8,128]{2,1,0:T(8,128)S(1)} %add_add_fusion.1), channel_id=1, source_target_pairs={{0,8},{8,16},{16,24},{24,0},{1,9},{9,17},{17,25},{25,1},{2,10},{10... | collective-permute-start | bytes 49160 | tf_op jit(solution)/shard_map/ppermute | solution.py:469
  22.9 16.2 %all-to-all-start = ((f32[8,4,8,128]{3,2,1,0:T(8,128)}), f32[8,4,8,128]{3,2,1,0:T(8,128)S(1)}, u32[]{:S(2)}, u32[]{:S(2)}) async-start(f32[8,4,8,128]{3,2,1,0:T(8,128)} %broadcast_in_dim.2), calls=%async_computation | async-start | bytes 262144 | tf_op jit(solution)/shard_map/all_to_all | solution.py:542

commit v3 on v2

--- a/solution.py
+++ b/solution.py
@@ -1,3 +1,5 @@
+import functools
+
 import jax
 import jax.numpy as jnp
 from jax import lax
@@ -30,6 +32,7 @@
 HALF = PAIRS // 2
 BLOCKS = 12
 KYS = S * VG // BLOCKS
+GROUP = KYS // 2
 TILE = (8, 128)
 PRECISE = lax.Precision.HIGHEST
 
@@ -64,8 +67,13 @@
     return pltpu.make_async_copy(src.at[part], dst.at[part], sems.at[c])
 
 
+def half_chunk(src, dst, sems, c):
+    part = pl.ds(c * GROUP, GROUP)
+    return pltpu.make_async_copy(src.at[part], dst.at[part], sems.at[c])
+
+
 def moments_kernel(
-    kz_ref, f_hbm, own_ref, to_right_ref, to_left_ref, rise_ref, fall_ref, f_ref, acc_ref, f_sem,
+    kz_ref, f_hbm, own_ref, to_right_ref, to_left_ref, f_ref, rise_ref, fall_ref, acc_ref, f_sem,
 ):
     for c in range(BLOCKS):
         chunk(f_hbm, f_ref, f_sem, c).start()
@@ -235,7 +243,7 @@
     stick = [by_owner(lambda p: stick_ref[p, s]) for s in range(S)]
     surface_ref[1] = jnp.concatenate(desorb + [zero] * 4, axis=0)
     surface_ref[2] = jnp.concatenate(lateral + [zero] * 4, axis=0)
-    counts = [[stoich_ref[j, s].astype(jnp.float32) for s in range(S)] for j in range(NSURF)]
+    counts = [[stoich_ref[s, j].astype(jnp.float32) for s in range(S)] for j in range(NSURF)]
     for s in range(S):
         column_sum = counts[0][s]
         for j in range(1, NSURF):
@@ -258,6 +266,7 @@
     cz = speed_of(kz_ref[0])
     cy = c[VG // 2 :]
     temps = [temp, pltpu.roll(temp, 64, 1)]
+    low = lax.broadcasted_iota(jnp.int32, (VG, 128), 1) < 64
     for s in range(S):
         m = SPECIES_MASS[s]
         e = jnp.exp(-m * (c * c) / (2.0 * temp))
@@ -288,55 +297,126 @@
         )
         for x in range(CX):
             rate = -m / (2.0 * temps[x])
-            wall_x_ref[s, x] = jnp.exp(rate * (c * c))
-            wall_y_ref[s, x] = (TIME_STEP * cy) * jnp.exp(rate * (cy * cy)) * jnp.exp(rate * (cz * cz))
+            wall_x_ref[s, x] = jnp.where(low, jnp.exp(rate * (c * c)), 0.0)
+            wall_y_ref[s, x] = (cy / jnp.abs(cz)) * jnp.exp(rate * (cy * cy)) * jnp.exp(rate * (cz * cz))
+
+
+def shift_kernel(s, kz_ref, f_ref, t_ref, z0_ref, z1_ref):
+    low = lanes() < 64
+    cz = speed_of(kz_ref[0])
+    acz = jnp.abs(cz)
+    coef_z = TIME_STEP * acz
+    octet = speed_of(lax.broadcasted_iota(jnp.int32, TILE, 0))
+    coef_x = [jnp.abs(octet + 8.0 * SPACING * q) / acz for q in range(4)]
+    source = lax.broadcasted_iota(jnp.int32, (256, 128), 0) % 128
+    target = lax.broadcasted_iota(jnp.int32, (256, 128), 1)
+    wanted = target // 64 * 64 + (target % 64 + jnp.where(cz > 0.0, 63, 1)) % 64
+    turn = (source == wanted).astype(jnp.float32).astype(jnp.bfloat16)
+
+    def along_z(first, to):
+        value = f_ref[pl.ds(first, GROUP)].reshape(GROUP * 128, 128)
+        high = value.astype(jnp.bfloat16)
+        rest = (value - high.astype(jnp.float32)).astype(jnp.bfloat16)
+        to[...] = jnp.dot(
+            jnp.concatenate([high, rest], axis=1), turn, preferred_element_type=jnp.float32
+        )
+
+    def advance(first, lower, z_ref):
+        for i in range(GROUP):
+            k = first + i
+            coef_y = jnp.abs(speed_of(k % VG)) / acz
+            own = (1.0 / coef_z - 1.0) - coef_y
+            for q in range(4):
+                f = [f_ref[k, pl.ds(32 * q + r, 8, 4), :] for r in range(4)]
+                far = [along(v, 64) for v in f]
+                coef_own = own - coef_x[q]
+                for r in range(4):
+                    h, x = r // 2, r % 2
+                    value = coef_own * f[r] + z_ref[pl.ds(128 * i + 32 * q + r, 8, 4), :]
+                    if q < 2 and x == 0:
+                        value = value + coef_x[q] * f[r + 1]
+                    if q >= 2 and x == 1:
+                        value = value + coef_x[q] * f[r - 1]
+                    if lower and h == 0:
+                        value = value + jnp.where(low, 0.0, coef_y * far[r])
+                    elif lower or h == 0:
+                        value = value + coef_y * jnp.where(low, far[x], far[x + 2])
+                    else:
+                        value = value + coef_y * jnp.where(low, far[r], f[r])
+                    t_ref[k - s * VG, 32 * r + 8 * q : 32 * r + 8 * q + 8, :] = value
+
+    def one_chunk(c, lower):
+        first = s * VG + c * KYS
+        after = s * VG + jnp.minimum(c + 1, 3) * KYS
+        along_z(first + GROUP, z1_ref)
+        advance(first, lower, z0_ref)
+        along_z(after, z0_ref)
+        advance(first + GROUP, lower, z1_ref)
+
+    along_z(s * VG, z0_ref)
+    for lower in (False, True):
+
+        def part(p, carry, lower=lower):
+            one_chunk(2 * int(lower) + p, lower)
+            return carry
+
+        lax.fori_loop(0, 2, part, 0)
 
 
 def step_kernel(
-    kz_ref, parts_ref, surface_ref, sums_ref, cell_ref, wall_x_ref, wall_y_ref,
-    left_ref, right_ref, f_hbm,
+    kz_ref, part0_ref, part1_ref, part2_ref, part3_ref, surface_ref, sums_ref, cell_ref,
+    wall_x_ref, wall_y_ref, left_ref, right_ref, t0_ref, t1_ref, t2_ref,
     cover_ref, out_hbm,
-    f_ref, out_ref, ex_ref, ey_ref, wy_ref, f_sem, out_sem,
+    out_ref, ex_ref, ey_ref, wy_ref, keep_ref, out_sem,
 ):
-    for c in range(BLOCKS):
-        chunk(f_hbm, f_ref, f_sem, c).start()
     row = rows()
     totals = []
     for t in range(4):
-        v = parts_ref[0, t]
-        for peer in range(1, N_Z):
-            v = v + parts_ref[peer, t]
-        totals.append(v)
+        totals.append((part0_ref[t] + part1_ref[t]) + (part2_ref[t] + part3_ref[t]))
     incident = [totals[3][4 + s : 5 + s] for s in range(S)]
-    start = surface_ref[0]
-    desorb = surface_ref[1]
-    lateral = surface_ref[2]
-    feed = (
-        surface_ref[3] * incident[0]
-        + surface_ref[4] * incident[1]
-        + surface_ref[5] * incident[2]
-    )
-    covers = start
+    start = [surface_ref[0, j : j + 1, :] for j in range(NSURF)]
+    desorb = [surface_ref[1, j : j + 1, :] for j in range(NSURF)]
+    lateral = [surface_ref[2, j : j + 1, :] for j in range(NSURF)]
+    feed = [
+        surface_ref[3, j : j + 1, :] * incident[0]
+        + surface_ref[4, j : j + 1, :] * incident[1]
+        + surface_ref[5, j : j + 1, :] * incident[2]
+        for j in range(NSURF)
+    ]
+
+    def tree(values):
+        values = list(values)
+        while len(values) > 1:
+            values = [
+                values[i] + values[i + 1] if i + 1 < len(values) else values[i]
+                for i in range(0, len(values), 2)
+            ]
+        return values[0]
 
     def total(v):
         return jnp.sum(v, axis=0, keepdims=True)
 
+    covers = start
     for _ in range(NEWTON):
-        vacant = 1.0 - total(covers)
-        squared = covers * covers
-        net = feed * vacant - desorb * covers - lateral * (squared * covers)
-        residual = covers - start - SURFACE_STEP * net
-        inverse = 1.0 / (1.0 + SURFACE_STEP * (desorb + 3.0 * lateral * squared))
-        scaled = residual * inverse
-        coupling = SURFACE_STEP * feed * inverse
-        update = scaled - coupling * (total(scaled) / (1.0 + total(coupling)))
-        covers = covers - DAMPING * update
-    released = desorb * covers + lateral * (covers * covers * covers)
-    vacant = 1.0 - total(covers)
-    cover_face = jnp.dot(
-        covers, selector(cell_ref[...]), precision=PRECISE, preferred_element_type=jnp.float32
-    )
-    cover_ref[...] = cover_face[0:NSURF]
+        vacant = 1.0 - tree(covers)
+        scaled, coupling = [], []
+        for j in range(NSURF):
+            th = covers[j]
+            squared = lateral[j] * (th * th)
+            net = feed[j] * vacant - desorb[j] * th - squared * th
+            residual = th - start[j] - SURFACE_STEP * net
+            inverse = 1.0 / (1.0 + SURFACE_STEP * (desorb[j] + 3.0 * squared))
+            scaled.append(residual * inverse)
+            coupling.append((SURFACE_STEP * feed[j]) * inverse)
+        ratio = tree(scaled) / (1.0 + tree(coupling))
+        covers = [
+            th - DAMPING * (y - u * ratio) for th, y, u in zip(covers, scaled, coupling)
+        ]
+    released = [
+        desorb[j] * covers[j] + lateral[j] * (covers[j] * covers[j] * covers[j])
+        for j in range(NSURF)
+    ]
+    vacant = 1.0 - tree(covers)
 
     def quantity(q):
         v = totals[q // 2]
@@ -347,31 +427,36 @@
     mom = [quantity(3 + a) for a in range(3)]
     energy = quantity(6)
     wall_dens = []
+    wall_mom = [0.0, 0.0, 0.0]
+    wall_energy = 0.0
     for s in range(S):
         m = SPECIES_MASS[s]
-        emitted = incident[s] * (1.0 - sums_ref[s, 6:7] * vacant) + total(
-            surface_ref[6 + s] * released
+        emitted = incident[s] * (1.0 - sums_ref[s, 6:7] * vacant) + tree(
+            [surface_ref[6 + s, j : j + 1, :] * released[j] for j in range(NSURF)]
         )
         wd = emitted * sums_ref[s, 0:1]
         wall_dens.append(wd)
         dens[s] = dens[s] + to_tile(wd * sums_ref[s, 1:2])
         for a in range(3):
-            mom[a] = mom[a] + to_tile((m * wd) * sums_ref[s, 2 + a : 3 + a])
-        energy = energy + to_tile((m * wd) * sums_ref[s, 5:6])
+            wall_mom[a] = wall_mom[a] + (m * wd) * sums_ref[s, 2 + a : 3 + a]
+        wall_energy = wall_energy + (m * wd) * sums_ref[s, 5:6]
+    mom = [mom[a] + to_tile(wall_mom[a]) for a in range(3)]
+    energy = energy + to_tile(wall_energy)
     gas = dens[0] + dens[1] + dens[2]
     mass = SPECIES_MASS[0] * dens[0] + SPECIES_MASS[1] * dens[1] + SPECIES_MASS[2] * dens[2]
     bulk = [v / mass for v in mom]
     flow = bulk[0] * bulk[0] + bulk[1] * bulk[1] + bulk[2] * bulk[2]
     temperature = (energy - mass * flow) / (3.0 * gas)
     cz = speed_of(kz_ref[0])
+    acz = jnp.abs(cz)
+    coef_z = TIME_STEP * acz
     grid = speed_of(lax.broadcasted_iota(jnp.int32, (VG, 128), 0))
-    keeps = []
     for s in range(S):
         rate = -SPECIES_MASS[s] / (2.0 * temperature)
         keep = jnp.exp((-TIME_STEP * COLLISION_RATE[s]) * gas)
         off = cz - bulk[2]
         scale = (1.0 - keep) * dens[s] * jnp.exp(rate * (off * off))
-        keeps.append(keep)
+        keep_ref[s] = coef_z * keep
         for r in range(4):
             at = slice(r, r + 1)
 
@@ -388,68 +473,50 @@
         wy_ref[s, 0] = wall_y_ref[s, 0] * wall_dens[s]
         wy_ref[s, 1] = wall_y_ref[s, 1] * other
 
-    lane = lanes()
-    low = lane < 64
-    acz = jnp.abs(cz)
-    rise_z = cz > 0.0
-    shift_z = jnp.where(rise_z, 1, 127)
-    edge = (lane % 64) == jnp.where(rise_z, 63, 0)
-    coef_z = TIME_STEP * acz
     octet = speed_of(lax.broadcasted_iota(jnp.int32, TILE, 0))
-    coef_x = [TIME_STEP * jnp.abs(octet + 8.0 * SPACING * q) for q in range(4)]
+    coef_x = [jnp.abs(octet + 8.0 * SPACING * q) / acz for q in range(4)]
+
+    def advance(first, s, lower):
+        t_ref = (t0_ref, t1_ref, t2_ref)[s]
+        keep = [jnp.broadcast_to(keep_ref[s, r : r + 1, :], TILE) for r in range(4)]
+        for i in range(GROUP):
+            k = first + i
+            ky = k - s * VG
+            ey = [jnp.broadcast_to(ey_ref[s, r, pl.ds(ky, 1), :], TILE) for r in range(4)]
+            if lower:
+                wy = [
+                    jnp.broadcast_to(wy_ref[s, x, pl.ds(ky - PAIRS, 1), :], TILE)
+                    for x in range(CX)
+                ]
+            for q in range(4):
+                for r in range(4):
+                    h, x = r // 2, r % 2
+                    value = t_ref[ky, 32 * r + 8 * q : 32 * r + 8 * q + 8, :]
+                    if q < 2 and x == 1:
+                        value = value + coef_x[q] * right_ref[k, pl.ds(16 * h + 8 * q, 8), :]
+                    if q >= 2 and x == 0:
+                        value = value + coef_x[q] * left_ref[k, pl.ds(16 * h + 8 * (q - 2), 8), :]
+                    if lower and h == 0:
+                        value = value + wall_x_ref[s, x, 8 * q : 8 * q + 8, :] * wy[x]
+                    value = keep[r] * value + ex_ref[s, r, 8 * q : 8 * q + 8, :] * ey[r]
+                    out_ref[k, pl.ds(32 * q + r, 8, 4), :] = value
 
     for s in range(S):
-        keep = [jnp.broadcast_to(keeps[s][r : r + 1], TILE) for r in range(4)]
         for lower in (False, True):
 
-            def one(k, carry, s=s, lower=lower, keep=keep):
-                ky = k - s * VG
-                acy = jnp.abs(speed_of(ky))
-                coef_y = TIME_STEP * acy
-                coef_own = 1.0 - coef_z - coef_y
-                ey = [
-                    jnp.broadcast_to(ey_ref[s, r, pl.ds(ky, 1), :], TILE) for r in range(4)
-                ]
-                if lower:
-                    wy = [
-                        jnp.broadcast_to(wy_ref[s, x, pl.ds(ky - PAIRS, 1), :], TILE)
-                        for x in range(CX)
-                    ]
-                for q in range(4):
-                    f = [f_ref[k, pl.ds(32 * q + r, 8, 4), :] for r in range(4)]
-                    far = [along(v, 64) for v in f]
-                    for r in range(4):
-                        h, x = r // 2, r % 2
-                        if q < 2:
-                            near = f[r + 1] if x == 0 else right_ref[k, pl.ds(16 * h + 8 * q, 8), :]
-                        else:
-                            near = (
-                                f[r - 1] if x == 1
-                                else left_ref[k, pl.ds(16 * h + 8 * (q - 2), 8), :]
-                            )
-                        value = (
-                            coef_own * f[r]
-                            + coef_x[q] * (near - f[r])
-                            + coef_z * pltpu.roll(jnp.where(edge, far[r], f[r]), shift_z, 1)
-                        )
-                        if lower and h == 0:
-                            wall = wall_x_ref[s, x, 8 * q : 8 * q + 8, :] * wy[x]
-                            value = value + jnp.where(low, wall, coef_y * far[r])
-                        elif lower or h == 0:
-                            value = value + coef_y * jnp.where(low, far[x], far[x + 2])
-                        else:
-                            value = value + coef_y * jnp.where(low, far[r], f[r])
-                        value = keep[r] * value + ex_ref[s, r, 8 * q : 8 * q + 8, :] * ey[r]
-                        out_ref[k, pl.ds(32 * q + r, 8, 4), :] = value
+            def part(p, carry, s=s, lower=lower):
+                g = 8 * s + 4 * int(lower) + p
+                advance(g * GROUP, s, lower)
+                half_chunk(out_ref, out_hbm, out_sem, g).start()
                 return carry
 
-            for part in range(2):
-                c = 4 * s + 2 * int(lower) + part
-                chunk(f_hbm, f_ref, f_sem, c).wait()
-                lax.fori_loop(0, KYS, lambda i, v: one(c * KYS + i, v), 0, unroll=4)
-                chunk(out_ref, out_hbm, out_sem, c).start()
-    for c in range(BLOCKS):
-        chunk(out_ref, out_hbm, out_sem, c).wait()
+            lax.fori_loop(0, 4, part, 0)
+    cover_ref[...] = jnp.dot(
+        jnp.concatenate(covers, axis=0), selector(cell_ref[...]), precision=PRECISE,
+        preferred_element_type=jnp.float32,
+    )
+    for c in range(2 * BLOCKS):
+        half_chunk(out_ref, out_hbm, out_sem, c).wait()
 
 
 SMEM = pl.BlockSpec(memory_space=pltpu.SMEM)
@@ -457,6 +524,7 @@
 HBM = pl.BlockSpec(memory_space=pl.ANY)
 F32 = jnp.float32
 BIG = pltpu.CompilerParams(vmem_limit_bytes=16 * 1024 * 1024)
+SMALL = pltpu.CompilerParams(vmem_limit_bytes=4 * 1024 * 1024)
 DMA = pltpu.SemaphoreType.DMA
 
 
@@ -477,11 +545,11 @@
     return pl.pallas_call(
         moments_kernel,
         in_specs=[SMEM, HBM],
-        out_specs=[VMEM] * 5,
+        out_specs=[VMEM] * 6,
         out_shape=[pltpu.VMEM((4, 8, 128), F32)] * 3
+        + [pltpu.VMEM((S * VG, 128, 128), F32)]
         + [pltpu.VMEM((S * VG, 32, 128), F32)] * 2,
         scratch_shapes=[
-            pltpu.VMEM((S * VG, 128, 128), F32),
             pltpu.VMEM((S, 20, 8, 128), F32),
             DMA((BLOCKS,)),
         ],
@@ -500,26 +568,45 @@
             pltpu.VMEM((S, CX, VG, 128), F32),
             pltpu.VMEM((S, CX, VG // 2, 128), F32),
         ],
+        compiler_params=SMALL,
     )(*args)
+
+
+def shift_call(s, kz, field):
+    return pl.pallas_call(
+        functools.partial(shift_kernel, s),
+        in_specs=[SMEM, VMEM],
+        out_specs=VMEM,
+        out_shape=pltpu.VMEM((VG, 128, 128), F32),
+        scratch_shapes=[
+            pltpu.VMEM((GROUP * 128, 128), F32),
+            pltpu.VMEM((GROUP * 128, 128), F32),
+        ],
+        compiler_params=BIG,
+    )(kz, near(field))
 
 
 def step_call(*args):
     return pl.pallas_call(
         step_kernel,
-        in_specs=[SMEM] + [VMEM] * 8 + [HBM],
+        in_specs=[SMEM] + [VMEM] * 14,
         out_specs=[VMEM, HBM],
         out_shape=[shape(NSURF, 128), shape(S * VG, 128, 128)],
         scratch_shapes=[
             pltpu.VMEM((S * VG, 128, 128), F32),
-            pltpu.VMEM((S * VG, 128, 128), F32),
             pltpu.VMEM((S, 4, VG, 128), F32),
             pltpu.VMEM((S, 4, VG, 128), F32),
             pltpu.VMEM((S, CX, VG // 2, 128), F32),
-            DMA((BLOCKS,)),
-            DMA((BLOCKS,)),
+            pltpu.VMEM((S, 8, 128), F32),
+            DMA((2 * BLOCKS,)),
         ],
         compiler_params=BIG,
     )(*args)
+
+
+def paired(value, axis):
+    peers = lax.axis_size(axis)
+    return lax.ppermute(value, axis, [(i, i ^ 1) for i in range(peers)])
 
 
 def per_device(
@@ -532,22 +619,35 @@
         .reshape(S * VG, 128, 128)
     )
     field = pltpu.with_memory_space_constraint(field, pltpu.HBM)
-    own, to_right, to_left, rise, fall = moments_call(kz, field)
+    own, to_right, to_left, held, rise, fall = moments_call(kz, field)
+    together = lax.optimization_barrier
+    face_row = face_cell.reshape(1, 128)
+
+    temp, own = together((wall_temp.reshape(1, 128), own))
+    walls = wall_call(
+        kz, stoichiometry.T, sticking, surface_rates, temp, coverage, face_row,
+        face_owner.reshape(1, 128),
+    )
     own = own + shifted(to_right, "space", 1) + shifted(to_left, "space", -1)
-    own, rise, fall = lax.optimization_barrier((own, rise, fall))
+    own, rise, fall, held, walls = together((own, rise, fall, held, walls))
+
     from_left = shifted(rise, "space", 1)
     from_right = shifted(fall, "space", -1)
+    moved0 = shift_call(0, kz, held)
     own = own + shifted(own, "x", 1) + shifted(own, "x", 3) + shifted(own, "x", 2)
-    copies = jnp.broadcast_to(own[None], (N_Z,) + own.shape)
-    parts = lax.all_to_all(copies, "z", 0, 0)
-    face_row = face_cell.reshape(1, 128)
-    surface, sums, wall_x, wall_y = wall_call(
-        kz, stoichiometry, sticking, surface_rates,
-        wall_temp.reshape(1, 128), coverage, face_row, face_owner.reshape(1, 128),
-    )
+    own, moved0, held = together((own, moved0, held))
+
+    moved1 = shift_call(1, kz, held)
+    own = own + paired(own, "z")
+    own, moved1, held = together((own, moved1, held))
+
+    moved2 = shift_call(2, kz, held)
+    parts = [own, shifted(own, "z", 2), shifted(own, "z", 6), shifted(own, "z", 4)]
+    surface, sums, wall_x, wall_y = walls
+    vmem = [near(v) for v in parts + [surface, sums]]
     covers, advanced = step_call(
-        kz, near(parts), near(surface), near(sums), face_row, near(wall_x), near(wall_y),
-        near(from_left), near(from_right), field,
+        kz, *vmem, face_row, near(wall_x), near(wall_y), near(from_left), near(from_right),
+        near(moved0), near(moved1), near(moved2),
     )
     advanced = (
         advanced.reshape(S, VG * VG, 2, CX, 128)

time: 48.6 us -> 41.5 us (0.85)
  waiting for transfers between devices: 11 us -> 6.6 us
  Pallas kernels: 15.7 us -> 13.7 us
  local copies, waits for them, and re-layouts: 1.35 us -> 0.03 us
  starting transfers between devices: 19.5 us -> 20.3 us
    ppermute x7 -> x10, starting transfers between devices: 11 us -> 20.2 us  [shifted(): lax.ppermute(value, axis, [(i, (i + by) % peers) for i in range(peers)])]
    all_to_all x1 -> x0, starting transfers between devices: 8.57 us -> none  [per_device(): parts = lax.all_to_all(copies, 'z', 0, 0)]
    all_to_all x1 -> x0, waiting for transfers between devices: 5.53 us -> none  [per_device(): parts = lax.all_to_all(copies, 'z', 0, 0)]
    ppermute x0 -> x1, waiting for transfers between devices: none -> 1.95 us  [paired(): return lax.ppermute(value, axis, [(i, i ^ 1) for i in range(peers)])]
    pallas_call x2 -> x5, Pallas kernels: 14.3 us -> 12.7 us  [the longest x3 5 us: shift_call(): pl.pallas_call(functools.partial(shift_kernel, s), in_specs=[SMEM, VMEM],...]
    ppermute x7 -> x10, waiting for transfers between devices: 5.51 us -> 4.65 us  [shifted(): lax.ppermute(value, axis, [(i, (i + by) % peers) for i in range(peers)])]
    unnamed x5 -> x14, local copies, waits for them, and re-layouts: 0.7 us -> 0.03 us
    broadcast_in_dim x1 -> x0, local copies, waits for them, and re-layouts: 0.66 us -> none  [per_device(): copies = jnp.broadcast_to(own[None], (N_Z,) + own.shape)]
  transfers between devices with their start and end apart: 8 -> 11, of which waited for: 5 -> 4; matrix products, arithmetic and copies ran while one was open for 3% -> 0% of each run, Pallas kernels for 3% -> 15%
where the time goes in v3:
time: 41.5 us; the launch traced here: 41.4 us
  starting transfers between devices  20.3 us (49%)
  Pallas kernels  13.7 us (33%)
  waiting for transfers between devices  6.6 us (16%)
  between operations  0.78 us (2%)
    ppermute x10, starting transfers between devices, shifted(): lax.ppermute(value, axis, [(i, (i + by) % peers) for i in range(peers)])  20.2 us
    pallas_call x3, Pallas kernels, shift_call(): pl.pallas_call(functools.partial(shift_kernel, s), in_specs=[SMEM, VMEM],...  5 us
    ppermute x10, waiting for transfers between devices, shifted(): lax.ppermute(value, axis, [(i, (i + by) % peers) for i in range(peers)])  4.65 us
    pallas_call x1, Pallas kernels, step_call(): pl.pallas_call(step_kernel, in_specs=[SMEM] + [VMEM] * 14, out_specs=[VME...  4.17 us
    pallas_call x1, Pallas kernels, moments_call(): pl.pallas_call(moments_kernel, in_specs=[SMEM, HBM], out_specs=[VMEM] * 6...  3.52 us
    ppermute x1, waiting for transfers between devices, paired(): return lax.ppermute(value, axis, [(i, i ^ 1) for i in range(peers)])  1.95 us
    pallas_call x1, Pallas kernels, wall_call(): pl.pallas_call(wall_kernel, in_specs=[SMEM] * 4 + [VMEM] * 4, out_specs=[...  1.04 us
  transfers between devices with their start and end apart: 11, of which 4 were waited for; matrix products, arithmetic and copies ran while one was open for 0% of the time, Pallas kernels for 15%

profile of v3, /device:TPU:32, one launch (start us, length us, event | category | flops | bytes accessed | tf_op | source)
XLA Modules:
  0.0 41.4 jit_solution(1446281379887416169)
XLA Ops:
  0.6 0.0 copy-start
  0.6 0.0 copy-start.1
  0.7 0.0 copy-start.2
  0.7 0.0 copy-start.3
  0.7 0.0 copy-start.4
  0.7 0.0 copy-start.5
  0.7 0.0 copy-start.6
  0.7 3.5 %shard_map.95 = (f32[4,8,128]{2,1,0:T(8,128)S(1)}, f32[4,8,128]{2,1,0:T(8,128)S(1)}, f32[4,8,128]{2,1,0:T(8,128)S(1)}, f32[96,128,128]{2,1,0:T(8,128)S(1)}, f32[...) custom-call(s32[1]{0:T(128)} %bitcast.kz_ref, f32[96,128,128]{2,1,0:T(8,128)} %bitcast.17), custom_call_target="tpu_custom_call" | custom-call | tf_op jit(solution)/shard_map/pallas_call | solution.py:545
  4.2 0.0 collective-permute-start
  4.3 2.9 %collective-permute-start.1 = (f32[4,8,128]{2,1,0:T(8,128)S(1)}, f32[4,8,128]{2,1,0:T(8,128)S(1)}, u32[]{:S(2)}, u32[]{:S(2)}) collective-permute-start(f32[4,8,128]{2,1,0:T(8,128)S(1)} %get-tuple-element.33), channel_id=1, source_target_pairs={{0,7},{1,0},{2,1},{3,2},{4,3},{5,4},{6,5},{7,6},{8,15},{9,8},{10,9... | collective-permute-start | bytes 49160 | tf_op jit(solution)/shard_map/ppermute | solution.py:537
  7.2 0.0 copy-done
  7.2 0.0 copy-done.1
  7.2 0.0 copy-done.2
  7.2 0.0 copy-done.3
  7.2 0.0 copy-done.4
  7.2 0.0 copy-done.5
  7.2 0.0 copy-done.6
  7.2 1.0 %shard_map.96 = (f32[9,16,128]{2,1,0:T(8,128)S(1)}, f32[3,8,128]{2,1,0:T(8,128)S(1)}, f32[3,2,32,128]{3,2,1,0:T(8,128)S(1)}, f32[3,2,16,128]{3,2,1,0:T(8,128)S(1)}) custom-call(s32[1]{0:T(128)} %bitcast.kz_ref, s32[3,12]{1,0:T(4,128)S(1)} %bitcast.14, f32[4,3]{1,0:T(4,128)S(1)} %copy-done.4, f32[4,2,12]{2,1,0:T(2,128)S(1)} %copy-done.1, ...), custom_call_target="tpu_custom_call" | custom-call | tf_op jit(solution)/shard_map/pallas_call | solution.py:561
  8.3 0.3 collective-permute-done
  8.6 0.0 collective-permute-done.1
  8.7 0.5 %collective-permute-start.9 = (f32[96,32,128]{2,1,0:T(8,128)S(1)}, f32[96,32,128]{2,1,0:T(8,128)S(1)}, u32[]{:S(2)}, u32[]{:S(2)}) collective-permute-start(f32[96,32,128]{2,1,0:T(8,128)S(1)} %get-tuple-element.51), channel_id=1, source_target_pairs={{0,1},{1,2},{2,3},{3,4},{4,5},{5,6},{6,7},{7,0},{8,9},{9,10},{10,1... | collective-permute-start | bytes 4718600 | tf_op jit(solution)/shard_map/ppermute | solution.py:537
  9.1 2.5 %collective-permute-start.10 = (f32[96,32,128]{2,1,0:T(8,128)S(1)}, f32[96,32,128]{2,1,0:T(8,128)S(1)}, u32[]{:S(2)}, u32[]{:S(2)}) collective-permute-start(f32[96,32,128]{2,1,0:T(8,128)S(1)} %get-tuple-element.52), channel_id=1, source_target_pairs={{0,7},{1,0},{2,1},{3,2},{4,3},{5,4},{6,5},{7,6},{8,15},{9,8},{10,9... | collective-permute-start | bytes 4718600 | tf_op jit(solution)/shard_map/ppermute | solution.py:537
  11.6 3.0 %collective-permute-start.4 = (f32[4,8,128]{2,1,0:T(8,128)S(1)}, f32[4,8,128]{2,1,0:T(8,128)S(1)}, u32[]{:S(2)}, u32[]{:S(2)}) collective-permute-start(f32[4,8,128]{2,1,0:T(8,128)S(1)} %add_add_fusion.1), channel_id=1, source_target_pairs={{0,16},{8,24},{16,0},{24,8},{1,17},{9,25},{17,1},{25,9},{2,18},{10... | collective-permute-start | bytes 49160 | tf_op jit(solution)/shard_map/ppermute | solution.py:537
  14.6 1.1 %collective-permute-start.3 = (f32[4,8,128]{2,1,0:T(8,128)S(1)}, f32[4,8,128]{2,1,0:T(8,128)S(1)}, u32[]{:S(2)}, u32[]{:S(2)}) collective-permute-start(f32[4,8,128]{2,1,0:T(8,128)S(1)} %add_add_fusion.1), channel_id=1, source_target_pairs={{0,24},{8,0},{16,8},{24,16},{1,25},{9,1},{17,9},{25,17},{2,26},{10... | collective-permute-start | bytes 49160 | tf_op jit(solution)/shard_map/ppermute | solution.py:537
  15.8 0.9 %collective-permute-start.2 = (f32[4,8,128]{2,1,0:T(8,128)S(1)}, f32[4,8,128]{2,1,0:T(8,128)S(1)}, u32[]{:S(2)}, u32[]{:S(2)}) collective-permute-start(f32[4,8,128]{2,1,0:T(8,128)S(1)} %add_add_fusion.1), channel_id=1, source_target_pairs={{0,8},{8,16},{16,24},{24,0},{1,9},{9,17},{17,25},{25,1},{2,10},{10... | collective-permute-start | bytes 49160 | tf_op jit(solution)/shard_map/ppermute | solution.py:537
  16.7 1.7 %shard_map.97.t0_ref = f32[32,128,128]{2,1,0:T(8,128)S(1)} custom-call(s32[1]{0:T(128)} %bitcast.kz_ref, f32[96,128,128]{2,1,0:T(8,128)S(1)} %get-tuple-element.55.f_ref), custom_call_target="tpu_custom_call" | custom-call | tf_op jit(solution)/shard_map/pallas_call | solution.py:576
  18.3 0.0 collective-permute-done.4
  18.3 0.0 collective-permute-done.3
  18.4 2.4 %collective-permute-done.2 = f32[4,8,128]{2,1,0:T(8,128)S(1)} collective-permute-done((f32[4,8,128]{2,1,0:T(8,128)S(1)}, f32[4,8,128]{2,1,0:T(8,128)S(1)}, u32[]{:S(2)}, u32[]{:S(2)}) %collective-permute-start.2) | collective-permute-done | bytes 16416 | tf_op jit(solution)/shard_map/ppermute | solution.py:537
  20.7 0.1 collective-permute-start.5
  20.8 1.7 %shard_map.98.t1_ref = f32[32,128,128]{2,1,0:T(8,128)S(1)} custom-call(s32[1]{0:T(128)} %bitcast.kz_ref, f32[96,128,128]{2,1,0:T(8,128)S(1)} %get-tuple-element.55.f_ref), custom_call_target="tpu_custom_call" | custom-call | tf_op jit(solution)/shard_map/pallas_call | solution.py:576
  22.5 2.0 %collective-permute-done.5 = f32[4,8,128]{2,1,0:T(8,128)S(1)} collective-permute-done((f32[4,8,128]{2,1,0:T(8,128)S(1)}, f32[4,8,128]{2,1,0:T(8,128)S(1)}, u32[]{:S(2)}, u32[]{:S(2)}) %collective-permute-start.5) | collective-permute-done | bytes 16416 | tf_op jit(solution)/shard_map/ppermute | solution.py:609
  24.5 6.3 %collective-permute-start.8 = (f32[4,8,128]{2,1,0:T(8,128)S(1)}, f32[4,8,128]{2,1,0:T(8,128)S(1)}, u32[]{:S(2)}, u32[]{:S(2)}) collective-permute-start(f32[4,8,128]{2,1,0:T(8,128)S(1)} %add.27.part0_ref), channel_id=1, source_target_pairs={{0,128},{32,160},{64,192},{96,224},{128,0},{160,32},{192,64},{224,... | collective-permute-start | bytes 49160 | tf_op jit(solution)/shard_map/ppermute | solution.py:537
  30.8 0.6 %collective-permute-start.7 = (f32[4,8,128]{2,1,0:T(8,128)S(1)}, f32[4,8,128]{2,1,0:T(8,128)S(1)}, u32[]{:S(2)}, u32[]{:S(2)}) collective-permute-start(f32[4,8,128]{2,1,0:T(8,128)S(1)} %add.27.part0_ref), channel_id=1, source_target_pairs={{0,192},{32,224},{64,0},{96,32},{128,64},{160,96},{192,128},{224,1... | collective-permute-start | bytes 49160 | tf_op jit(solution)/shard_map/ppermute | solution.py:537
  31.3 2.4 %collective-permute-start.6 = (f32[4,8,128]{2,1,0:T(8,128)S(1)}, f32[4,8,128]{2,1,0:T(8,128)S(1)}, u32[]{:S(2)}, u32[]{:S(2)}) collective-permute-start(f32[4,8,128]{2,1,0:T(8,128)S(1)} %add.27.part0_ref), channel_id=1, source_target_pairs={{0,64},{32,96},{64,128},{96,160},{128,192},{160,224},{192,0},{224,... | collective-permute-start | bytes 49160 | tf_op jit(solution)/shard_map/ppermute | solution.py:537
  33.7 1.7 %shard_map.99.t2_ref = f32[32,128,128]{2,1,0:T(8,128)S(1)} custom-call(s32[1]{0:T(128)} %bitcast.kz_ref, f32[96,128,128]{2,1,0:T(8,128)S(1)} %get-tuple-element.55.f_ref), custom_call_target="tpu_custom_call" | custom-call | tf_op jit(solution)/shard_map/pallas_call | solution.py:576
  35.4 0.0 collective-permute-done.8.part3_ref
  35.4 0.0 collective-permute-done.7.part2_ref
  35.4 1.9 %collective-permute-done.6.part1_ref = f32[4,8,128]{2,1,0:T(8,128)S(1)} collective-permute-done((f32[4,8,128]{2,1,0:T(8,128)S(1)}, f32[4,8,128]{2,1,0:T(8,128)S(1)}, u32[]{:S(2)}, u32[]{:S(2)}) %collective-permute-start.6) | collective-permute-done | bytes 16416 | tf_op jit(solution)/shard_map/ppermute | solution.py:537
  37.3 0.0 collective-permute-done.9.left_ref
  37.3 0.0 collective-permute-done.10.right_ref
  37.3 4.2 %shard_map.100 = (f32[12,128]{1,0:T(8,128)}, f32[96,128,128]{2,1,0:T(8,128)}) custom-call(s32[1]{0:T(128)} %bitcast.kz_ref, f32[4,8,128]{2,1,0:T(8,128)S(1)} %add.27.part0_ref, f32[4,8,128]{2,1,0:T(8,128)S(1)} %collective-permute-done.6.part1_ref, f32[4,8,128]{2,1,0:T(8,128)S(1)} %collective-permute-done.7.part2_ref, ...), custom_call_target="tpu_custom_call" | custom-call | tf_op jit(solution)/shard_map/pallas_call | solution.py:590
  (3 shorter events, 0.0 us)
Async XLA Ops:
  0.6 6.6 %copy-start = (f32[12,128]{1,0:T(8,128)S(1)}, f32[12,128]{1,0:T(8,128)}, u32[]{:S(2)}) copy-start(f32[12,128]{1,0:T(8,128)} %cover_ref.1) | copy-start | bytes 18436
  0.6 6.6 %copy-start.1 = (f32[4,2,12]{2,1,0:T(2,128)S(1)}, f32[4,2,12]{2,1,0:T(2,128)}, u32[]{:S(2)}) copy-start(f32[4,2,12]{2,1,0:T(2,128)} %rates_ref.1) | copy-start | bytes 1156
  0.7 6.6 %copy-start.2 = (s32[1,128]{1,0:T(1,128)S(1)}, s32[1,128]{1,0:T(1,128)}, u32[]{:S(2)}) copy-start(s32[1,128]{1,0:T(1,128)} %cell_ref.3) | copy-start | bytes 1540
  0.7 6.5 %copy-start.3 = (s32[12,3]{0,1:T(4,128)S(1)}, s32[12,3]{0,1:T(4,128)}, u32[]{:S(2)}) copy-start(s32[12,3]{0,1:T(4,128)} %param.13) | copy-start | bytes 436
  0.7 6.5 %copy-start.4 = (f32[4,3]{1,0:T(4,128)S(1)}, f32[4,3]{1,0:T(4,128)}, u32[]{:S(2)}) copy-start(f32[4,3]{1,0:T(4,128)} %stick_ref.1) | copy-start | bytes 148
  0.7 6.5 %copy-start.5 = (f32[128]{0:T(128)S(1)}, f32[128]{0:T(128)}, u32[]{:S(2)}) copy-start(f32[128]{0:T(128)} %param.9) | copy-start | bytes 1540
  0.7 6.5 %copy-start.6 = (s32[128]{0:T(128)S(1)}, s32[128]{0:T(128)}, u32[]{:S(2)}) copy-start(s32[128]{0:T(128)} %param.12) | copy-start | bytes 1540
  4.2 4.4 %collective-permute-start = (f32[4,8,128]{2,1,0:T(8,128)S(1)}, f32[4,8,128]{2,1,0:T(8,128)S(1)}, u32[]{:S(2)}, u32[]{:S(2)}) collective-permute-start(f32[4,8,128]{2,1,0:T(8,128)S(1)} %get-tuple-element.32), channel_id=1, source_target_pairs={{0,1},{1,2},{2,3},{3,4},{4,5},{5,6},{6,7},{7,0},{8,9},{9,10},{10,1... | collective-permute-start | bytes 49160 | tf_op jit(solution)/shard_map/ppermute | solution.py:537
  4.3 4.4 %collective-permute-start.1 = (f32[4,8,128]{2,1,0:T(8,128)S(1)}, f32[4,8,128]{2,1,0:T(8,128)S(1)}, u32[]{:S(2)}, u32[]{:S(2)}) collective-permute-start(f32[4,8,128]{2,1,0:T(8,128)S(1)} %get-tuple-element.33), channel_id=1, source_target_pairs={{0,7},{1,0},{2,1},{3,2},{4,3},{5,4},{6,5},{7,6},{8,15},{9,8},{10,9... | collective-permute-start | bytes 49160 | tf_op jit(solution)/shard_map/ppermute | solution.py:537
  8.7 28.6 %collective-permute-start.9 = (f32[96,32,128]{2,1,0:T(8,128)S(1)}, f32[96,32,128]{2,1,0:T(8,128)S(1)}, u32[]{:S(2)}, u32[]{:S(2)}) collective-permute-start(f32[96,32,128]{2,1,0:T(8,128)S(1)} %get-tuple-element.51), channel_id=1, source_target_pairs={{0,1},{1,2},{2,3},{3,4},{4,5},{5,6},{6,7},{7,0},{8,9},{9,10},{10,1... | collective-permute-start | bytes 4718600 | tf_op jit(solution)/shard_map/ppermute | solution.py:537
  9.1 28.2 %collective-permute-start.10 = (f32[96,32,128]{2,1,0:T(8,128)S(1)}, f32[96,32,128]{2,1,0:T(8,128)S(1)}, u32[]{:S(2)}, u32[]{:S(2)}) collective-permute-start(f32[96,32,128]{2,1,0:T(8,128)S(1)} %get-tuple-element.52), channel_id=1, source_target_pairs={{0,7},{1,0},{2,1},{3,2},{4,3},{5,4},{6,5},{7,6},{8,15},{9,8},{10,9... | collective-permute-start | bytes 4718600 | tf_op jit(solution)/shard_map/ppermute | solution.py:537
  11.6 6.7 %collective-permute-start.4 = (f32[4,8,128]{2,1,0:T(8,128)S(1)}, f32[4,8,128]{2,1,0:T(8,128)S(1)}, u32[]{:S(2)}, u32[]{:S(2)}) collective-permute-start(f32[4,8,128]{2,1,0:T(8,128)S(1)} %add_add_fusion.1), channel_id=1, source_target_pairs={{0,16},{8,24},{16,0},{24,8},{1,17},{9,25},{17,1},{25,9},{2,18},{10... | collective-permute-start | bytes 49160 | tf_op jit(solution)/shard_map/ppermute | solution.py:537
  14.6 3.7 %collective-permute-start.3 = (f32[4,8,128]{2,1,0:T(8,128)S(1)}, f32[4,8,128]{2,1,0:T(8,128)S(1)}, u32[]{:S(2)}, u32[]{:S(2)}) collective-permute-start(f32[4,8,128]{2,1,0:T(8,128)S(1)} %add_add_fusion.1), channel_id=1, source_target_pairs={{0,24},{8,0},{16,8},{24,16},{1,25},{9,1},{17,9},{25,17},{2,26},{10... | collective-permute-start | bytes 49160 | tf_op jit(solution)/shard_map/ppermute | solution.py:537
  15.8 4.9 %collective-permute-start.2 = (f32[4,8,128]{2,1,0:T(8,128)S(1)}, f32[4,8,128]{2,1,0:T(8,128)S(1)}, u32[]{:S(2)}, u32[]{:S(2)}) collective-permute-start(f32[4,8,128]{2,1,0:T(8,128)S(1)} %add_add_fusion.1), channel_id=1, source_target_pairs={{0,8},{8,16},{16,24},{24,0},{1,9},{9,17},{17,25},{25,1},{2,10},{10... | collective-permute-start | bytes 49160 | tf_op jit(solution)/shard_map/ppermute | solution.py:537
  20.7 3.7 %collective-permute-start.5 = (f32[4,8,128]{2,1,0:T(8,128)S(1)}, f32[4,8,128]{2,1,0:T(8,128)S(1)}, u32[]{:S(2)}, u32[]{:S(2)}) collective-permute-start(f32[4,8,128]{2,1,0:T(8,128)S(1)} %add_add_fusion), channel_id=1, source_target_pairs={{0,32},{32,0},{64,96},{96,64},{128,160},{160,128},{192,224},{224,1... | collective-permute-start | bytes 49160 | tf_op jit(solution)/shard_map/ppermute | solution.py:609
  24.5 10.9 %collective-permute-start.8 = (f32[4,8,128]{2,1,0:T(8,128)S(1)}, f32[4,8,128]{2,1,0:T(8,128)S(1)}, u32[]{:S(2)}, u32[]{:S(2)}) collective-permute-start(f32[4,8,128]{2,1,0:T(8,128)S(1)} %add.27.part0_ref), channel_id=1, source_target_pairs={{0,128},{32,160},{64,192},{96,224},{128,0},{160,32},{192,64},{224,... | collective-permute-start | bytes 49160 | tf_op jit(solution)/shard_map/ppermute | solution.py:537
  30.8 4.6 %collective-permute-start.7 = (f32[4,8,128]{2,1,0:T(8,128)S(1)}, f32[4,8,128]{2,1,0:T(8,128)S(1)}, u32[]{:S(2)}, u32[]{:S(2)}) collective-permute-start(f32[4,8,128]{2,1,0:T(8,128)S(1)} %add.27.part0_ref), channel_id=1, source_target_pairs={{0,192},{32,224},{64,0},{96,32},{128,64},{160,96},{192,128},{224,1... | collective-permute-start | bytes 49160 | tf_op jit(solution)/shard_map/ppermute | solution.py:537
  31.3 6.0 %collective-permute-start.6 = (f32[4,8,128]{2,1,0:T(8,128)S(1)}, f32[4,8,128]{2,1,0:T(8,128)S(1)}, u32[]{:S(2)}, u32[]{:S(2)}) collective-permute-start(f32[4,8,128]{2,1,0:T(8,128)S(1)} %add.27.part0_ref), channel_id=1, source_target_pairs={{0,64},{32,96},{64,128},{96,160},{128,192},{160,224},{192,0},{224,... | collective-permute-start | bytes 49160 | tf_op jit(solution)/shard_map/ppermute | solution.py:537

commit v4 on v3

--- a/solution.py
+++ b/solution.py
@@ -73,13 +73,16 @@
 
 
 def moments_kernel(
-    kz_ref, f_hbm, own_ref, to_right_ref, to_left_ref, f_ref, rise_ref, fall_ref, acc_ref, f_sem,
+    f_hbm, own_ref, to_far_ref, to_near_ref, f_ref, far_ref, near_ref, acc_ref, f_sem,
 ):
     for c in range(BLOCKS):
         chunk(f_hbm, f_ref, f_sem, c).start()
     base = pair_speed()
     speeds = [jnp.abs(base + 2.0 * SPACING * j) for j in range(PAIRS)]
     acc_ref[...] = jnp.zeros_like(acc_ref)
+    second = lax.axis_index("space") % 2 == 1
+    far_row = jnp.where(second, 65, 0)
+    near_row = 65 - far_row
 
     def one(k, carry):
         zero = jnp.zeros(TILE, jnp.float32)
@@ -99,8 +102,8 @@
         for h in range(2):
             for q in range(2):
                 to = pl.ds(16 * h + 8 * q, 8)
-                fall_ref[k, to, :] = f_ref[k, pl.ds(32 * q + 2 * h, 8, 4), :]
-                rise_ref[k, to, :] = f_ref[k, pl.ds(64 + 32 * q + 2 * h + 1, 8, 4), :]
+                far_ref[k, to, :] = f_ref[k, pl.ds(far_row + 32 * q + 2 * h, 8, 4), :]
+                near_ref[k, to, :] = f_ref[k, pl.ds(near_row + 32 * q + 2 * h, 8, 4), :]
         cy = speed_of(k % VG)
         cy2 = cy * cy
         acy = jnp.abs(cy)
@@ -120,7 +123,7 @@
     def turn(c, carry):
         species, half = c // 4, c % 4 // 2
         chunk(f_hbm, f_ref, f_sem, c).wait()
-        total = lax.fori_loop(0, KYS, lambda i, v: one(c * KYS + i, v), start, unroll=4)
+        total = lax.fori_loop(0, KYS, lambda i, v: one(c * KYS + i, v), start, unroll=8)
         for q in range(12):
             acc_ref[species, q] += total[q]
         for q in range(4):
@@ -130,7 +133,7 @@
     lax.fori_loop(0, BLOCKS, turn, 0)
     row = rows()
     lane = lanes()
-    cz = speed_of(kz_ref[0])
+    cz = own_speed_z()
     acz = jnp.abs(cz)
     rise = cz > 0.0
     odd = row % 2 == 1
@@ -192,8 +195,14 @@
             if out is own_ref:
                 out[t] = value
             else:
-                to_right_ref[t] = jnp.where(odd, 0.0, down(value, -1))
-                to_left_ref[t] = jnp.where(odd, down(value, 1), 0.0)
+                to_right = jnp.where(odd, 0.0, down(value, -1))
+                to_left = jnp.where(odd, down(value, 1), 0.0)
+                to_far_ref[t] = jnp.where(second, to_right, to_left)
+                to_near_ref[t] = jnp.where(second, to_left, to_right)
+
+
+def own_speed_z():
+    return speed_of(lax.axis_index("z") * lax.axis_size("x") + lax.axis_index("x"))
 
 
 def selector(face_cell):
@@ -213,7 +222,7 @@
 
 
 def wall_kernel(
-    kz_ref, stoich_ref, stick_ref, rates_ref, temp_ref, cover_ref, cell_ref, owner_ref,
+    stoich_ref, stick_ref, rates_ref, temp_ref, cover_ref, cell_ref, owner_ref,
     surface_ref, sums_ref, wall_x_ref, wall_y_ref,
 ):
     select = selector(cell_ref[...])
@@ -263,7 +272,7 @@
     k_rows = lax.broadcasted_iota(jnp.int32, (VG, 128), 0)
     c = speed_of(k_rows)
     up = jnp.maximum(c, 0.0)
-    cz = speed_of(kz_ref[0])
+    cz = own_speed_z()
     cy = c[VG // 2 :]
     temps = [temp, pltpu.roll(temp, 64, 1)]
     low = lax.broadcasted_iota(jnp.int32, (VG, 128), 1) < 64
@@ -301,9 +310,9 @@
             wall_y_ref[s, x] = (cy / jnp.abs(cz)) * jnp.exp(rate * (cy * cy)) * jnp.exp(rate * (cz * cz))
 
 
-def shift_kernel(s, kz_ref, f_ref, t_ref, z0_ref, z1_ref):
+def shift_kernel(s, f_ref, t_ref, z0_ref, z1_ref):
     low = lanes() < 64
-    cz = speed_of(kz_ref[0])
+    cz = own_speed_z()
     acz = jnp.abs(cz)
     coef_z = TIME_STEP * acz
     octet = speed_of(lax.broadcasted_iota(jnp.int32, TILE, 0))
@@ -364,8 +373,8 @@
 
 
 def step_kernel(
-    kz_ref, part0_ref, part1_ref, part2_ref, part3_ref, surface_ref, sums_ref, cell_ref,
-    wall_x_ref, wall_y_ref, left_ref, right_ref, t0_ref, t1_ref, t2_ref,
+    part0_ref, part1_ref, part2_ref, part3_ref, surface_ref, sums_ref, cell_ref,
+    wall_x_ref, wall_y_ref, far_ref, near_ref, t0_ref, t1_ref, t2_ref,
     cover_ref, out_hbm,
     out_ref, ex_ref, ey_ref, wy_ref, keep_ref, out_sem,
 ):
@@ -447,7 +456,7 @@
     bulk = [v / mass for v in mom]
     flow = bulk[0] * bulk[0] + bulk[1] * bulk[1] + bulk[2] * bulk[2]
     temperature = (energy - mass * flow) / (3.0 * gas)
-    cz = speed_of(kz_ref[0])
+    cz = own_speed_z()
     acz = jnp.abs(cz)
     coef_z = TIME_STEP * acz
     grid = speed_of(lax.broadcasted_iota(jnp.int32, (VG, 128), 0))
@@ -475,6 +484,7 @@
 
     octet = speed_of(lax.broadcasted_iota(jnp.int32, TILE, 0))
     coef_x = [jnp.abs(octet + 8.0 * SPACING * q) / acz for q in range(4)]
+    second = lax.axis_index("space") % 2 == 1
 
     def advance(first, s, lower):
         t_ref = (t0_ref, t1_ref, t2_ref)[s]
@@ -492,10 +502,13 @@
                 for r in range(4):
                     h, x = r // 2, r % 2
                     value = t_ref[ky, 32 * r + 8 * q : 32 * r + 8 * q + 8, :]
+                    at = pl.ds(16 * h + 8 * (q % 2), 8)
                     if q < 2 and x == 1:
-                        value = value + coef_x[q] * right_ref[k, pl.ds(16 * h + 8 * q, 8), :]
+                        beside = jnp.where(second, far_ref[k, at, :], near_ref[k, at, :])
+                        value = value + coef_x[q] * beside
                     if q >= 2 and x == 0:
-                        value = value + coef_x[q] * left_ref[k, pl.ds(16 * h + 8 * (q - 2), 8), :]
+                        beside = jnp.where(second, near_ref[k, at, :], far_ref[k, at, :])
+                        value = value + coef_x[q] * beside
                     if lower and h == 0:
                         value = value + wall_x_ref[s, x, 8 * q : 8 * q + 8, :] * wy[x]
                     value = keep[r] * value + ex_ref[s, r, 8 * q : 8 * q + 8, :] * ey[r]
@@ -526,6 +539,7 @@
 BIG = pltpu.CompilerParams(vmem_limit_bytes=16 * 1024 * 1024)
 SMALL = pltpu.CompilerParams(vmem_limit_bytes=4 * 1024 * 1024)
 DMA = pltpu.SemaphoreType.DMA
+LONG = pl.CostEstimate(flops=10**10, bytes_accessed=10**7, transcendentals=0)
 
 
 def shape(*dims):
@@ -541,10 +555,10 @@
     return pltpu.with_memory_space_constraint(value, pltpu.VMEM)
 
 
-def moments_call(kz, field):
+def moments_call(field):
     return pl.pallas_call(
         moments_kernel,
-        in_specs=[SMEM, HBM],
+        in_specs=[HBM],
         out_specs=[VMEM] * 6,
         out_shape=[pltpu.VMEM((4, 8, 128), F32)] * 3
         + [pltpu.VMEM((S * VG, 128, 128), F32)]
@@ -554,13 +568,13 @@
             DMA((BLOCKS,)),
         ],
         compiler_params=BIG,
-    )(kz, field)
+    )(field)
 
 
 def wall_call(*args):
     return pl.pallas_call(
         wall_kernel,
-        in_specs=[SMEM] * 4 + [VMEM] * 4,
+        in_specs=[SMEM] * 3 + [VMEM] * 4,
         out_specs=[VMEM] * 4,
         out_shape=[
             pltpu.VMEM((9, 16, 128), F32),
@@ -572,10 +586,10 @@
     )(*args)
 
 
-def shift_call(s, kz, field):
+def shift_call(s, field):
     return pl.pallas_call(
         functools.partial(shift_kernel, s),
-        in_specs=[SMEM, VMEM],
+        in_specs=[VMEM],
         out_specs=VMEM,
         out_shape=pltpu.VMEM((VG, 128, 128), F32),
         scratch_shapes=[
@@ -583,13 +597,14 @@
             pltpu.VMEM((GROUP * 128, 128), F32),
         ],
         compiler_params=BIG,
-    )(kz, near(field))
+        cost_estimate=LONG,
+    )(near(field))
 
 
 def step_call(*args):
     return pl.pallas_call(
         step_kernel,
-        in_specs=[SMEM] + [VMEM] * 14,
+        in_specs=[VMEM] * 14,
         out_specs=[VMEM, HBM],
         out_shape=[shape(NSURF, 128), shape(S * VG, 128, 128)],
         scratch_shapes=[
@@ -609,44 +624,49 @@
     return lax.ppermute(value, axis, [(i, i ^ 1) for i in range(peers)])
 
 
+def crossed(value, axis, by):
+    peers = lax.axis_size(axis)
+    pairs = [(i, (i + (by if i % 2 else -by)) % peers) for i in range(peers)]
+    return lax.ppermute(value, axis, pairs)
+
+
 def per_device(
     distribution, wall_temp, coverage, face_cell, face_owner, stoichiometry, sticking, surface_rates
 ):
-    kz = lax.axis_index(("z", "x")).astype(jnp.int32).reshape(1)
     field = (
         distribution.reshape(S, VG * VG, CX, 2, 128)
         .transpose(0, 1, 3, 2, 4)
         .reshape(S * VG, 128, 128)
     )
     field = pltpu.with_memory_space_constraint(field, pltpu.HBM)
-    own, to_right, to_left, held, rise, fall = moments_call(kz, field)
+    own, to_far, to_near, held, far, nigh = moments_call(field)
     together = lax.optimization_barrier
     face_row = face_cell.reshape(1, 128)
 
     temp, own = together((wall_temp.reshape(1, 128), own))
     walls = wall_call(
-        kz, stoichiometry.T, sticking, surface_rates, temp, coverage, face_row,
+        stoichiometry.T, sticking, surface_rates, temp, coverage, face_row,
         face_owner.reshape(1, 128),
     )
-    own = own + shifted(to_right, "space", 1) + shifted(to_left, "space", -1)
-    own, rise, fall, held, walls = together((own, rise, fall, held, walls))
-
-    from_left = shifted(rise, "space", 1)
-    from_right = shifted(fall, "space", -1)
-    moved0 = shift_call(0, kz, held)
+    own = own + crossed(to_far, "space", 1) + paired(to_near, "space")
+    own, held, walls = together((own, held, walls))
+
+    far = crossed(near(far), "space", 1)
+    nigh = paired(near(nigh), "space")
+    moved0 = shift_call(0, held)
     own = own + shifted(own, "x", 1) + shifted(own, "x", 3) + shifted(own, "x", 2)
     own, moved0, held = together((own, moved0, held))
 
-    moved1 = shift_call(1, kz, held)
+    moved1 = shift_call(1, held)
     own = own + paired(own, "z")
     own, moved1, held = together((own, moved1, held))
 
-    moved2 = shift_call(2, kz, held)
-    parts = [own, shifted(own, "z", 2), shifted(own, "z", 6), shifted(own, "z", 4)]
+    moved2 = shift_call(2, held)
+    parts = [own] + [crossed(own, "z", by) for by in (1, 2, 3)]
     surface, sums, wall_x, wall_y = walls
     vmem = [near(v) for v in parts + [surface, sums]]
     covers, advanced = step_call(
-        kz, *vmem, face_row, near(wall_x), near(wall_y), near(from_left), near(from_right),
+        *vmem, face_row, near(wall_x), near(wall_y), near(far), near(nigh),
         near(moved0), near(moved1), near(moved2),
     )
     advanced = (

time: 41.5 us -> 37.9 us (0.913)
  starting transfers between devices: 20.3 us -> 17 us
  waiting for transfers between devices: 6.6 us -> 6 us
    ppermute x10 -> x3, starting transfers between devices: 20.2 us -> 5.14 us  [shifted(): lax.ppermute(value, axis, [(i, (i + by) % peers) for i in range(peers)])]
    ppermute x0 -> x5, starting transfers between devices: none -> 11.7 us  [crossed(): return lax.ppermute(value, axis, pairs)]
    ppermute x10 -> x3, waiting for transfers between devices: 4.65 us -> 2.38 us  [shifted(): lax.ppermute(value, axis, [(i, (i + by) % peers) for i in range(peers)])]
    ppermute x0 -> x5, waiting for transfers between devices: none -> 1.68 us  [crossed(): return lax.ppermute(value, axis, pairs)]
    ppermute x1 -> x3, waiting for transfers between devices: 1.95 us -> 1.94 us  [paired(): return lax.ppermute(value, axis, [(i, i ^ 1) for i in range(peers)])]
  transfers between devices with their start and end apart: 11 -> 11, of which waited for: 4 -> 3; matrix products, arithmetic and copies ran while one was open for 0% -> 0% of each run, Pallas kernels for 15% -> 16%
where the time goes in v4:
time: 37.9 us; the launch traced here: 37.5 us
  starting transfers between devices  17 us (45%)
  Pallas kernels  13.6 us (36%)
  waiting for transfers between devices  6 us (16%)
  between operations  0.79 us (2%)
    ppermute x5, starting transfers between devices, crossed(): return lax.ppermute(value, axis, pairs)  11.7 us
    ppermute x3, starting transfers between devices, shifted(): lax.ppermute(value, axis, [(i, (i + by) % peers) for i in range(peers)])  5.14 us
    pallas_call x3, Pallas kernels, shift_call(): pl.pallas_call(functools.partial(shift_kernel, s), in_specs=[VMEM], out_s...  5.04 us
    pallas_call x1, Pallas kernels, step_call(): pl.pallas_call(step_kernel, in_specs=[VMEM] * 14, out_specs=[VMEM, HBM],...  4.17 us
    pallas_call x1, Pallas kernels, moments_call(): pl.pallas_call(moments_kernel, in_specs=[HBM], out_specs=[VMEM] * 6, out_...  3.36 us
    ppermute x3, waiting for transfers between devices, shifted(): lax.ppermute(value, axis, [(i, (i + by) % peers) for i in range(peers)])  2.38 us
    ppermute x3, waiting for transfers between devices, paired(): return lax.ppermute(value, axis, [(i, i ^ 1) for i in range(peers)])  1.94 us
    ppermute x5, waiting for transfers between devices, crossed(): return lax.ppermute(value, axis, pairs)  1.68 us
  transfers between devices with their start and end apart: 11, of which 3 were waited for; matrix products, arithmetic and copies ran while one was open for 0% of the time, Pallas kernels for 16%

profile of v4, /device:TPU:32, one launch (start us, length us, event | category | flops | bytes accessed | tf_op | source)
XLA Modules:
  0.0 37.5 jit_solution(3297799449815293031)
XLA Ops:
  0.6 0.0 copy-start
  0.6 0.0 copy-start.1
  0.7 0.0 copy-start.2
  0.7 0.0 copy-start.3
  0.7 0.0 copy-start.4
  0.7 0.0 copy-start.5
  0.7 0.0 copy-start.6
  0.7 3.4 %shard_map.95 = (f32[4,8,128]{2,1,0:T(8,128)S(1)}, f32[4,8,128]{2,1,0:T(8,128)S(1)}, f32[4,8,128]{2,1,0:T(8,128)S(1)}, f32[96,128,128]{2,1,0:T(8,128)S(1)}, f32[...) custom-call(f32[96,128,128]{2,1,0:T(8,128)} %bitcast.16), custom_call_target="tpu_custom_call" | custom-call | tf_op jit(solution)/shard_map/pallas_call | solution.py:559
  4.1 2.5 %collective-permute-start = (f32[4,8,128]{2,1,0:T(8,128)S(1)}, f32[4,8,128]{2,1,0:T(8,128)S(1)}, u32[]{:S(2)}, u32[]{:S(2)}) collective-permute-start(f32[4,8,128]{2,1,0:T(8,128)S(1)} %get-tuple-element.30), channel_id=1, source_target_pairs={{0,7},{1,2},{2,1},{3,4},{4,3},{5,6},{6,5},{7,0},{8,15},{9,10},{10,... | collective-permute-start | bytes 49160 | tf_op jit(solution)/shard_map/ppermute | solution.py:630
  6.6 0.0 collective-permute-start.1
  6.6 0.9 %collective-permute-start.9 = (f32[96,32,128]{2,1,0:T(8,128)S(1)}, f32[96,32,128]{2,1,0:T(8,128)S(1)}, u32[]{:S(2)}, u32[]{:S(2)}) collective-permute-start(f32[96,32,128]{2,1,0:T(8,128)S(1)} %get-tuple-element.47), channel_id=1, source_target_pairs={{0,7},{1,2},{2,1},{3,4},{4,3},{5,6},{6,5},{7,0},{8,15},{9,10},{10,... | collective-permute-start | bytes 4718600 | tf_op jit(solution)/shard_map/ppermute | solution.py:630
  7.5 0.1 collective-permute-start.10
  7.5 0.0 copy-done
  7.5 0.0 copy-done.1
  7.5 0.0 copy-done.2
  7.5 0.0 copy-done.3
  7.6 0.0 copy-done.4
  7.6 0.0 copy-done.5
  7.6 0.0 copy-done.6
  7.6 1.0 %shard_map.96 = (f32[9,16,128]{2,1,0:T(8,128)S(1)}, f32[3,8,128]{2,1,0:T(8,128)S(1)}, f32[3,2,32,128]{3,2,1,0:T(8,128)S(1)}, f32[3,2,16,128]{3,2,1,0:T(8,128)S(1)}) custom-call(s32[3,12]{1,0:T(4,128)S(1)} %bitcast.13, f32[4,3]{1,0:T(4,128)S(1)} %copy-done.4, f32[4,2,12]{2,1,0:T(2,128)S(1)} %copy-done.1, f32[1,128]{1,0:T(1,128)S(1)} %bitcast.14, ...), custom_call_target="tpu_custom_call" | custom-call | tf_op jit(solution)/shard_map/pallas_call | solution.py:575
  8.6 0.0 collective-permute-done
  8.6 0.0 collective-permute-done.1
  8.7 3.1 %collective-permute-start.4 = (f32[4,8,128]{2,1,0:T(8,128)S(1)}, f32[4,8,128]{2,1,0:T(8,128)S(1)}, u32[]{:S(2)}, u32[]{:S(2)}) collective-permute-start(f32[4,8,128]{2,1,0:T(8,128)S(1)} %add_add_fusion.1), channel_id=1, source_target_pairs={{0,16},{8,24},{16,0},{24,8},{1,17},{9,25},{17,1},{25,9},{2,18},{10... | collective-permute-start | bytes 49160 | tf_op jit(solution)/shard_map/ppermute | solution.py:551
  11.8 1.1 %collective-permute-start.3 = (f32[4,8,128]{2,1,0:T(8,128)S(1)}, f32[4,8,128]{2,1,0:T(8,128)S(1)}, u32[]{:S(2)}, u32[]{:S(2)}) collective-permute-start(f32[4,8,128]{2,1,0:T(8,128)S(1)} %add_add_fusion.1), channel_id=1, source_target_pairs={{0,24},{8,0},{16,8},{24,16},{1,25},{9,1},{17,9},{25,17},{2,26},{10... | collective-permute-start | bytes 49160 | tf_op jit(solution)/shard_map/ppermute | solution.py:551
  12.9 0.9 %collective-permute-start.2 = (f32[4,8,128]{2,1,0:T(8,128)S(1)}, f32[4,8,128]{2,1,0:T(8,128)S(1)}, u32[]{:S(2)}, u32[]{:S(2)}) collective-permute-start(f32[4,8,128]{2,1,0:T(8,128)S(1)} %add_add_fusion.1), channel_id=1, source_target_pairs={{0,8},{8,16},{16,24},{24,0},{1,9},{9,17},{17,25},{25,1},{2,10},{10... | collective-permute-start | bytes 49160 | tf_op jit(solution)/shard_map/ppermute | solution.py:551
  13.8 1.7 %shard_map.97.t0_ref = f32[32,128,128]{2,1,0:T(8,128)S(1)} custom-call(f32[96,128,128]{2,1,0:T(8,128)S(1)} %get-tuple-element.51.f_ref), custom_call_target="tpu_custom_call" | custom-call | flops 10000000000 | bytes 10000000 | tf_op jit(solution)/shard_map/pallas_call | solution.py:590
  15.5 0.0 collective-permute-done.4
  15.5 0.0 collective-permute-done.3
  15.5 2.4 %collective-permute-done.2 = f32[4,8,128]{2,1,0:T(8,128)S(1)} collective-permute-done((f32[4,8,128]{2,1,0:T(8,128)S(1)}, f32[4,8,128]{2,1,0:T(8,128)S(1)}, u32[]{:S(2)}, u32[]{:S(2)}) %collective-permute-start.2) | collective-permute-done | bytes 16416 | tf_op jit(solution)/shard_map/ppermute | solution.py:551
  17.9 0.1 collective-permute-start.5
  18.0 1.7 %shard_map.98.t1_ref = f32[32,128,128]{2,1,0:T(8,128)S(1)} custom-call(f32[96,128,128]{2,1,0:T(8,128)S(1)} %get-tuple-element.51.f_ref), custom_call_target="tpu_custom_call" | custom-call | flops 10000000000 | bytes 10000000 | tf_op jit(solution)/shard_map/pallas_call | solution.py:590
  19.7 1.9 %collective-permute-done.5 = f32[4,8,128]{2,1,0:T(8,128)S(1)} collective-permute-done((f32[4,8,128]{2,1,0:T(8,128)S(1)}, f32[4,8,128]{2,1,0:T(8,128)S(1)}, u32[]{:S(2)}, u32[]{:S(2)}) %collective-permute-start.5) | collective-permute-done | bytes 16416 | tf_op jit(solution)/shard_map/ppermute | solution.py:624
  21.6 5.8 %collective-permute-start.8 = (f32[4,8,128]{2,1,0:T(8,128)S(1)}, f32[4,8,128]{2,1,0:T(8,128)S(1)}, u32[]{:S(2)}, u32[]{:S(2)}) collective-permute-start(f32[4,8,128]{2,1,0:T(8,128)S(1)} %add.23.part0_ref), channel_id=1, source_target_pairs={{0,160},{32,128},{64,224},{96,192},{128,32},{160,0},{192,96},{224,... | collective-permute-start | bytes 49160 | tf_op jit(solution)/shard_map/ppermute | solution.py:630
  27.4 1.5 %collective-permute-start.7 = (f32[4,8,128]{2,1,0:T(8,128)S(1)}, f32[4,8,128]{2,1,0:T(8,128)S(1)}, u32[]{:S(2)}, u32[]{:S(2)}) collective-permute-start(f32[4,8,128]{2,1,0:T(8,128)S(1)} %add.23.part0_ref), channel_id=1, source_target_pairs={{0,192},{32,96},{64,0},{96,160},{128,64},{160,224},{192,128},{224,... | collective-permute-start | bytes 49160 | tf_op jit(solution)/shard_map/ppermute | solution.py:630
  28.9 1.0 %collective-permute-start.6 = (f32[4,8,128]{2,1,0:T(8,128)S(1)}, f32[4,8,128]{2,1,0:T(8,128)S(1)}, u32[]{:S(2)}, u32[]{:S(2)}) collective-permute-start(f32[4,8,128]{2,1,0:T(8,128)S(1)} %add.23.part0_ref), channel_id=1, source_target_pairs={{0,224},{32,64},{64,32},{96,128},{128,96},{160,192},{192,160},{224... | collective-permute-start | bytes 49160 | tf_op jit(solution)/shard_map/ppermute | solution.py:630
  29.9 1.7 %shard_map.99.t2_ref = f32[32,128,128]{2,1,0:T(8,128)S(1)} custom-call(f32[96,128,128]{2,1,0:T(8,128)S(1)} %get-tuple-element.51.f_ref), custom_call_target="tpu_custom_call" | custom-call | flops 10000000000 | bytes 10000000 | tf_op jit(solution)/shard_map/pallas_call | solution.py:590
  31.6 0.0 collective-permute-done.8.part3_ref
  31.6 1.7 %collective-permute-done.7.part2_ref = f32[4,8,128]{2,1,0:T(8,128)S(1)} collective-permute-done((f32[4,8,128]{2,1,0:T(8,128)S(1)}, f32[4,8,128]{2,1,0:T(8,128)S(1)}, u32[]{:S(2)}, u32[]{:S(2)}) %collective-permute-start.7) | collective-permute-done | bytes 16416 | tf_op jit(solution)/shard_map/ppermute | solution.py:630
  33.3 0.0 collective-permute-done.6.part1_ref
  33.3 0.0 collective-permute-done.9.far_ref
  33.3 0.0 collective-permute-done.10.near_ref
  33.3 4.2 %shard_map.100 = (f32[12,128]{1,0:T(8,128)}, f32[96,128,128]{2,1,0:T(8,128)}) custom-call(f32[4,8,128]{2,1,0:T(8,128)S(1)} %add.23.part0_ref, f32[4,8,128]{2,1,0:T(8,128)S(1)} %collective-permute-done.6.part1_ref, f32[4,8,128]{2,1,0:T(8,128)S(1)} %collective-permute-done.7.part2_ref, f32[4,8,128]{2,1,0:T(8,128)S(1)} %collective-permute-done.8.part3_ref, ...), custom_call_target="tpu_custom_call" | custom-call | tf_op jit(solution)/shard_map/pallas_call | solution.py:605
  (3 shorter events, 0.0 us)
Async XLA Ops:
  0.6 6.9 %copy-start = (f32[12,128]{1,0:T(8,128)S(1)}, f32[12,128]{1,0:T(8,128)}, u32[]{:S(2)}) copy-start(f32[12,128]{1,0:T(8,128)} %cover_ref.1) | copy-start | bytes 18436
  0.6 6.9 %copy-start.1 = (f32[4,2,12]{2,1,0:T(2,128)S(1)}, f32[4,2,12]{2,1,0:T(2,128)}, u32[]{:S(2)}) copy-start(f32[4,2,12]{2,1,0:T(2,128)} %rates_ref.1) | copy-start | bytes 1156
  0.7 6.9 %copy-start.2 = (s32[1,128]{1,0:T(1,128)S(1)}, s32[1,128]{1,0:T(1,128)}, u32[]{:S(2)}) copy-start(s32[1,128]{1,0:T(1,128)} %cell_ref.3) | copy-start | bytes 1540
  0.7 6.9 %copy-start.3 = (s32[12,3]{0,1:T(4,128)S(1)}, s32[12,3]{0,1:T(4,128)}, u32[]{:S(2)}) copy-start(s32[12,3]{0,1:T(4,128)} %param.13) | copy-start | bytes 436
  0.7 6.9 %copy-start.4 = (f32[4,3]{1,0:T(4,128)S(1)}, f32[4,3]{1,0:T(4,128)}, u32[]{:S(2)}) copy-start(f32[4,3]{1,0:T(4,128)} %stick_ref.1) | copy-start | bytes 148
  0.7 6.9 %copy-start.5 = (f32[128]{0:T(128)S(1)}, f32[128]{0:T(128)}, u32[]{:S(2)}) copy-start(f32[128]{0:T(128)} %param.9) | copy-start | bytes 1540
  0.7 6.9 %copy-start.6 = (s32[128]{0:T(128)S(1)}, s32[128]{0:T(128)}, u32[]{:S(2)}) copy-start(s32[128]{0:T(128)} %param.12) | copy-start | bytes 1540
  4.1 4.6 %collective-permute-start = (f32[4,8,128]{2,1,0:T(8,128)S(1)}, f32[4,8,128]{2,1,0:T(8,128)S(1)}, u32[]{:S(2)}, u32[]{:S(2)}) collective-permute-start(f32[4,8,128]{2,1,0:T(8,128)S(1)} %get-tuple-element.30), channel_id=1, source_target_pairs={{0,7},{1,2},{2,1},{3,4},{4,3},{5,6},{6,5},{7,0},{8,15},{9,10},{10,... | collective-permute-start | bytes 49160 | tf_op jit(solution)/shard_map/ppermute | solution.py:630
  6.6 2.0 %collective-permute-start.1 = (f32[4,8,128]{2,1,0:T(8,128)S(1)}, f32[4,8,128]{2,1,0:T(8,128)S(1)}, u32[]{:S(2)}, u32[]{:S(2)}) collective-permute-start(f32[4,8,128]{2,1,0:T(8,128)S(1)} %get-tuple-element.31), channel_id=1, source_target_pairs={{0,1},{1,0},{2,3},{3,2},{4,5},{5,4},{6,7},{7,6},{8,9},{9,8},{10,11... | collective-permute-start | bytes 49160 | tf_op jit(solution)/shard_map/ppermute | solution.py:624
  6.6 26.7 %collective-permute-start.9 = (f32[96,32,128]{2,1,0:T(8,128)S(1)}, f32[96,32,128]{2,1,0:T(8,128)S(1)}, u32[]{:S(2)}, u32[]{:S(2)}) collective-permute-start(f32[96,32,128]{2,1,0:T(8,128)S(1)} %get-tuple-element.47), channel_id=1, source_target_pairs={{0,7},{1,2},{2,1},{3,4},{4,3},{5,6},{6,5},{7,0},{8,15},{9,10},{10,... | collective-permute-start | bytes 4718600 | tf_op jit(solution)/shard_map/ppermute | solution.py:630
  7.5 25.8 %collective-permute-start.10 = (f32[96,32,128]{2,1,0:T(8,128)S(1)}, f32[96,32,128]{2,1,0:T(8,128)S(1)}, u32[]{:S(2)}, u32[]{:S(2)}) collective-permute-start(f32[96,32,128]{2,1,0:T(8,128)S(1)} %get-tuple-element.48), channel_id=1, source_target_pairs={{0,1},{1,0},{2,3},{3,2},{4,5},{5,4},{6,7},{7,6},{8,9},{9,8},{10,11... | collective-permute-start | bytes 4718600 | tf_op jit(solution)/shard_map/ppermute | solution.py:624
  8.7 6.8 %collective-permute-start.4 = (f32[4,8,128]{2,1,0:T(8,128)S(1)}, f32[4,8,128]{2,1,0:T(8,128)S(1)}, u32[]{:S(2)}, u32[]{:S(2)}) collective-permute-start(f32[4,8,128]{2,1,0:T(8,128)S(1)} %add_add_fusion.1), channel_id=1, source_target_pairs={{0,16},{8,24},{16,0},{24,8},{1,17},{9,25},{17,1},{25,9},{2,18},{10... | collective-permute-start | bytes 49160 | tf_op jit(solution)/shard_map/ppermute | solution.py:551
  11.8 3.7 %collective-permute-start.3 = (f32[4,8,128]{2,1,0:T(8,128)S(1)}, f32[4,8,128]{2,1,0:T(8,128)S(1)}, u32[]{:S(2)}, u32[]{:S(2)}) collective-permute-start(f32[4,8,128]{2,1,0:T(8,128)S(1)} %add_add_fusion.1), channel_id=1, source_target_pairs={{0,24},{8,0},{16,8},{24,16},{1,25},{9,1},{17,9},{25,17},{2,26},{10... | collective-permute-start | bytes 49160 | tf_op jit(solution)/shard_map/ppermute | solution.py:551
  12.9 4.9 %collective-permute-start.2 = (f32[4,8,128]{2,1,0:T(8,128)S(1)}, f32[4,8,128]{2,1,0:T(8,128)S(1)}, u32[]{:S(2)}, u32[]{:S(2)}) collective-permute-start(f32[4,8,128]{2,1,0:T(8,128)S(1)} %add_add_fusion.1), channel_id=1, source_target_pairs={{0,8},{8,16},{16,24},{24,0},{1,9},{9,17},{17,25},{25,1},{2,10},{10... | collective-permute-start | bytes 49160 | tf_op jit(solution)/shard_map/ppermute | solution.py:551
  17.9 3.7 %collective-permute-start.5 = (f32[4,8,128]{2,1,0:T(8,128)S(1)}, f32[4,8,128]{2,1,0:T(8,128)S(1)}, u32[]{:S(2)}, u32[]{:S(2)}) collective-permute-start(f32[4,8,128]{2,1,0:T(8,128)S(1)} %add_add_fusion), channel_id=1, source_target_pairs={{0,32},{32,0},{64,96},{96,64},{128,160},{160,128},{192,224},{224,1... | collective-permute-start | bytes 49160 | tf_op jit(solution)/shard_map/ppermute | solution.py:624
  21.6 10.0 %collective-permute-start.8 = (f32[4,8,128]{2,1,0:T(8,128)S(1)}, f32[4,8,128]{2,1,0:T(8,128)S(1)}, u32[]{:S(2)}, u32[]{:S(2)}) collective-permute-start(f32[4,8,128]{2,1,0:T(8,128)S(1)} %add.23.part0_ref), channel_id=1, source_target_pairs={{0,160},{32,128},{64,224},{96,192},{128,32},{160,0},{192,96},{224,... | collective-permute-start | bytes 49160 | tf_op jit(solution)/shard_map/ppermute | solution.py:630
  27.4 5.8 %collective-permute-start.7 = (f32[4,8,128]{2,1,0:T(8,128)S(1)}, f32[4,8,128]{2,1,0:T(8,128)S(1)}, u32[]{:S(2)}, u32[]{:S(2)}) collective-permute-start(f32[4,8,128]{2,1,0:T(8,128)S(1)} %add.23.part0_ref), channel_id=1, source_target_pairs={{0,192},{32,96},{64,0},{96,160},{128,64},{160,224},{192,128},{224,... | collective-permute-start | bytes 49160 | tf_op jit(solution)/shard_map/ppermute | solution.py:630
  28.9 4.4 %collective-permute-start.6 = (f32[4,8,128]{2,1,0:T(8,128)S(1)}, f32[4,8,128]{2,1,0:T(8,128)S(1)}, u32[]{:S(2)}, u32[]{:S(2)}) collective-permute-start(f32[4,8,128]{2,1,0:T(8,128)S(1)} %add.23.part0_ref), channel_id=1, source_target_pairs={{0,224},{32,64},{64,32},{96,128},{128,96},{160,192},{192,160},{224... | collective-permute-start | bytes 49160 | tf_op jit(solution)/shard_map/ppermute | solution.py:630

commit v5 on v4

--- a/solution.py
+++ b/solution.py
@@ -546,11 +546,6 @@
     return jax.ShapeDtypeStruct(dims, F32)
 
 
-def shifted(value, axis, by):
-    peers = lax.axis_size(axis)
-    return lax.ppermute(value, axis, [(i, (i + by) % peers) for i in range(peers)])
-
-
 def near(value):
     return pltpu.with_memory_space_constraint(value, pltpu.VMEM)
 
@@ -619,9 +614,9 @@
     )(*args)
 
 
-def paired(value, axis):
+def paired(value, axis, by=1):
     peers = lax.axis_size(axis)
-    return lax.ppermute(value, axis, [(i, i ^ 1) for i in range(peers)])
+    return lax.ppermute(value, axis, [(i, i ^ by) for i in range(peers)])
 
 
 def crossed(value, axis, by):
@@ -654,7 +649,7 @@
     far = crossed(near(far), "space", 1)
     nigh = paired(near(nigh), "space")
     moved0 = shift_call(0, held)
-    own = own + shifted(own, "x", 1) + shifted(own, "x", 3) + shifted(own, "x", 2)
+    own = own + paired(own, "x", 1) + paired(own, "x", 3) + paired(own, "x", 2)
     own, moved0, held = together((own, moved0, held))
 
     moved1 = shift_call(1, held)

time: 37.9 us -> 36.8 us (0.971)
  starting transfers between devices: 17 us -> 16.2 us
    ppermute x6, starting transfers between devices: 5.32 us -> 4.52 us  [paired(): return lax.ppermute(value, axis, [(i, i ^ by) for i in range(peers)])]
  transfers between devices with their start and end apart: 11 -> 11, of which waited for: 3 -> 3; matrix products, arithmetic and copies ran while one was open for 0% -> 0% of each run, Pallas kernels for 16% -> 17%
where the time goes in v5:
time: 36.8 us; the launch traced here: 36.4 us
  starting transfers between devices  16.2 us (44%)
  Pallas kernels  13.6 us (37%)
  waiting for transfers between devices  5.75 us (16%)
  between operations  0.79 us (2%)
    ppermute x5, starting transfers between devices, crossed(): return lax.ppermute(value, axis, pairs)  11.7 us
    pallas_call x3, Pallas kernels, shift_call(): pl.pallas_call(functools.partial(shift_kernel, s), in_specs=[VMEM], out_s...  5.04 us
    ppermute x6, starting transfers between devices, paired(): return lax.ppermute(value, axis, [(i, i ^ by) for i in range(peers)])  4.52 us
    pallas_call x1, Pallas kernels, step_call(): pl.pallas_call(step_kernel, in_specs=[VMEM] * 14, out_specs=[VMEM, HBM],...  4.17 us
    ppermute x6, waiting for transfers between devices, paired(): return lax.ppermute(value, axis, [(i, i ^ by) for i in range(peers)])  4.07 us
    pallas_call x1, Pallas kernels, moments_call(): pl.pallas_call(moments_kernel, in_specs=[HBM], out_specs=[VMEM] * 6, out_...  3.36 us
    ppermute x5, waiting for transfers between devices, crossed(): return lax.ppermute(value, axis, pairs)  1.68 us
    pallas_call x1, Pallas kernels, wall_call(): pl.pallas_call(wall_kernel, in_specs=[SMEM] * 3 + [VMEM] * 4, out_specs=[...  1.04 us
  transfers between devices with their start and end apart: 11, of which 3 were waited for; matrix products, arithmetic and copies ran while one was open for 0% of the time, Pallas kernels for 17%

profile of v5, /device:TPU:32, one launch (start us, length us, event | category | flops | bytes accessed | tf_op | source)
XLA Modules:
  0.0 36.4 jit_solution(4514586160459281524)
XLA Ops:
  0.6 0.0 copy-start
  0.6 0.0 copy-start.1
  0.7 0.0 copy-start.2
  0.7 0.0 copy-start.3
  0.7 0.0 copy-start.4
  0.7 0.0 copy-start.5
  0.7 0.0 copy-start.6
  0.7 3.4 %shard_map.95 = (f32[4,8,128]{2,1,0:T(8,128)S(1)}, f32[4,8,128]{2,1,0:T(8,128)S(1)}, f32[4,8,128]{2,1,0:T(8,128)S(1)}, f32[96,128,128]{2,1,0:T(8,128)S(1)}, f32[...) custom-call(f32[96,128,128]{2,1,0:T(8,128)} %bitcast.16), custom_call_target="tpu_custom_call" | custom-call | tf_op jit(solution)/shard_map/pallas_call | solution.py:554
  4.1 2.5 %collective-permute-start = (f32[4,8,128]{2,1,0:T(8,128)S(1)}, f32[4,8,128]{2,1,0:T(8,128)S(1)}, u32[]{:S(2)}, u32[]{:S(2)}) collective-permute-start(f32[4,8,128]{2,1,0:T(8,128)S(1)} %get-tuple-element.30), channel_id=1, source_target_pairs={{0,7},{1,2},{2,1},{3,4},{4,3},{5,6},{6,5},{7,0},{8,15},{9,10},{10,... | collective-permute-start | bytes 49160 | tf_op jit(solution)/shard_map/ppermute | solution.py:625
  6.6 0.0 collective-permute-start.1
  6.6 0.9 %collective-permute-start.9 = (f32[96,32,128]{2,1,0:T(8,128)S(1)}, f32[96,32,128]{2,1,0:T(8,128)S(1)}, u32[]{:S(2)}, u32[]{:S(2)}) collective-permute-start(f32[96,32,128]{2,1,0:T(8,128)S(1)} %get-tuple-element.47), channel_id=1, source_target_pairs={{0,7},{1,2},{2,1},{3,4},{4,3},{5,6},{6,5},{7,0},{8,15},{9,10},{10,... | collective-permute-start | bytes 4718600 | tf_op jit(solution)/shard_map/ppermute | solution.py:625
  7.5 0.1 collective-permute-start.10
  7.5 0.0 copy-done
  7.5 0.0 copy-done.1
  7.5 0.0 copy-done.2
  7.5 0.0 copy-done.3
  7.6 0.0 copy-done.4
  7.6 0.0 copy-done.5
  7.6 0.0 copy-done.6
  7.6 1.0 %shard_map.96 = (f32[9,16,128]{2,1,0:T(8,128)S(1)}, f32[3,8,128]{2,1,0:T(8,128)S(1)}, f32[3,2,32,128]{3,2,1,0:T(8,128)S(1)}, f32[3,2,16,128]{3,2,1,0:T(8,128)S(1)}) custom-call(s32[3,12]{1,0:T(4,128)S(1)} %bitcast.13, f32[4,3]{1,0:T(4,128)S(1)} %copy-done.4, f32[4,2,12]{2,1,0:T(2,128)S(1)} %copy-done.1, f32[1,128]{1,0:T(1,128)S(1)} %bitcast.14, ...), custom_call_target="tpu_custom_call" | custom-call | tf_op jit(solution)/shard_map/pallas_call | solution.py:570
  8.6 0.0 collective-permute-done
  8.6 0.0 collective-permute-done.1
  8.7 3.1 %collective-permute-start.4 = (f32[4,8,128]{2,1,0:T(8,128)S(1)}, f32[4,8,128]{2,1,0:T(8,128)S(1)}, u32[]{:S(2)}, u32[]{:S(2)}) collective-permute-start(f32[4,8,128]{2,1,0:T(8,128)S(1)} %add_add_fusion.1), channel_id=1, source_target_pairs={{0,16},{8,24},{16,0},{24,8},{1,17},{9,25},{17,1},{25,9},{2,18},{10... | collective-permute-start | bytes 49160 | tf_op jit(solution)/shard_map/ppermute | solution.py:619
  11.8 1.1 %collective-permute-start.3 = (f32[4,8,128]{2,1,0:T(8,128)S(1)}, f32[4,8,128]{2,1,0:T(8,128)S(1)}, u32[]{:S(2)}, u32[]{:S(2)}) collective-permute-start(f32[4,8,128]{2,1,0:T(8,128)S(1)} %add_add_fusion.1), channel_id=1, source_target_pairs={{0,24},{8,16},{16,8},{24,0},{1,25},{9,17},{17,9},{25,1},{2,26},{10... | collective-permute-start | bytes 49160 | tf_op jit(solution)/shard_map/ppermute | solution.py:619
  12.9 0.0 collective-permute-start.2
  12.9 1.7 %shard_map.97.t0_ref = f32[32,128,128]{2,1,0:T(8,128)S(1)} custom-call(f32[96,128,128]{2,1,0:T(8,128)S(1)} %get-tuple-element.51.f_ref), custom_call_target="tpu_custom_call" | custom-call | flops 10000000000 | bytes 10000000 | tf_op jit(solution)/shard_map/pallas_call | solution.py:585
  14.6 0.0 collective-permute-done.4
  14.6 2.1 %collective-permute-done.3 = f32[4,8,128]{2,1,0:T(8,128)S(1)} collective-permute-done((f32[4,8,128]{2,1,0:T(8,128)S(1)}, f32[4,8,128]{2,1,0:T(8,128)S(1)}, u32[]{:S(2)}, u32[]{:S(2)}) %collective-permute-start.3) | collective-permute-done | bytes 16416 | tf_op jit(solution)/shard_map/ppermute | solution.py:619
  16.7 0.0 collective-permute-done.2
  16.7 0.2 collective-permute-start.5
  16.9 1.7 %shard_map.98.t1_ref = f32[32,128,128]{2,1,0:T(8,128)S(1)} custom-call(f32[96,128,128]{2,1,0:T(8,128)S(1)} %get-tuple-element.51.f_ref), custom_call_target="tpu_custom_call" | custom-call | flops 10000000000 | bytes 10000000 | tf_op jit(solution)/shard_map/pallas_call | solution.py:585
  18.6 1.9 %collective-permute-done.5 = f32[4,8,128]{2,1,0:T(8,128)S(1)} collective-permute-done((f32[4,8,128]{2,1,0:T(8,128)S(1)}, f32[4,8,128]{2,1,0:T(8,128)S(1)}, u32[]{:S(2)}, u32[]{:S(2)}) %collective-permute-start.5) | collective-permute-done | bytes 16416 | tf_op jit(solution)/shard_map/ppermute | solution.py:619
  20.6 5.8 %collective-permute-start.8 = (f32[4,8,128]{2,1,0:T(8,128)S(1)}, f32[4,8,128]{2,1,0:T(8,128)S(1)}, u32[]{:S(2)}, u32[]{:S(2)}) collective-permute-start(f32[4,8,128]{2,1,0:T(8,128)S(1)} %add.23.part0_ref), channel_id=1, source_target_pairs={{0,160},{32,128},{64,224},{96,192},{128,32},{160,0},{192,96},{224,... | collective-permute-start | bytes 49160 | tf_op jit(solution)/shard_map/ppermute | solution.py:625
  26.4 1.5 %collective-permute-start.7 = (f32[4,8,128]{2,1,0:T(8,128)S(1)}, f32[4,8,128]{2,1,0:T(8,128)S(1)}, u32[]{:S(2)}, u32[]{:S(2)}) collective-permute-start(f32[4,8,128]{2,1,0:T(8,128)S(1)} %add.23.part0_ref), channel_id=1, source_target_pairs={{0,192},{32,96},{64,0},{96,160},{128,64},{160,224},{192,128},{224,... | collective-permute-start | bytes 49160 | tf_op jit(solution)/shard_map/ppermute | solution.py:625
  27.9 1.0 %collective-permute-start.6 = (f32[4,8,128]{2,1,0:T(8,128)S(1)}, f32[4,8,128]{2,1,0:T(8,128)S(1)}, u32[]{:S(2)}, u32[]{:S(2)}) collective-permute-start(f32[4,8,128]{2,1,0:T(8,128)S(1)} %add.23.part0_ref), channel_id=1, source_target_pairs={{0,224},{32,64},{64,32},{96,128},{128,96},{160,192},{192,160},{224... | collective-permute-start | bytes 49160 | tf_op jit(solution)/shard_map/ppermute | solution.py:625
  28.9 1.7 %shard_map.99.t2_ref = f32[32,128,128]{2,1,0:T(8,128)S(1)} custom-call(f32[96,128,128]{2,1,0:T(8,128)S(1)} %get-tuple-element.51.f_ref), custom_call_target="tpu_custom_call" | custom-call | flops 10000000000 | bytes 10000000 | tf_op jit(solution)/shard_map/pallas_call | solution.py:585
  30.6 0.0 collective-permute-done.8.part3_ref
  30.6 1.7 %collective-permute-done.7.part2_ref = f32[4,8,128]{2,1,0:T(8,128)S(1)} collective-permute-done((f32[4,8,128]{2,1,0:T(8,128)S(1)}, f32[4,8,128]{2,1,0:T(8,128)S(1)}, u32[]{:S(2)}, u32[]{:S(2)}) %collective-permute-start.7) | collective-permute-done | bytes 16416 | tf_op jit(solution)/shard_map/ppermute | solution.py:625
  32.3 0.0 collective-permute-done.6.part1_ref
  32.3 0.0 collective-permute-done.9.far_ref
  32.3 0.0 collective-permute-done.10.near_ref
  32.3 4.2 %shard_map.100 = (f32[12,128]{1,0:T(8,128)}, f32[96,128,128]{2,1,0:T(8,128)}) custom-call(f32[4,8,128]{2,1,0:T(8,128)S(1)} %add.23.part0_ref, f32[4,8,128]{2,1,0:T(8,128)S(1)} %collective-permute-done.6.part1_ref, f32[4,8,128]{2,1,0:T(8,128)S(1)} %collective-permute-done.7.part2_ref, f32[4,8,128]{2,1,0:T(8,128)S(1)} %collective-permute-done.8.part3_ref, ...), custom_call_target="tpu_custom_call" | custom-call | tf_op jit(solution)/shard_map/pallas_call | solution.py:600
  (3 shorter events, 0.0 us)
Async XLA Ops:
  0.6 6.9 %copy-start = (f32[12,128]{1,0:T(8,128)S(1)}, f32[12,128]{1,0:T(8,128)}, u32[]{:S(2)}) copy-start(f32[12,128]{1,0:T(8,128)} %cover_ref.1) | copy-start | bytes 18436
  0.6 6.9 %copy-start.1 = (f32[4,2,12]{2,1,0:T(2,128)S(1)}, f32[4,2,12]{2,1,0:T(2,128)}, u32[]{:S(2)}) copy-start(f32[4,2,12]{2,1,0:T(2,128)} %rates_ref.1) | copy-start | bytes 1156
  0.7 6.9 %copy-start.2 = (s32[1,128]{1,0:T(1,128)S(1)}, s32[1,128]{1,0:T(1,128)}, u32[]{:S(2)}) copy-start(s32[1,128]{1,0:T(1,128)} %cell_ref.3) | copy-start | bytes 1540
  0.7 6.9 %copy-start.3 = (s32[12,3]{0,1:T(4,128)S(1)}, s32[12,3]{0,1:T(4,128)}, u32[]{:S(2)}) copy-start(s32[12,3]{0,1:T(4,128)} %param.13) | copy-start | bytes 436
  0.7 6.9 %copy-start.4 = (f32[4,3]{1,0:T(4,128)S(1)}, f32[4,3]{1,0:T(4,128)}, u32[]{:S(2)}) copy-start(f32[4,3]{1,0:T(4,128)} %stick_ref.1) | copy-start | bytes 148
  0.7 6.9 %copy-start.5 = (f32[128]{0:T(128)S(1)}, f32[128]{0:T(128)}, u32[]{:S(2)}) copy-start(f32[128]{0:T(128)} %param.9) | copy-start | bytes 1540
  0.7 6.9 %copy-start.6 = (s32[128]{0:T(128)S(1)}, s32[128]{0:T(128)}, u32[]{:S(2)}) copy-start(s32[128]{0:T(128)} %param.12) | copy-start | bytes 1540
  4.1 4.6 %collective-permute-start = (f32[4,8,128]{2,1,0:T(8,128)S(1)}, f32[4,8,128]{2,1,0:T(8,128)S(1)}, u32[]{:S(2)}, u32[]{:S(2)}) collective-permute-start(f32[4,8,128]{2,1,0:T(8,128)S(1)} %get-tuple-element.30), channel_id=1, source_target_pairs={{0,7},{1,2},{2,1},{3,4},{4,3},{5,6},{6,5},{7,0},{8,15},{9,10},{10,... | collective-permute-start | bytes 49160 | tf_op jit(solution)/shard_map/ppermute | solution.py:625
  6.6 2.0 %collective-permute-start.1 = (f32[4,8,128]{2,1,0:T(8,128)S(1)}, f32[4,8,128]{2,1,0:T(8,128)S(1)}, u32[]{:S(2)}, u32[]{:S(2)}) collective-permute-start(f32[4,8,128]{2,1,0:T(8,128)S(1)} %get-tuple-element.31), channel_id=1, source_target_pairs={{0,1},{1,0},{2,3},{3,2},{4,5},{5,4},{6,7},{7,6},{8,9},{9,8},{10,11... | collective-permute-start | bytes 49160 | tf_op jit(solution)/shard_map/ppermute | solution.py:619
  6.6 25.6 %collective-permute-start.9 = (f32[96,32,128]{2,1,0:T(8,128)S(1)}, f32[96,32,128]{2,1,0:T(8,128)S(1)}, u32[]{:S(2)}, u32[]{:S(2)}) collective-permute-start(f32[96,32,128]{2,1,0:T(8,128)S(1)} %get-tuple-element.47), channel_id=1, source_target_pairs={{0,7},{1,2},{2,1},{3,4},{4,3},{5,6},{6,5},{7,0},{8,15},{9,10},{10,... | collective-permute-start | bytes 4718600 | tf_op jit(solution)/shard_map/ppermute | solution.py:625
  7.5 24.8 %collective-permute-start.10 = (f32[96,32,128]{2,1,0:T(8,128)S(1)}, f32[96,32,128]{2,1,0:T(8,128)S(1)}, u32[]{:S(2)}, u32[]{:S(2)}) collective-permute-start(f32[96,32,128]{2,1,0:T(8,128)S(1)} %get-tuple-element.48), channel_id=1, source_target_pairs={{0,1},{1,0},{2,3},{3,2},{4,5},{5,4},{6,7},{7,6},{8,9},{9,8},{10,11... | collective-permute-start | bytes 4718600 | tf_op jit(solution)/shard_map/ppermute | solution.py:619
  8.7 5.9 %collective-permute-start.4 = (f32[4,8,128]{2,1,0:T(8,128)S(1)}, f32[4,8,128]{2,1,0:T(8,128)S(1)}, u32[]{:S(2)}, u32[]{:S(2)}) collective-permute-start(f32[4,8,128]{2,1,0:T(8,128)S(1)} %add_add_fusion.1), channel_id=1, source_target_pairs={{0,16},{8,24},{16,0},{24,8},{1,17},{9,25},{17,1},{25,9},{2,18},{10... | collective-permute-start | bytes 49160 | tf_op jit(solution)/shard_map/ppermute | solution.py:619
  11.8 4.9 %collective-permute-start.3 = (f32[4,8,128]{2,1,0:T(8,128)S(1)}, f32[4,8,128]{2,1,0:T(8,128)S(1)}, u32[]{:S(2)}, u32[]{:S(2)}) collective-permute-start(f32[4,8,128]{2,1,0:T(8,128)S(1)} %add_add_fusion.1), channel_id=1, source_target_pairs={{0,24},{8,16},{16,8},{24,0},{1,25},{9,17},{17,9},{25,1},{2,26},{10... | collective-permute-start | bytes 49160 | tf_op jit(solution)/shard_map/ppermute | solution.py:619
  12.9 3.8 %collective-permute-start.2 = (f32[4,8,128]{2,1,0:T(8,128)S(1)}, f32[4,8,128]{2,1,0:T(8,128)S(1)}, u32[]{:S(2)}, u32[]{:S(2)}) collective-permute-start(f32[4,8,128]{2,1,0:T(8,128)S(1)} %add_add_fusion.1), channel_id=1, source_target_pairs={{0,8},{8,0},{16,24},{24,16},{1,9},{9,1},{17,25},{25,17},{2,10},{10... | collective-permute-start | bytes 49160 | tf_op jit(solution)/shard_map/ppermute | solution.py:619
  16.7 3.8 %collective-permute-start.5 = (f32[4,8,128]{2,1,0:T(8,128)S(1)}, f32[4,8,128]{2,1,0:T(8,128)S(1)}, u32[]{:S(2)}, u32[]{:S(2)}) collective-permute-start(f32[4,8,128]{2,1,0:T(8,128)S(1)} %add_add_fusion), channel_id=1, source_target_pairs={{0,32},{32,0},{64,96},{96,64},{128,160},{160,128},{192,224},{224,1... | collective-permute-start | bytes 49160 | tf_op jit(solution)/shard_map/ppermute | solution.py:619
  20.6 10.0 %collective-permute-start.8 = (f32[4,8,128]{2,1,0:T(8,128)S(1)}, f32[4,8,128]{2,1,0:T(8,128)S(1)}, u32[]{:S(2)}, u32[]{:S(2)}) collective-permute-start(f32[4,8,128]{2,1,0:T(8,128)S(1)} %add.23.part0_ref), channel_id=1, source_target_pairs={{0,160},{32,128},{64,224},{96,192},{128,32},{160,0},{192,96},{224,... | collective-permute-start | bytes 49160 | tf_op jit(solution)/shard_map/ppermute | solution.py:625
  26.4 5.8 %collective-permute-start.7 = (f32[4,8,128]{2,1,0:T(8,128)S(1)}, f32[4,8,128]{2,1,0:T(8,128)S(1)}, u32[]{:S(2)}, u32[]{:S(2)}) collective-permute-start(f32[4,8,128]{2,1,0:T(8,128)S(1)} %add.23.part0_ref), channel_id=1, source_target_pairs={{0,192},{32,96},{64,0},{96,160},{128,64},{160,224},{192,128},{224,... | collective-permute-start | bytes 49160 | tf_op jit(solution)/shard_map/ppermute | solution.py:625
  27.9 4.4 %collective-permute-start.6 = (f32[4,8,128]{2,1,0:T(8,128)S(1)}, f32[4,8,128]{2,1,0:T(8,128)S(1)}, u32[]{:S(2)}, u32[]{:S(2)}) collective-permute-start(f32[4,8,128]{2,1,0:T(8,128)S(1)} %add.23.part0_ref), channel_id=1, source_target_pairs={{0,224},{32,64},{64,32},{96,128},{128,96},{160,192},{192,160},{224... | collective-permute-start | bytes 49160 | tf_op jit(solution)/shard_map/ppermute | solution.py:625

commit v6 on v5

--- a/solution.py
+++ b/solution.py
@@ -638,26 +638,26 @@
     together = lax.optimization_barrier
     face_row = face_cell.reshape(1, 128)
 
+    own = own + crossed(to_far, "space", 1) + paired(to_near, "space")
+    own, held = together((own, held))
+
+    far = crossed(near(far), "space", 1)
+    nigh = paired(near(nigh), "space")
+    moved0 = shift_call(0, held)
+    own = own + paired(own, "x", 1) + paired(own, "x", 2) + paired(own, "x", 3)
+    own, moved0, held = together((own, moved0, held))
+
+    moved1 = shift_call(1, held)
+    own = own + paired(own, "z")
+    own, moved1, held = together((own, moved1, held))
+
     temp, own = together((wall_temp.reshape(1, 128), own))
     walls = wall_call(
         stoichiometry.T, sticking, surface_rates, temp, coverage, face_row,
         face_owner.reshape(1, 128),
     )
-    own = own + crossed(to_far, "space", 1) + paired(to_near, "space")
-    own, held, walls = together((own, held, walls))
-
-    far = crossed(near(far), "space", 1)
-    nigh = paired(near(nigh), "space")
-    moved0 = shift_call(0, held)
-    own = own + paired(own, "x", 1) + paired(own, "x", 3) + paired(own, "x", 2)
-    own, moved0, held = together((own, moved0, held))
-
-    moved1 = shift_call(1, held)
-    own = own + paired(own, "z")
-    own, moved1, held = together((own, moved1, held))
-
     moved2 = shift_call(2, held)
-    parts = [own] + [crossed(own, "z", by) for by in (1, 2, 3)]
+    parts = [own] + [crossed(own, "z", by) for by in (1, 3, 2)]
     surface, sums, wall_x, wall_y = walls
     vmem = [near(v) for v in parts + [surface, sums]]
     covers, advanced = step_call(

time: 36.8 us -> 36.9 us (level)
  the two profiles are of different devices: /device:TPU:32 before, /device:TPU:4 now
where the time goes in v6:
time: 36.9 us; the launch traced here: 36.8 us
  starting transfers between devices  17.9 us (49%)
  Pallas kernels  13.6 us (37%)
  waiting for transfers between devices  4.55 us (12%)
  between operations  0.78 us (2%)
    ppermute x5, starting transfers between devices, crossed(): return lax.ppermute(value, axis, pairs)  11.7 us
    ppermute x6, starting transfers between devices, paired(): return lax.ppermute(value, axis, [(i, i ^ by) for i in range(peers)])  6.17 us
    pallas_call x3, Pallas kernels, shift_call(): pl.pallas_call(functools.partial(shift_kernel, s), in_specs=[VMEM], out_s...  5.05 us
    pallas_call x1, Pallas kernels, step_call(): pl.pallas_call(step_kernel, in_specs=[VMEM] * 14, out_specs=[VMEM, HBM],...  4.17 us
    pallas_call x1, Pallas kernels, moments_call(): pl.pallas_call(moments_kernel, in_specs=[HBM], out_specs=[VMEM] * 6, out_...  3.32 us
    ppermute x5, waiting for transfers between devices, crossed(): return lax.ppermute(value, axis, pairs)  3.19 us
    ppermute x6, waiting for transfers between devices, paired(): return lax.ppermute(value, axis, [(i, i ^ by) for i in range(peers)])  1.36 us
    pallas_call x1, Pallas kernels, wall_call(): pl.pallas_call(wall_kernel, in_specs=[SMEM] * 3 + [VMEM] * 4, out_specs=[...  1.04 us
  transfers between devices with their start and end apart: 11, of which 5 were waited for; matrix products, arithmetic and copies ran while one was open for 0% of the time, Pallas kernels for 17%

profile of v6, /device:TPU:4, one launch (start us, length us, event | category | flops | bytes accessed | tf_op | source)
XLA Modules:
  0.0 36.8 jit_solution(8005373560896737272)
XLA Ops:
  0.6 3.3 %shard_map.95 = (f32[4,8,128]{2,1,0:T(8,128)S(1)}, f32[4,8,128]{2,1,0:T(8,128)S(1)}, f32[4,8,128]{2,1,0:T(8,128)S(1)}, f32[96,128,128]{2,1,0:T(8,128)S(1)}, f32[...) custom-call(f32[96,128,128]{2,1,0:T(8,128)} %bitcast.16), custom_call_target="tpu_custom_call" | custom-call | tf_op jit(solution)/shard_map/pallas_call | solution.py:554
  4.0 2.5 %collective-permute-start = (f32[4,8,128]{2,1,0:T(8,128)S(1)}, f32[4,8,128]{2,1,0:T(8,128)S(1)}, u32[]{:S(2)}, u32[]{:S(2)}) collective-permute-start(f32[4,8,128]{2,1,0:T(8,128)S(1)} %get-tuple-element.25), channel_id=1, source_target_pairs={{0,7},{1,2},{2,1},{3,4},{4,3},{5,6},{6,5},{7,0},{8,15},{9,10},{10,... | collective-permute-start | bytes 49160 | tf_op jit(solution)/shard_map/ppermute | solution.py:625
  6.5 0.0 collective-permute-start.1
  6.5 0.9 %collective-permute-start.9 = (f32[96,32,128]{2,1,0:T(8,128)S(1)}, f32[96,32,128]{2,1,0:T(8,128)S(1)}, u32[]{:S(2)}, u32[]{:S(2)}) collective-permute-start(f32[96,32,128]{2,1,0:T(8,128)S(1)} %get-tuple-element.39), channel_id=1, source_target_pairs={{0,7},{1,2},{2,1},{3,4},{4,3},{5,6},{6,5},{7,0},{8,15},{9,10},{10,... | collective-permute-start | bytes 4718600 | tf_op jit(solution)/shard_map/ppermute | solution.py:625
  7.4 0.1 collective-permute-start.10
  7.4 1.0 %collective-permute-done = f32[4,8,128]{2,1,0:T(8,128)S(1)} collective-permute-done((f32[4,8,128]{2,1,0:T(8,128)S(1)}, f32[4,8,128]{2,1,0:T(8,128)S(1)}, u32[]{:S(2)}, u32[]{:S(2)}) %collective-permute-start) | collective-permute-done | bytes 16416 | tf_op jit(solution)/shard_map/ppermute | solution.py:625
  8.4 0.0 collective-permute-done.1
  8.4 0.6 %collective-permute-start.4 = (f32[4,8,128]{2,1,0:T(8,128)S(1)}, f32[4,8,128]{2,1,0:T(8,128)S(1)}, u32[]{:S(2)}, u32[]{:S(2)}) collective-permute-start(f32[4,8,128]{2,1,0:T(8,128)S(1)} %add_add_fusion.1), channel_id=1, source_target_pairs={{0,24},{8,16},{16,8},{24,0},{1,25},{9,17},{17,9},{25,1},{2,26},{10... | collective-permute-start | bytes 49160 | tf_op jit(solution)/shard_map/ppermute | solution.py:619
  9.1 2.7 %collective-permute-start.3 = (f32[4,8,128]{2,1,0:T(8,128)S(1)}, f32[4,8,128]{2,1,0:T(8,128)S(1)}, u32[]{:S(2)}, u32[]{:S(2)}) collective-permute-start(f32[4,8,128]{2,1,0:T(8,128)S(1)} %add_add_fusion.1), channel_id=1, source_target_pairs={{0,16},{8,24},{16,0},{24,8},{1,17},{9,25},{17,1},{25,9},{2,18},{10... | collective-permute-start | bytes 49160 | tf_op jit(solution)/shard_map/ppermute | solution.py:619
  11.8 0.8 %collective-permute-start.2 = (f32[4,8,128]{2,1,0:T(8,128)S(1)}, f32[4,8,128]{2,1,0:T(8,128)S(1)}, u32[]{:S(2)}, u32[]{:S(2)}) collective-permute-start(f32[4,8,128]{2,1,0:T(8,128)S(1)} %add_add_fusion.1), channel_id=1, source_target_pairs={{0,8},{8,0},{16,24},{24,16},{1,9},{9,1},{17,25},{25,17},{2,10},{10... | collective-permute-start | bytes 49160 | tf_op jit(solution)/shard_map/ppermute | solution.py:619
  12.6 1.7 %shard_map.96.t0_ref = f32[32,128,128]{2,1,0:T(8,128)S(1)} custom-call(f32[96,128,128]{2,1,0:T(8,128)S(1)} %get-tuple-element.43.f_ref), custom_call_target="tpu_custom_call" | custom-call | flops 10000000000 | bytes 10000000 | tf_op jit(solution)/shard_map/pallas_call | solution.py:585
  14.3 0.0 collective-permute-done.4
  14.3 0.0 collective-permute-done.3
  14.3 1.2 %collective-permute-done.2 = f32[4,8,128]{2,1,0:T(8,128)S(1)} collective-permute-done((f32[4,8,128]{2,1,0:T(8,128)S(1)}, f32[4,8,128]{2,1,0:T(8,128)S(1)}, u32[]{:S(2)}, u32[]{:S(2)}) %collective-permute-start.2) | collective-permute-done | bytes 16416 | tf_op jit(solution)/shard_map/ppermute | solution.py:619
  15.5 1.9 %collective-permute-start.5 = (f32[4,8,128]{2,1,0:T(8,128)S(1)}, f32[4,8,128]{2,1,0:T(8,128)S(1)}, u32[]{:S(2)}, u32[]{:S(2)}) collective-permute-start(f32[4,8,128]{2,1,0:T(8,128)S(1)} %add_add_fusion), channel_id=1, source_target_pairs={{0,32},{32,0},{64,96},{96,64},{128,160},{160,128},{192,224},{224,1... | collective-permute-start | bytes 49160 | tf_op jit(solution)/shard_map/ppermute | solution.py:619
  17.4 1.7 %shard_map.97.t1_ref = f32[32,128,128]{2,1,0:T(8,128)S(1)} custom-call(f32[96,128,128]{2,1,0:T(8,128)S(1)} %get-tuple-element.43.f_ref), custom_call_target="tpu_custom_call" | custom-call | flops 10000000000 | bytes 10000000 | tf_op jit(solution)/shard_map/pallas_call | solution.py:585
  19.1 0.1 collective-permute-done.5
  19.3 0.0 copy-start
  19.3 0.0 copy-start.1
  19.3 0.0 copy-start.2
  19.3 0.0 copy-start.3
  19.3 0.0 copy-start.4
  19.3 0.0 copy-start.5
  19.3 0.0 copy-start.6
  19.3 6.4 %collective-permute-start.8 = (f32[4,8,128]{2,1,0:T(8,128)S(1)}, f32[4,8,128]{2,1,0:T(8,128)S(1)}, u32[]{:S(2)}, u32[]{:S(2)}) collective-permute-start(f32[4,8,128]{2,1,0:T(8,128)S(1)} %add.23.part0_ref), channel_id=1, source_target_pairs={{0,192},{32,96},{64,0},{96,160},{128,64},{160,224},{192,128},{224,... | collective-permute-start | bytes 49160 | tf_op jit(solution)/shard_map/ppermute | solution.py:625
  25.7 1.9 %collective-permute-start.7 = (f32[4,8,128]{2,1,0:T(8,128)S(1)}, f32[4,8,128]{2,1,0:T(8,128)S(1)}, u32[]{:S(2)}, u32[]{:S(2)}) collective-permute-start(f32[4,8,128]{2,1,0:T(8,128)S(1)} %add.23.part0_ref), channel_id=1, source_target_pairs={{0,160},{32,128},{64,224},{96,192},{128,32},{160,0},{192,96},{224,... | collective-permute-start | bytes 49160 | tf_op jit(solution)/shard_map/ppermute | solution.py:625
  27.6 0.0 collective-permute-start.6
  27.6 1.7 %shard_map.99.t2_ref = f32[32,128,128]{2,1,0:T(8,128)S(1)} custom-call(f32[96,128,128]{2,1,0:T(8,128)S(1)} %get-tuple-element.43.f_ref), custom_call_target="tpu_custom_call" | custom-call | flops 10000000000 | bytes 10000000 | tf_op jit(solution)/shard_map/pallas_call | solution.py:585
  29.3 0.0 copy-done
  29.3 0.0 copy-done.1
  29.4 0.0 copy-done.2
  29.4 0.0 copy-done.3
  29.4 0.0 copy-done.4
  29.4 0.0 copy-done.5
  29.4 0.0 copy-done.6
  29.4 1.0 %shard_map.98 = (f32[9,16,128]{2,1,0:T(8,128)S(1)}, f32[3,8,128]{2,1,0:T(8,128)S(1)}, f32[3,2,32,128]{3,2,1,0:T(8,128)S(1)}, f32[3,2,16,128]{3,2,1,0:T(8,128)S(1)}) custom-call(s32[3,12]{1,0:T(4,128)S(1)} %bitcast.13, f32[4,3]{1,0:T(4,128)S(1)} %copy-done.4, f32[4,2,12]{2,1,0:T(2,128)S(1)} %copy-done.1, f32[1,128]{1,0:T(1,128)S(1)} %bitcast.14, ...), custom_call_target="tpu_custom_call" | custom-call | tf_op jit(solution)/shard_map/pallas_call | solution.py:570
  30.4 0.0 collective-permute-done.8.part3_ref
  30.5 2.0 %collective-permute-done.7.part2_ref = f32[4,8,128]{2,1,0:T(8,128)S(1)} collective-permute-done((f32[4,8,128]{2,1,0:T(8,128)S(1)}, f32[4,8,128]{2,1,0:T(8,128)S(1)}, u32[]{:S(2)}, u32[]{:S(2)}) %collective-permute-start.7) | collective-permute-done | bytes 16416 | tf_op jit(solution)/shard_map/ppermute | solution.py:625
  32.5 0.2 collective-permute-done.6.part1_ref
  32.6 0.0 collective-permute-done.9.far_ref
  32.6 0.0 collective-permute-done.10.near_ref
  32.7 4.2 %shard_map.100 = (f32[12,128]{1,0:T(8,128)}, f32[96,128,128]{2,1,0:T(8,128)}) custom-call(f32[4,8,128]{2,1,0:T(8,128)S(1)} %add.23.part0_ref, f32[4,8,128]{2,1,0:T(8,128)S(1)} %collective-permute-done.6.part1_ref, f32[4,8,128]{2,1,0:T(8,128)S(1)} %collective-permute-done.7.part2_ref, f32[4,8,128]{2,1,0:T(8,128)S(1)} %collective-permute-done.8.part3_ref, ...), custom_call_target="tpu_custom_call" | custom-call | tf_op jit(solution)/shard_map/pallas_call | solution.py:600
  (3 shorter events, 0.0 us)
Async XLA Ops:
  4.0 4.5 %collective-permute-start = (f32[4,8,128]{2,1,0:T(8,128)S(1)}, f32[4,8,128]{2,1,0:T(8,128)S(1)}, u32[]{:S(2)}, u32[]{:S(2)}) collective-permute-start(f32[4,8,128]{2,1,0:T(8,128)S(1)} %get-tuple-element.25), channel_id=1, source_target_pairs={{0,7},{1,2},{2,1},{3,4},{4,3},{5,6},{6,5},{7,0},{8,15},{9,10},{10,... | collective-permute-start | bytes 49160 | tf_op jit(solution)/shard_map/ppermute | solution.py:625
  6.5 1.9 %collective-permute-start.1 = (f32[4,8,128]{2,1,0:T(8,128)S(1)}, f32[4,8,128]{2,1,0:T(8,128)S(1)}, u32[]{:S(2)}, u32[]{:S(2)}) collective-permute-start(f32[4,8,128]{2,1,0:T(8,128)S(1)} %get-tuple-element.26), channel_id=1, source_target_pairs={{0,1},{1,0},{2,3},{3,2},{4,5},{5,4},{6,7},{7,6},{8,9},{9,8},{10,11... | collective-permute-start | bytes 49160 | tf_op jit(solution)/shard_map/ppermute | solution.py:619
  6.5 26.1 %collective-permute-start.9 = (f32[96,32,128]{2,1,0:T(8,128)S(1)}, f32[96,32,128]{2,1,0:T(8,128)S(1)}, u32[]{:S(2)}, u32[]{:S(2)}) collective-permute-start(f32[96,32,128]{2,1,0:T(8,128)S(1)} %get-tuple-element.39), channel_id=1, source_target_pairs={{0,7},{1,2},{2,1},{3,4},{4,3},{5,6},{6,5},{7,0},{8,15},{9,10},{10,... | collective-permute-start | bytes 4718600 | tf_op jit(solution)/shard_map/ppermute | solution.py:625
  7.4 25.3 %collective-permute-start.10 = (f32[96,32,128]{2,1,0:T(8,128)S(1)}, f32[96,32,128]{2,1,0:T(8,128)S(1)}, u32[]{:S(2)}, u32[]{:S(2)}) collective-permute-start(f32[96,32,128]{2,1,0:T(8,128)S(1)} %get-tuple-element.40), channel_id=1, source_target_pairs={{0,1},{1,0},{2,3},{3,2},{4,5},{5,4},{6,7},{7,6},{8,9},{9,8},{10,11... | collective-permute-start | bytes 4718600 | tf_op jit(solution)/shard_map/ppermute | solution.py:619
  8.4 5.9 %collective-permute-start.4 = (f32[4,8,128]{2,1,0:T(8,128)S(1)}, f32[4,8,128]{2,1,0:T(8,128)S(1)}, u32[]{:S(2)}, u32[]{:S(2)}) collective-permute-start(f32[4,8,128]{2,1,0:T(8,128)S(1)} %add_add_fusion.1), channel_id=1, source_target_pairs={{0,24},{8,16},{16,8},{24,0},{1,25},{9,17},{17,9},{25,1},{2,26},{10... | collective-permute-start | bytes 49160 | tf_op jit(solution)/shard_map/ppermute | solution.py:619
  9.1 5.3 %collective-permute-start.3 = (f32[4,8,128]{2,1,0:T(8,128)S(1)}, f32[4,8,128]{2,1,0:T(8,128)S(1)}, u32[]{:S(2)}, u32[]{:S(2)}) collective-permute-start(f32[4,8,128]{2,1,0:T(8,128)S(1)} %add_add_fusion.1), channel_id=1, source_target_pairs={{0,16},{8,24},{16,0},{24,8},{1,17},{9,25},{17,1},{25,9},{2,18},{10... | collective-permute-start | bytes 49160 | tf_op jit(solution)/shard_map/ppermute | solution.py:619
  11.8 3.7 %collective-permute-start.2 = (f32[4,8,128]{2,1,0:T(8,128)S(1)}, f32[4,8,128]{2,1,0:T(8,128)S(1)}, u32[]{:S(2)}, u32[]{:S(2)}) collective-permute-start(f32[4,8,128]{2,1,0:T(8,128)S(1)} %add_add_fusion.1), channel_id=1, source_target_pairs={{0,8},{8,0},{16,24},{24,16},{1,9},{9,1},{17,25},{25,17},{2,10},{10... | collective-permute-start | bytes 49160 | tf_op jit(solution)/shard_map/ppermute | solution.py:619
  15.5 3.7 %collective-permute-start.5 = (f32[4,8,128]{2,1,0:T(8,128)S(1)}, f32[4,8,128]{2,1,0:T(8,128)S(1)}, u32[]{:S(2)}, u32[]{:S(2)}) collective-permute-start(f32[4,8,128]{2,1,0:T(8,128)S(1)} %add_add_fusion), channel_id=1, source_target_pairs={{0,32},{32,0},{64,96},{96,64},{128,160},{160,128},{192,224},{224,1... | collective-permute-start | bytes 49160 | tf_op jit(solution)/shard_map/ppermute | solution.py:619
  19.3 10.1 %copy-start = (f32[12,128]{1,0:T(8,128)S(1)}, f32[12,128]{1,0:T(8,128)}, u32[]{:S(2)}) copy-start(f32[12,128]{1,0:T(8,128)} %cover_ref.1) | copy-start | bytes 18436
  19.3 10.1 %copy-start.1 = (f32[4,2,12]{2,1,0:T(2,128)S(1)}, f32[4,2,12]{2,1,0:T(2,128)}, u32[]{:S(2)}) copy-start(f32[4,2,12]{2,1,0:T(2,128)} %rates_ref.1) | copy-start | bytes 1156
  19.3 10.1 %copy-start.2 = (s32[1,128]{1,0:T(1,128)S(1)}, s32[1,128]{1,0:T(1,128)}, u32[]{:S(2)}) copy-start(s32[1,128]{1,0:T(1,128)} %cell_ref.3) | copy-start | bytes 1540
  19.3 10.1 %copy-start.3 = (s32[12,3]{0,1:T(4,128)S(1)}, s32[12,3]{0,1:T(4,128)}, u32[]{:S(2)}) copy-start(s32[12,3]{0,1:T(4,128)} %param.13) | copy-start | bytes 436
  19.3 10.1 %copy-start.4 = (f32[4,3]{1,0:T(4,128)S(1)}, f32[4,3]{1,0:T(4,128)}, u32[]{:S(2)}) copy-start(f32[4,3]{1,0:T(4,128)} %stick_ref.1) | copy-start | bytes 148
  19.3 10.1 %copy-start.5 = (f32[128]{0:T(128)S(1)}, f32[128]{0:T(128)}, u32[]{:S(2)}) copy-start(f32[128]{0:T(128)} %param.9) | copy-start | bytes 1540
  19.3 10.1 %copy-start.6 = (s32[128]{0:T(128)S(1)}, s32[128]{0:T(128)}, u32[]{:S(2)}) copy-start(s32[128]{0:T(128)} %param.12) | copy-start | bytes 1540
  19.3 11.1 %collective-permute-start.8 = (f32[4,8,128]{2,1,0:T(8,128)S(1)}, f32[4,8,128]{2,1,0:T(8,128)S(1)}, u32[]{:S(2)}, u32[]{:S(2)}) collective-permute-start(f32[4,8,128]{2,1,0:T(8,128)S(1)} %add.23.part0_ref), channel_id=1, source_target_pairs={{0,192},{32,96},{64,0},{96,160},{128,64},{160,224},{192,128},{224,... | collective-permute-start | bytes 49160 | tf_op jit(solution)/shard_map/ppermute | solution.py:625
  25.7 6.7 %collective-permute-start.7 = (f32[4,8,128]{2,1,0:T(8,128)S(1)}, f32[4,8,128]{2,1,0:T(8,128)S(1)}, u32[]{:S(2)}, u32[]{:S(2)}) collective-permute-start(f32[4,8,128]{2,1,0:T(8,128)S(1)} %add.23.part0_ref), channel_id=1, source_target_pairs={{0,160},{32,128},{64,224},{96,192},{128,32},{160,0},{192,96},{224,... | collective-permute-start | bytes 49160 | tf_op jit(solution)/shard_map/ppermute | solution.py:625
  27.6 5.0 %collective-permute-start.6 = (f32[4,8,128]{2,1,0:T(8,128)S(1)}, f32[4,8,128]{2,1,0:T(8,128)S(1)}, u32[]{:S(2)}, u32[]{:S(2)}) collective-permute-start(f32[4,8,128]{2,1,0:T(8,128)S(1)} %add.23.part0_ref), channel_id=1, source_target_pairs={{0,224},{32,64},{64,32},{96,128},{128,96},{160,192},{192,160},{224... | collective-permute-start | bytes 49160 | tf_op jit(solution)/shard_map/ppermute | solution.py:625

commit v7 on v6

--- a/solution.py
+++ b/solution.py
@@ -644,20 +644,20 @@
     far = crossed(near(far), "space", 1)
     nigh = paired(near(nigh), "space")
     moved0 = shift_call(0, held)
-    own = own + paired(own, "x", 1) + paired(own, "x", 2) + paired(own, "x", 3)
+    own = own + paired(own, "x", 1) + paired(own, "x", 3) + paired(own, "x", 2)
     own, moved0, held = together((own, moved0, held))
-
-    moved1 = shift_call(1, held)
-    own = own + paired(own, "z")
-    own, moved1, held = together((own, moved1, held))
 
     temp, own = together((wall_temp.reshape(1, 128), own))
     walls = wall_call(
         stoichiometry.T, sticking, surface_rates, temp, coverage, face_row,
         face_owner.reshape(1, 128),
     )
+    moved1 = shift_call(1, held)
+    own = own + paired(own, "z")
+    own, moved1, held, walls = together((own, moved1, held, walls))
+
     moved2 = shift_call(2, held)
-    parts = [own] + [crossed(own, "z", by) for by in (1, 3, 2)]
+    parts = [own] + [crossed(own, "z", by) for by in (1, 2, 3)]
     surface, sums, wall_x, wall_y = walls
     vmem = [near(v) for v in parts + [surface, sums]]
     covers, advanced = step_call(

time: 36.9 us -> 36.6 us (level)
  the two profiles are of different devices: /device:TPU:4 before, /device:TPU:32 now
where the time goes in v7:
time: 36.6 us; the launch traced here: 36.5 us
  starting transfers between devices  16.4 us (45%)
  Pallas kernels  13.6 us (37%)
  waiting for transfers between devices  5.63 us (15%)
  between operations  0.8 us (2%)
    ppermute x5, starting transfers between devices, crossed(): return lax.ppermute(value, axis, pairs)  11.9 us
    pallas_call x3, Pallas kernels, shift_call(): pl.pallas_call(functools.partial(shift_kernel, s), in_specs=[VMEM], out_s...  5.05 us
    ppermute x6, starting transfers between devices, paired(): return lax.ppermute(value, axis, [(i, i ^ by) for i in range(peers)])  4.52 us
    pallas_call x1, Pallas kernels, step_call(): pl.pallas_call(step_kernel, in_specs=[VMEM] * 14, out_specs=[VMEM, HBM],...  4.17 us
    pallas_call x1, Pallas kernels, moments_call(): pl.pallas_call(moments_kernel, in_specs=[HBM], out_specs=[VMEM] * 6, out_...  3.32 us
    ppermute x6, waiting for transfers between devices, paired(): return lax.ppermute(value, axis, [(i, i ^ by) for i in range(peers)])  2.96 us
    ppermute x5, waiting for transfers between devices, crossed(): return lax.ppermute(value, axis, pairs)  2.67 us
    pallas_call x1, Pallas kernels, wall_call(): pl.pallas_call(wall_kernel, in_specs=[SMEM] * 3 + [VMEM] * 4, out_specs=[...  1.04 us
  transfers between devices with their start and end apart: 11, of which 4 were waited for; matrix products, arithmetic and copies ran while one was open for 0% of the time, Pallas kernels for 17%

profile of v7, /device:TPU:32, one launch (start us, length us, event | category | flops | bytes accessed | tf_op | source)
XLA Modules:
  0.0 36.5 jit_solution(17042975214003779596)
XLA Ops:
  0.6 3.3 %shard_map.95 = (f32[4,8,128]{2,1,0:T(8,128)S(1)}, f32[4,8,128]{2,1,0:T(8,128)S(1)}, f32[4,8,128]{2,1,0:T(8,128)S(1)}, f32[96,128,128]{2,1,0:T(8,128)S(1)}, f32[...) custom-call(f32[96,128,128]{2,1,0:T(8,128)} %bitcast.16), custom_call_target="tpu_custom_call" | custom-call | tf_op jit(solution)/shard_map/pallas_call | solution.py:554
  4.0 2.5 %collective-permute-start = (f32[4,8,128]{2,1,0:T(8,128)S(1)}, f32[4,8,128]{2,1,0:T(8,128)S(1)}, u32[]{:S(2)}, u32[]{:S(2)}) collective-permute-start(f32[4,8,128]{2,1,0:T(8,128)S(1)} %get-tuple-element.29), channel_id=1, source_target_pairs={{0,7},{1,2},{2,1},{3,4},{4,3},{5,6},{6,5},{7,0},{8,15},{9,10},{10,... | collective-permute-start | bytes 49160 | tf_op jit(solution)/shard_map/ppermute | solution.py:625
  6.5 0.0 collective-permute-start.1
  6.5 0.9 %collective-permute-start.9 = (f32[96,32,128]{2,1,0:T(8,128)S(1)}, f32[96,32,128]{2,1,0:T(8,128)S(1)}, u32[]{:S(2)}, u32[]{:S(2)}) collective-permute-start(f32[96,32,128]{2,1,0:T(8,128)S(1)} %get-tuple-element.47), channel_id=1, source_target_pairs={{0,7},{1,2},{2,1},{3,4},{4,3},{5,6},{6,5},{7,0},{8,15},{9,10},{10,... | collective-permute-start | bytes 4718600 | tf_op jit(solution)/shard_map/ppermute | solution.py:625
  7.4 0.1 collective-permute-start.10
  7.4 1.0 %collective-permute-done = f32[4,8,128]{2,1,0:T(8,128)S(1)} collective-permute-done((f32[4,8,128]{2,1,0:T(8,128)S(1)}, f32[4,8,128]{2,1,0:T(8,128)S(1)}, u32[]{:S(2)}, u32[]{:S(2)}) %collective-permute-start) | collective-permute-done | bytes 16416 | tf_op jit(solution)/shard_map/ppermute | solution.py:625
  8.4 0.0 collective-permute-done.1
  8.4 3.1 %collective-permute-start.4 = (f32[4,8,128]{2,1,0:T(8,128)S(1)}, f32[4,8,128]{2,1,0:T(8,128)S(1)}, u32[]{:S(2)}, u32[]{:S(2)}) collective-permute-start(f32[4,8,128]{2,1,0:T(8,128)S(1)} %add_add_fusion.1), channel_id=1, source_target_pairs={{0,16},{8,24},{16,0},{24,8},{1,17},{9,25},{17,1},{25,9},{2,18},{10... | collective-permute-start | bytes 49160 | tf_op jit(solution)/shard_map/ppermute | solution.py:619
  11.5 1.1 %collective-permute-start.3 = (f32[4,8,128]{2,1,0:T(8,128)S(1)}, f32[4,8,128]{2,1,0:T(8,128)S(1)}, u32[]{:S(2)}, u32[]{:S(2)}) collective-permute-start(f32[4,8,128]{2,1,0:T(8,128)S(1)} %add_add_fusion.1), channel_id=1, source_target_pairs={{0,24},{8,16},{16,8},{24,0},{1,25},{9,17},{17,9},{25,1},{2,26},{10... | collective-permute-start | bytes 49160 | tf_op jit(solution)/shard_map/ppermute | solution.py:619
  12.7 0.0 collective-permute-start.2
  12.7 1.7 %shard_map.96.t0_ref = f32[32,128,128]{2,1,0:T(8,128)S(1)} custom-call(f32[96,128,128]{2,1,0:T(8,128)S(1)} %get-tuple-element.51.f_ref), custom_call_target="tpu_custom_call" | custom-call | flops 10000000000 | bytes 10000000 | tf_op jit(solution)/shard_map/pallas_call | solution.py:585
  14.4 0.0 collective-permute-done.4
  14.4 2.1 %collective-permute-done.3 = f32[4,8,128]{2,1,0:T(8,128)S(1)} collective-permute-done((f32[4,8,128]{2,1,0:T(8,128)S(1)}, f32[4,8,128]{2,1,0:T(8,128)S(1)}, u32[]{:S(2)}, u32[]{:S(2)}) %collective-permute-start.3) | collective-permute-done | bytes 16416 | tf_op jit(solution)/shard_map/ppermute | solution.py:619
  16.5 0.0 collective-permute-done.2
  16.5 0.0 copy-start
  16.5 0.0 copy-start.1
  16.5 0.0 copy-start.2
  16.5 0.0 copy-start.3
  16.6 0.0 copy-start.4
  16.6 0.0 copy-start.5
  16.6 0.0 copy-start.6
  16.6 0.2 collective-permute-start.5
  16.8 1.7 %shard_map.97.t1_ref = f32[32,128,128]{2,1,0:T(8,128)S(1)} custom-call(f32[96,128,128]{2,1,0:T(8,128)S(1)} %get-tuple-element.51.f_ref), custom_call_target="tpu_custom_call" | custom-call | flops 10000000000 | bytes 10000000 | tf_op jit(solution)/shard_map/pallas_call | solution.py:585
  18.5 0.0 copy-done
  18.5 0.0 copy-done.1
  18.5 0.0 copy-done.2
  18.5 0.0 copy-done.3
  18.5 0.0 copy-done.4
  18.5 0.0 copy-done.5
  18.5 0.0 copy-done.6
  18.5 1.0 %shard_map.98 = (f32[9,16,128]{2,1,0:T(8,128)S(1)}, f32[3,8,128]{2,1,0:T(8,128)S(1)}, f32[3,2,32,128]{3,2,1,0:T(8,128)S(1)}, f32[3,2,16,128]{3,2,1,0:T(8,128)S(1)}) custom-call(s32[3,12]{1,0:T(4,128)S(1)} %bitcast.13, f32[4,3]{1,0:T(4,128)S(1)} %copy-done.4, f32[4,2,12]{2,1,0:T(2,128)S(1)} %copy-done.1, f32[1,128]{1,0:T(1,128)S(1)} %bitcast.14, ...), custom_call_target="tpu_custom_call" | custom-call | tf_op jit(solution)/shard_map/pallas_call | solution.py:570
  19.6 0.8 %collective-permute-done.5 = f32[4,8,128]{2,1,0:T(8,128)S(1)} collective-permute-done((f32[4,8,128]{2,1,0:T(8,128)S(1)}, f32[4,8,128]{2,1,0:T(8,128)S(1)}, u32[]{:S(2)}, u32[]{:S(2)}) %collective-permute-start.5) | collective-permute-done | bytes 16416 | tf_op jit(solution)/shard_map/ppermute | solution.py:619
  20.4 6.0 %collective-permute-start.8 = (f32[4,8,128]{2,1,0:T(8,128)S(1)}, f32[4,8,128]{2,1,0:T(8,128)S(1)}, u32[]{:S(2)}, u32[]{:S(2)}) collective-permute-start(f32[4,8,128]{2,1,0:T(8,128)S(1)} %add.23.part0_ref), channel_id=1, source_target_pairs={{0,160},{32,128},{64,224},{96,192},{128,32},{160,0},{192,96},{224,... | collective-permute-start | bytes 49160 | tf_op jit(solution)/shard_map/ppermute | solution.py:625
  26.4 1.5 %collective-permute-start.7 = (f32[4,8,128]{2,1,0:T(8,128)S(1)}, f32[4,8,128]{2,1,0:T(8,128)S(1)}, u32[]{:S(2)}, u32[]{:S(2)}) collective-permute-start(f32[4,8,128]{2,1,0:T(8,128)S(1)} %add.23.part0_ref), channel_id=1, source_target_pairs={{0,192},{32,96},{64,0},{96,160},{128,64},{160,224},{192,128},{224,... | collective-permute-start | bytes 49160 | tf_op jit(solution)/shard_map/ppermute | solution.py:625
  27.9 1.0 %collective-permute-start.6 = (f32[4,8,128]{2,1,0:T(8,128)S(1)}, f32[4,8,128]{2,1,0:T(8,128)S(1)}, u32[]{:S(2)}, u32[]{:S(2)}) collective-permute-start(f32[4,8,128]{2,1,0:T(8,128)S(1)} %add.23.part0_ref), channel_id=1, source_target_pairs={{0,224},{32,64},{64,32},{96,128},{128,96},{160,192},{192,160},{224... | collective-permute-start | bytes 49160 | tf_op jit(solution)/shard_map/ppermute | solution.py:625
  28.9 1.7 %shard_map.99.t2_ref = f32[32,128,128]{2,1,0:T(8,128)S(1)} custom-call(f32[96,128,128]{2,1,0:T(8,128)S(1)} %get-tuple-element.51.f_ref), custom_call_target="tpu_custom_call" | custom-call | flops 10000000000 | bytes 10000000 | tf_op jit(solution)/shard_map/pallas_call | solution.py:585
  30.6 0.0 collective-permute-done.8.part3_ref
  30.6 1.7 %collective-permute-done.7.part2_ref = f32[4,8,128]{2,1,0:T(8,128)S(1)} collective-permute-done((f32[4,8,128]{2,1,0:T(8,128)S(1)}, f32[4,8,128]{2,1,0:T(8,128)S(1)}, u32[]{:S(2)}, u32[]{:S(2)}) %collective-permute-start.7) | collective-permute-done | bytes 16416 | tf_op jit(solution)/shard_map/ppermute | solution.py:625
  32.3 0.0 collective-permute-done.6.part1_ref
  32.3 0.0 collective-permute-done.9.far_ref
  32.3 0.0 collective-permute-done.10.near_ref
  32.3 4.2 %shard_map.100 = (f32[12,128]{1,0:T(8,128)}, f32[96,128,128]{2,1,0:T(8,128)}) custom-call(f32[4,8,128]{2,1,0:T(8,128)S(1)} %add.23.part0_ref, f32[4,8,128]{2,1,0:T(8,128)S(1)} %collective-permute-done.6.part1_ref, f32[4,8,128]{2,1,0:T(8,128)S(1)} %collective-permute-done.7.part2_ref, f32[4,8,128]{2,1,0:T(8,128)S(1)} %collective-permute-done.8.part3_ref, ...), custom_call_target="tpu_custom_call" | custom-call | tf_op jit(solution)/shard_map/pallas_call | solution.py:600
  (3 shorter events, 0.0 us)
Async XLA Ops:
  4.0 4.5 %collective-permute-start = (f32[4,8,128]{2,1,0:T(8,128)S(1)}, f32[4,8,128]{2,1,0:T(8,128)S(1)}, u32[]{:S(2)}, u32[]{:S(2)}) collective-permute-start(f32[4,8,128]{2,1,0:T(8,128)S(1)} %get-tuple-element.29), channel_id=1, source_target_pairs={{0,7},{1,2},{2,1},{3,4},{4,3},{5,6},{6,5},{7,0},{8,15},{9,10},{10,... | collective-permute-start | bytes 49160 | tf_op jit(solution)/shard_map/ppermute | solution.py:625
  6.5 1.9 %collective-permute-start.1 = (f32[4,8,128]{2,1,0:T(8,128)S(1)}, f32[4,8,128]{2,1,0:T(8,128)S(1)}, u32[]{:S(2)}, u32[]{:S(2)}) collective-permute-start(f32[4,8,128]{2,1,0:T(8,128)S(1)} %get-tuple-element.30), channel_id=1, source_target_pairs={{0,1},{1,0},{2,3},{3,2},{4,5},{5,4},{6,7},{7,6},{8,9},{9,8},{10,11... | collective-permute-start | bytes 49160 | tf_op jit(solution)/shard_map/ppermute | solution.py:619
  6.5 25.8 %collective-permute-start.9 = (f32[96,32,128]{2,1,0:T(8,128)S(1)}, f32[96,32,128]{2,1,0:T(8,128)S(1)}, u32[]{:S(2)}, u32[]{:S(2)}) collective-permute-start(f32[96,32,128]{2,1,0:T(8,128)S(1)} %get-tuple-element.47), channel_id=1, source_target_pairs={{0,7},{1,2},{2,1},{3,4},{4,3},{5,6},{6,5},{7,0},{8,15},{9,10},{10,... | collective-permute-start | bytes 4718600 | tf_op jit(solution)/shard_map/ppermute | solution.py:625
  7.4 24.9 %collective-permute-start.10 = (f32[96,32,128]{2,1,0:T(8,128)S(1)}, f32[96,32,128]{2,1,0:T(8,128)S(1)}, u32[]{:S(2)}, u32[]{:S(2)}) collective-permute-start(f32[96,32,128]{2,1,0:T(8,128)S(1)} %get-tuple-element.48), channel_id=1, source_target_pairs={{0,1},{1,0},{2,3},{3,2},{4,5},{5,4},{6,7},{7,6},{8,9},{9,8},{10,11... | collective-permute-start | bytes 4718600 | tf_op jit(solution)/shard_map/ppermute | solution.py:619
  8.4 5.9 %collective-permute-start.4 = (f32[4,8,128]{2,1,0:T(8,128)S(1)}, f32[4,8,128]{2,1,0:T(8,128)S(1)}, u32[]{:S(2)}, u32[]{:S(2)}) collective-permute-start(f32[4,8,128]{2,1,0:T(8,128)S(1)} %add_add_fusion.1), channel_id=1, source_target_pairs={{0,16},{8,24},{16,0},{24,8},{1,17},{9,25},{17,1},{25,9},{2,18},{10... | collective-permute-start | bytes 49160 | tf_op jit(solution)/shard_map/ppermute | solution.py:619
  11.5 4.9 %collective-permute-start.3 = (f32[4,8,128]{2,1,0:T(8,128)S(1)}, f32[4,8,128]{2,1,0:T(8,128)S(1)}, u32[]{:S(2)}, u32[]{:S(2)}) collective-permute-start(f32[4,8,128]{2,1,0:T(8,128)S(1)} %add_add_fusion.1), channel_id=1, source_target_pairs={{0,24},{8,16},{16,8},{24,0},{1,25},{9,17},{17,9},{25,1},{2,26},{10... | collective-permute-start | bytes 49160 | tf_op jit(solution)/shard_map/ppermute | solution.py:619
  12.7 3.8 %collective-permute-start.2 = (f32[4,8,128]{2,1,0:T(8,128)S(1)}, f32[4,8,128]{2,1,0:T(8,128)S(1)}, u32[]{:S(2)}, u32[]{:S(2)}) collective-permute-start(f32[4,8,128]{2,1,0:T(8,128)S(1)} %add_add_fusion.1), channel_id=1, source_target_pairs={{0,8},{8,0},{16,24},{24,16},{1,9},{9,1},{17,25},{25,17},{2,10},{10... | collective-permute-start | bytes 49160 | tf_op jit(solution)/shard_map/ppermute | solution.py:619
  16.5 2.0 %copy-start = (f32[12,128]{1,0:T(8,128)S(1)}, f32[12,128]{1,0:T(8,128)}, u32[]{:S(2)}) copy-start(f32[12,128]{1,0:T(8,128)} %cover_ref.1) | copy-start | bytes 18436
  16.5 2.0 %copy-start.1 = (f32[4,2,12]{2,1,0:T(2,128)S(1)}, f32[4,2,12]{2,1,0:T(2,128)}, u32[]{:S(2)}) copy-start(f32[4,2,12]{2,1,0:T(2,128)} %rates_ref.1) | copy-start | bytes 1156
  16.5 2.0 %copy-start.2 = (s32[1,128]{1,0:T(1,128)S(1)}, s32[1,128]{1,0:T(1,128)}, u32[]{:S(2)}) copy-start(s32[1,128]{1,0:T(1,128)} %cell_ref.3) | copy-start | bytes 1540
  16.5 2.0 %copy-start.3 = (s32[12,3]{0,1:T(4,128)S(1)}, s32[12,3]{0,1:T(4,128)}, u32[]{:S(2)}) copy-start(s32[12,3]{0,1:T(4,128)} %param.13) | copy-start | bytes 436
  16.6 2.0 %copy-start.4 = (f32[4,3]{1,0:T(4,128)S(1)}, f32[4,3]{1,0:T(4,128)}, u32[]{:S(2)}) copy-start(f32[4,3]{1,0:T(4,128)} %stick_ref.1) | copy-start | bytes 148
  16.6 2.0 %copy-start.5 = (f32[128]{0:T(128)S(1)}, f32[128]{0:T(128)}, u32[]{:S(2)}) copy-start(f32[128]{0:T(128)} %param.9) | copy-start | bytes 1540
  16.6 2.0 %copy-start.6 = (s32[128]{0:T(128)S(1)}, s32[128]{0:T(128)}, u32[]{:S(2)}) copy-start(s32[128]{0:T(128)} %param.12) | copy-start | bytes 1540
  16.6 3.8 %collective-permute-start.5 = (f32[4,8,128]{2,1,0:T(8,128)S(1)}, f32[4,8,128]{2,1,0:T(8,128)S(1)}, u32[]{:S(2)}, u32[]{:S(2)}) collective-permute-start(f32[4,8,128]{2,1,0:T(8,128)S(1)} %add_add_fusion), channel_id=1, source_target_pairs={{0,32},{32,0},{64,96},{96,64},{128,160},{160,128},{192,224},{224,1... | collective-permute-start | bytes 49160 | tf_op jit(solution)/shard_map/ppermute | solution.py:619
  20.4 10.2 %collective-permute-start.8 = (f32[4,8,128]{2,1,0:T(8,128)S(1)}, f32[4,8,128]{2,1,0:T(8,128)S(1)}, u32[]{:S(2)}, u32[]{:S(2)}) collective-permute-start(f32[4,8,128]{2,1,0:T(8,128)S(1)} %add.23.part0_ref), channel_id=1, source_target_pairs={{0,160},{32,128},{64,224},{96,192},{128,32},{160,0},{192,96},{224,... | collective-permute-start | bytes 49160 | tf_op jit(solution)/shard_map/ppermute | solution.py:625
  26.4 5.8 %collective-permute-start.7 = (f32[4,8,128]{2,1,0:T(8,128)S(1)}, f32[4,8,128]{2,1,0:T(8,128)S(1)}, u32[]{:S(2)}, u32[]{:S(2)}) collective-permute-start(f32[4,8,128]{2,1,0:T(8,128)S(1)} %add.23.part0_ref), channel_id=1, source_target_pairs={{0,192},{32,96},{64,0},{96,160},{128,64},{160,224},{192,128},{224,... | collective-permute-start | bytes 49160 | tf_op jit(solution)/shard_map/ppermute | solution.py:625
  27.9 4.4 %collective-permute-start.6 = (f32[4,8,128]{2,1,0:T(8,128)S(1)}, f32[4,8,128]{2,1,0:T(8,128)S(1)}, u32[]{:S(2)}, u32[]{:S(2)}) collective-permute-start(f32[4,8,128]{2,1,0:T(8,128)S(1)} %add.23.part0_ref), channel_id=1, source_target_pairs={{0,224},{32,64},{64,32},{96,128},{128,96},{160,192},{192,160},{224... | collective-permute-start | bytes 49160 | tf_op jit(solution)/shard_map/ppermute | solution.py:625

commit v8 on v7

--- a/solution.py
+++ b/solution.py
@@ -657,7 +657,7 @@
     own, moved1, held, walls = together((own, moved1, held, walls))
 
     moved2 = shift_call(2, held)
-    parts = [own] + [crossed(own, "z", by) for by in (1, 2, 3)]
+    parts = [own] + [crossed(own, "z", by) for by in (1, 3, 2)]
     surface, sums, wall_x, wall_y = walls
     vmem = [near(v) for v in parts + [surface, sums]]
     covers, advanced = step_call(

time: 36.6 us -> 37.3 us (1.019)
  the two profiles are of different devices: /device:TPU:32 before, /device:TPU:6 now
where the time goes in v8:
time: 37.3 us; the launch traced here: 37.2 us
  starting transfers between devices  16.5 us (44%)
  Pallas kernels  13.6 us (36%)
  waiting for transfers between devices  6.37 us (17%)
  between operations  0.8 us (2%)
    ppermute x5, starting transfers between devices, crossed(): return lax.ppermute(value, axis, pairs)  10.8 us
    ppermute x6, starting transfers between devices, paired(): return lax.ppermute(value, axis, [(i, i ^ by) for i in range(peers)])  5.67 us
    pallas_call x3, Pallas kernels, shift_call(): pl.pallas_call(functools.partial(shift_kernel, s), in_specs=[VMEM], out_s...  5.05 us
    ppermute x5, waiting for transfers between devices, crossed(): return lax.ppermute(value, axis, pairs)  4.31 us
    pallas_call x1, Pallas kernels, step_call(): pl.pallas_call(step_kernel, in_specs=[VMEM] * 14, out_specs=[VMEM, HBM],...  4.17 us
    pallas_call x1, Pallas kernels, moments_call(): pl.pallas_call(moments_kernel, in_specs=[HBM], out_specs=[VMEM] * 6, out_...  3.32 us
    ppermute x6, waiting for transfers between devices, paired(): return lax.ppermute(value, axis, [(i, i ^ by) for i in range(peers)])  2.06 us
    pallas_call x1, Pallas kernels, wall_call(): pl.pallas_call(wall_kernel, in_specs=[SMEM] * 3 + [VMEM] * 4, out_specs=[...  1.04 us
  transfers between devices with their start and end apart: 11, of which 6 were waited for; matrix products, arithmetic and copies ran while one was open for 0% of the time, Pallas kernels for 16%

profile of v8, /device:TPU:6, one launch (start us, length us, event | category | flops | bytes accessed | tf_op | source)
XLA Modules:
  0.0 37.2 jit_solution(13984580576773186978)
XLA Ops:
  0.6 3.3 %shard_map.95 = (f32[4,8,128]{2,1,0:T(8,128)S(1)}, f32[4,8,128]{2,1,0:T(8,128)S(1)}, f32[4,8,128]{2,1,0:T(8,128)S(1)}, f32[96,128,128]{2,1,0:T(8,128)S(1)}, f32[...) custom-call(f32[96,128,128]{2,1,0:T(8,128)} %bitcast.16), custom_call_target="tpu_custom_call" | custom-call | tf_op jit(solution)/shard_map/pallas_call | solution.py:554
  4.0 2.5 %collective-permute-start = (f32[4,8,128]{2,1,0:T(8,128)S(1)}, f32[4,8,128]{2,1,0:T(8,128)S(1)}, u32[]{:S(2)}, u32[]{:S(2)}) collective-permute-start(f32[4,8,128]{2,1,0:T(8,128)S(1)} %get-tuple-element.29), channel_id=1, source_target_pairs={{0,7},{1,2},{2,1},{3,4},{4,3},{5,6},{6,5},{7,0},{8,15},{9,10},{10,... | collective-permute-start | bytes 49160 | tf_op jit(solution)/shard_map/ppermute | solution.py:625
  6.5 0.0 collective-permute-start.1
  6.5 0.9 %collective-permute-start.9 = (f32[96,32,128]{2,1,0:T(8,128)S(1)}, f32[96,32,128]{2,1,0:T(8,128)S(1)}, u32[]{:S(2)}, u32[]{:S(2)}) collective-permute-start(f32[96,32,128]{2,1,0:T(8,128)S(1)} %get-tuple-element.47), channel_id=1, source_target_pairs={{0,7},{1,2},{2,1},{3,4},{4,3},{5,6},{6,5},{7,0},{8,15},{9,10},{10,... | collective-permute-start | bytes 4718600 | tf_op jit(solution)/shard_map/ppermute | solution.py:625
  7.4 0.1 collective-permute-start.10
  7.4 1.0 %collective-permute-done = f32[4,8,128]{2,1,0:T(8,128)S(1)} collective-permute-done((f32[4,8,128]{2,1,0:T(8,128)S(1)}, f32[4,8,128]{2,1,0:T(8,128)S(1)}, u32[]{:S(2)}, u32[]{:S(2)}) %collective-permute-start) | collective-permute-done | bytes 16416 | tf_op jit(solution)/shard_map/ppermute | solution.py:625
  8.4 0.0 collective-permute-done.1
  8.4 1.5 %collective-permute-start.4 = (f32[4,8,128]{2,1,0:T(8,128)S(1)}, f32[4,8,128]{2,1,0:T(8,128)S(1)}, u32[]{:S(2)}, u32[]{:S(2)}) collective-permute-start(f32[4,8,128]{2,1,0:T(8,128)S(1)} %add_add_fusion.1), channel_id=1, source_target_pairs={{0,16},{8,24},{16,0},{24,8},{1,17},{9,25},{17,1},{25,9},{2,18},{10... | collective-permute-start | bytes 49160 | tf_op jit(solution)/shard_map/ppermute | solution.py:619
  9.9 2.1 %collective-permute-start.3 = (f32[4,8,128]{2,1,0:T(8,128)S(1)}, f32[4,8,128]{2,1,0:T(8,128)S(1)}, u32[]{:S(2)}, u32[]{:S(2)}) collective-permute-start(f32[4,8,128]{2,1,0:T(8,128)S(1)} %add_add_fusion.1), channel_id=1, source_target_pairs={{0,24},{8,16},{16,8},{24,0},{1,25},{9,17},{17,9},{25,1},{2,26},{10... | collective-permute-start | bytes 49160 | tf_op jit(solution)/shard_map/ppermute | solution.py:619
  12.0 0.0 collective-permute-start.2
  12.0 1.7 %shard_map.96.t0_ref = f32[32,128,128]{2,1,0:T(8,128)S(1)} custom-call(f32[96,128,128]{2,1,0:T(8,128)S(1)} %get-tuple-element.51.f_ref), custom_call_target="tpu_custom_call" | custom-call | flops 10000000000 | bytes 10000000 | tf_op jit(solution)/shard_map/pallas_call | solution.py:585
  13.7 0.1 collective-permute-done.4
  13.8 1.1 %collective-permute-done.3 = f32[4,8,128]{2,1,0:T(8,128)S(1)} collective-permute-done((f32[4,8,128]{2,1,0:T(8,128)S(1)}, f32[4,8,128]{2,1,0:T(8,128)S(1)}, u32[]{:S(2)}, u32[]{:S(2)}) %collective-permute-start.3) | collective-permute-done | bytes 16416 | tf_op jit(solution)/shard_map/ppermute | solution.py:619
  14.9 0.9 %collective-permute-done.2 = f32[4,8,128]{2,1,0:T(8,128)S(1)} collective-permute-done((f32[4,8,128]{2,1,0:T(8,128)S(1)}, f32[4,8,128]{2,1,0:T(8,128)S(1)}, u32[]{:S(2)}, u32[]{:S(2)}) %collective-permute-start.2) | collective-permute-done | bytes 16416 | tf_op jit(solution)/shard_map/ppermute | solution.py:619
  15.8 0.0 copy-start
  15.8 0.0 copy-start.1
  15.8 0.0 copy-start.2
  15.8 0.0 copy-start.3
  15.8 0.0 copy-start.4
  15.8 0.0 copy-start.5
  15.8 0.0 copy-start.6
  15.8 2.0 %collective-permute-start.5 = (f32[4,8,128]{2,1,0:T(8,128)S(1)}, f32[4,8,128]{2,1,0:T(8,128)S(1)}, u32[]{:S(2)}, u32[]{:S(2)}) collective-permute-start(f32[4,8,128]{2,1,0:T(8,128)S(1)} %add_add_fusion), channel_id=1, source_target_pairs={{0,32},{32,0},{64,96},{96,64},{128,160},{160,128},{192,224},{224,1... | collective-permute-start | bytes 49160 | tf_op jit(solution)/shard_map/ppermute | solution.py:619
  17.9 1.7 %shard_map.97.t1_ref = f32[32,128,128]{2,1,0:T(8,128)S(1)} custom-call(f32[96,128,128]{2,1,0:T(8,128)S(1)} %get-tuple-element.51.f_ref), custom_call_target="tpu_custom_call" | custom-call | flops 10000000000 | bytes 10000000 | tf_op jit(solution)/shard_map/pallas_call | solution.py:585
  19.5 0.0 copy-done
  19.5 0.0 copy-done.1
  19.6 0.0 copy-done.2
  19.6 0.0 copy-done.3
  19.6 0.0 copy-done.4
  19.6 0.0 copy-done.5
  19.6 0.0 copy-done.6
  19.6 1.0 %shard_map.98 = (f32[9,16,128]{2,1,0:T(8,128)S(1)}, f32[3,8,128]{2,1,0:T(8,128)S(1)}, f32[3,2,32,128]{3,2,1,0:T(8,128)S(1)}, f32[3,2,16,128]{3,2,1,0:T(8,128)S(1)}) custom-call(s32[3,12]{1,0:T(4,128)S(1)} %bitcast.13, f32[4,3]{1,0:T(4,128)S(1)} %copy-done.4, f32[4,2,12]{2,1,0:T(2,128)S(1)} %copy-done.1, f32[1,128]{1,0:T(1,128)S(1)} %bitcast.14, ...), custom_call_target="tpu_custom_call" | custom-call | tf_op jit(solution)/shard_map/pallas_call | solution.py:570
  20.6 0.0 collective-permute-done.5
  20.7 5.5 %collective-permute-start.8 = (f32[4,8,128]{2,1,0:T(8,128)S(1)}, f32[4,8,128]{2,1,0:T(8,128)S(1)}, u32[]{:S(2)}, u32[]{:S(2)}) collective-permute-start(f32[4,8,128]{2,1,0:T(8,128)S(1)} %add.23.part0_ref), channel_id=1, source_target_pairs={{0,192},{32,96},{64,0},{96,160},{128,64},{160,224},{192,128},{224,... | collective-permute-start | bytes 49160 | tf_op jit(solution)/shard_map/ppermute | solution.py:625
  26.2 1.9 %collective-permute-start.7 = (f32[4,8,128]{2,1,0:T(8,128)S(1)}, f32[4,8,128]{2,1,0:T(8,128)S(1)}, u32[]{:S(2)}, u32[]{:S(2)}) collective-permute-start(f32[4,8,128]{2,1,0:T(8,128)S(1)} %add.23.part0_ref), channel_id=1, source_target_pairs={{0,160},{32,128},{64,224},{96,192},{128,32},{160,0},{192,96},{224,... | collective-permute-start | bytes 49160 | tf_op jit(solution)/shard_map/ppermute | solution.py:625
  28.1 0.0 collective-permute-start.6
  28.1 1.7 %shard_map.99.t2_ref = f32[32,128,128]{2,1,0:T(8,128)S(1)} custom-call(f32[96,128,128]{2,1,0:T(8,128)S(1)} %get-tuple-element.51.f_ref), custom_call_target="tpu_custom_call" | custom-call | flops 10000000000 | bytes 10000000 | tf_op jit(solution)/shard_map/pallas_call | solution.py:585
  29.8 0.0 collective-permute-done.8.part3_ref
  29.8 3.1 %collective-permute-done.7.part2_ref = f32[4,8,128]{2,1,0:T(8,128)S(1)} collective-permute-done((f32[4,8,128]{2,1,0:T(8,128)S(1)}, f32[4,8,128]{2,1,0:T(8,128)S(1)}, u32[]{:S(2)}, u32[]{:S(2)}) %collective-permute-start.7) | collective-permute-done | bytes 16416 | tf_op jit(solution)/shard_map/ppermute | solution.py:625
  32.9 0.2 collective-permute-done.6.part1_ref
  33.1 0.0 collective-permute-done.9.far_ref
  33.1 0.0 collective-permute-done.10.near_ref
  33.1 4.2 %shard_map.100 = (f32[12,128]{1,0:T(8,128)}, f32[96,128,128]{2,1,0:T(8,128)}) custom-call(f32[4,8,128]{2,1,0:T(8,128)S(1)} %add.23.part0_ref, f32[4,8,128]{2,1,0:T(8,128)S(1)} %collective-permute-done.6.part1_ref, f32[4,8,128]{2,1,0:T(8,128)S(1)} %collective-permute-done.7.part2_ref, f32[4,8,128]{2,1,0:T(8,128)S(1)} %collective-permute-done.8.part3_ref, ...), custom_call_target="tpu_custom_call" | custom-call | tf_op jit(solution)/shard_map/pallas_call | solution.py:600
  (3 shorter events, 0.0 us)
Async XLA Ops:
  4.0 4.5 %collective-permute-start = (f32[4,8,128]{2,1,0:T(8,128)S(1)}, f32[4,8,128]{2,1,0:T(8,128)S(1)}, u32[]{:S(2)}, u32[]{:S(2)}) collective-permute-start(f32[4,8,128]{2,1,0:T(8,128)S(1)} %get-tuple-element.29), channel_id=1, source_target_pairs={{0,7},{1,2},{2,1},{3,4},{4,3},{5,6},{6,5},{7,0},{8,15},{9,10},{10,... | collective-permute-start | bytes 49160 | tf_op jit(solution)/shard_map/ppermute | solution.py:625
  6.5 1.9 %collective-permute-start.1 = (f32[4,8,128]{2,1,0:T(8,128)S(1)}, f32[4,8,128]{2,1,0:T(8,128)S(1)}, u32[]{:S(2)}, u32[]{:S(2)}) collective-permute-start(f32[4,8,128]{2,1,0:T(8,128)S(1)} %get-tuple-element.30), channel_id=1, source_target_pairs={{0,1},{1,0},{2,3},{3,2},{4,5},{5,4},{6,7},{7,6},{8,9},{9,8},{10,11... | collective-permute-start | bytes 49160 | tf_op jit(solution)/shard_map/ppermute | solution.py:619
  6.5 26.6 %collective-permute-start.9 = (f32[96,32,128]{2,1,0:T(8,128)S(1)}, f32[96,32,128]{2,1,0:T(8,128)S(1)}, u32[]{:S(2)}, u32[]{:S(2)}) collective-permute-start(f32[96,32,128]{2,1,0:T(8,128)S(1)} %get-tuple-element.47), channel_id=1, source_target_pairs={{0,7},{1,2},{2,1},{3,4},{4,3},{5,6},{6,5},{7,0},{8,15},{9,10},{10,... | collective-permute-start | bytes 4718600 | tf_op jit(solution)/shard_map/ppermute | solution.py:625
  7.4 25.7 %collective-permute-start.10 = (f32[96,32,128]{2,1,0:T(8,128)S(1)}, f32[96,32,128]{2,1,0:T(8,128)S(1)}, u32[]{:S(2)}, u32[]{:S(2)}) collective-permute-start(f32[96,32,128]{2,1,0:T(8,128)S(1)} %get-tuple-element.48), channel_id=1, source_target_pairs={{0,1},{1,0},{2,3},{3,2},{4,5},{5,4},{6,7},{7,6},{8,9},{9,8},{10,11... | collective-permute-start | bytes 4718600 | tf_op jit(solution)/shard_map/ppermute | solution.py:619
  8.4 5.3 %collective-permute-start.4 = (f32[4,8,128]{2,1,0:T(8,128)S(1)}, f32[4,8,128]{2,1,0:T(8,128)S(1)}, u32[]{:S(2)}, u32[]{:S(2)}) collective-permute-start(f32[4,8,128]{2,1,0:T(8,128)S(1)} %add_add_fusion.1), channel_id=1, source_target_pairs={{0,16},{8,24},{16,0},{24,8},{1,17},{9,25},{17,1},{25,9},{2,18},{10... | collective-permute-start | bytes 49160 | tf_op jit(solution)/shard_map/ppermute | solution.py:619
  9.9 4.9 %collective-permute-start.3 = (f32[4,8,128]{2,1,0:T(8,128)S(1)}, f32[4,8,128]{2,1,0:T(8,128)S(1)}, u32[]{:S(2)}, u32[]{:S(2)}) collective-permute-start(f32[4,8,128]{2,1,0:T(8,128)S(1)} %add_add_fusion.1), channel_id=1, source_target_pairs={{0,24},{8,16},{16,8},{24,0},{1,25},{9,17},{17,9},{25,1},{2,26},{10... | collective-permute-start | bytes 49160 | tf_op jit(solution)/shard_map/ppermute | solution.py:619
  12.0 3.7 %collective-permute-start.2 = (f32[4,8,128]{2,1,0:T(8,128)S(1)}, f32[4,8,128]{2,1,0:T(8,128)S(1)}, u32[]{:S(2)}, u32[]{:S(2)}) collective-permute-start(f32[4,8,128]{2,1,0:T(8,128)S(1)} %add_add_fusion.1), channel_id=1, source_target_pairs={{0,8},{8,0},{16,24},{24,16},{1,9},{9,1},{17,25},{25,17},{2,10},{10... | collective-permute-start | bytes 49160 | tf_op jit(solution)/shard_map/ppermute | solution.py:619
  15.8 3.8 %copy-start = (f32[12,128]{1,0:T(8,128)S(1)}, f32[12,128]{1,0:T(8,128)}, u32[]{:S(2)}) copy-start(f32[12,128]{1,0:T(8,128)} %cover_ref.1) | copy-start | bytes 18436
  15.8 3.8 %copy-start.1 = (f32[4,2,12]{2,1,0:T(2,128)S(1)}, f32[4,2,12]{2,1,0:T(2,128)}, u32[]{:S(2)}) copy-start(f32[4,2,12]{2,1,0:T(2,128)} %rates_ref.1) | copy-start | bytes 1156
  15.8 3.8 %copy-start.2 = (s32[1,128]{1,0:T(1,128)S(1)}, s32[1,128]{1,0:T(1,128)}, u32[]{:S(2)}) copy-start(s32[1,128]{1,0:T(1,128)} %cell_ref.3) | copy-start | bytes 1540
  15.8 3.8 %copy-start.3 = (s32[12,3]{0,1:T(4,128)S(1)}, s32[12,3]{0,1:T(4,128)}, u32[]{:S(2)}) copy-start(s32[12,3]{0,1:T(4,128)} %param.13) | copy-start | bytes 436
  15.8 3.8 %copy-start.4 = (f32[4,3]{1,0:T(4,128)S(1)}, f32[4,3]{1,0:T(4,128)}, u32[]{:S(2)}) copy-start(f32[4,3]{1,0:T(4,128)} %stick_ref.1) | copy-start | bytes 148
  15.8 3.8 %copy-start.5 = (f32[128]{0:T(128)S(1)}, f32[128]{0:T(128)}, u32[]{:S(2)}) copy-start(f32[128]{0:T(128)} %param.9) | copy-start | bytes 1540
  15.8 3.8 %copy-start.6 = (s32[128]{0:T(128)S(1)}, s32[128]{0:T(128)}, u32[]{:S(2)}) copy-start(s32[128]{0:T(128)} %param.12) | copy-start | bytes 1540
  15.8 4.8 %collective-permute-start.5 = (f32[4,8,128]{2,1,0:T(8,128)S(1)}, f32[4,8,128]{2,1,0:T(8,128)S(1)}, u32[]{:S(2)}, u32[]{:S(2)}) collective-permute-start(f32[4,8,128]{2,1,0:T(8,128)S(1)} %add_add_fusion), channel_id=1, source_target_pairs={{0,32},{32,0},{64,96},{96,64},{128,160},{160,128},{192,224},{224,1... | collective-permute-start | bytes 49160 | tf_op jit(solution)/shard_map/ppermute | solution.py:619
  20.7 9.1 %collective-permute-start.8 = (f32[4,8,128]{2,1,0:T(8,128)S(1)}, f32[4,8,128]{2,1,0:T(8,128)S(1)}, u32[]{:S(2)}, u32[]{:S(2)}) collective-permute-start(f32[4,8,128]{2,1,0:T(8,128)S(1)} %add.23.part0_ref), channel_id=1, source_target_pairs={{0,192},{32,96},{64,0},{96,160},{128,64},{160,224},{192,128},{224,... | collective-permute-start | bytes 49160 | tf_op jit(solution)/shard_map/ppermute | solution.py:625
  26.2 6.8 %collective-permute-start.7 = (f32[4,8,128]{2,1,0:T(8,128)S(1)}, f32[4,8,128]{2,1,0:T(8,128)S(1)}, u32[]{:S(2)}, u32[]{:S(2)}) collective-permute-start(f32[4,8,128]{2,1,0:T(8,128)S(1)} %add.23.part0_ref), channel_id=1, source_target_pairs={{0,160},{32,128},{64,224},{96,192},{128,32},{160,0},{192,96},{224,... | collective-permute-start | bytes 49160 | tf_op jit(solution)/shard_map/ppermute | solution.py:625
  28.1 5.0 %collective-permute-start.6 = (f32[4,8,128]{2,1,0:T(8,128)S(1)}, f32[4,8,128]{2,1,0:T(8,128)S(1)}, u32[]{:S(2)}, u32[]{:S(2)}) collective-permute-start(f32[4,8,128]{2,1,0:T(8,128)S(1)} %add.23.part0_ref), channel_id=1, source_target_pairs={{0,224},{32,64},{64,32},{96,128},{128,96},{160,192},{192,160},{224... | collective-permute-start | bytes 49160 | tf_op jit(solution)/shard_map/ppermute | solution.py:625
